TPU v7x, 32 devices: a whole 2x2x4 slice. The times are simulated.
32 devices in a mesh: row: 8 (over z, y), col: 4 (over x, core).
Axes of the slice: x: 2, y: 2, z: 4, core: 2. Of those that a mesh axis runs over, the one named last changes fastest.
Arguments:
- pair_map: bfloat16 [32, 2048, 128], P('row', 'col'), may hold values from -6 to 6
- norm_gain: float32 [128], replicated, may hold values from 0.5 to 1.5
- in_weights: bfloat16 [3, 128, 512], replicated, may hold values from -0.5 to 0.5
- head_gain: float32 [3, 128], replicated, may hold values from 0.5 to 1.5
- out_weights: bfloat16 [3, 128, 128], replicated, may hold values from -0.5 to 0.5
- trans_gain: float32 [128], replicated, may hold values from 0.5 to 1.5
- up_weight: bfloat16 [128, 512], replicated, may hold values from -0.5 to 0.5
- down_weight: bfloat16 [512, 128], replicated, may hold values from -0.25 to 0.25
Outputs:
- result: bfloat16 [32, 2048, 128], P('row', 'col')
All inputs are finite; a program needn't handle non-finite values.
Results may differ from a plain program's by a relative error of at most 0.012.
Values may be sent and summed in bfloat16 or wider, within the bound.
No kernel may reach another device: no remote copies, remote signals or barrier semaphores. Data moves between devices by JAX's collectives and lax.ppermute only.
A program may use at most 64 MiB of HBM per device.

v0:
```python
import jax
import jax.numpy as jnp
from jax import lax
from jax.sharding import PartitionSpec as P

D = 128
HEADS = 4
HEAD = 32


epsilon = 1e-05


def feature(values):
    return jnp.where(values > 0, values + 1.0, jnp.exp(jnp.minimum(values, 0.0)))


def normalize(values, gain):
    meansq = jnp.mean(values * values, axis=-1, keepdims=True)
    return values * lax.rsqrt(meansq + epsilon) * gain


def open_branch(normed, weight):
    width = weight.shape[0]
    flat = jnp.dot(normed.reshape(-1, width), weight, preferred_element_type=jnp.float32)
    shape = normed.shape[:-1] + (HEADS, HEAD)
    query_feat = feature(flat[:, :width]).astype(jnp.bfloat16).reshape(shape)
    key_feat = feature(flat[:, width : 2 * width]).astype(jnp.bfloat16).reshape(shape)
    value_rows = flat[:, 2 * width : 3 * width].astype(jnp.bfloat16).reshape(shape)
    gate_vals = jax.nn.sigmoid(flat[:, 3 * width :]).reshape(normed.shape)
    return (query_feat, key_feat, value_rows, gate_vals)


def close_branch(head_out, gate_vals, gain, weight):
    mixed_out = (normalize(head_out.reshape(gate_vals.shape), gain) * gate_vals).astype(
        jnp.bfloat16
    )
    width = weight.shape[0]
    projected = jnp.dot(mixed_out.reshape(-1, width), weight, preferred_element_type=jnp.float32)
    return projected.reshape(gate_vals.shape).astype(jnp.bfloat16)


def shards(
    pair_map, norm_gain, in_weights, head_gain, out_weights, trans_gain, up_weight, down_weight
):
    row_count = pair_map.shape[0]
    widened = pair_map.astype(jnp.float32)
    normed = normalize(widened, norm_gain).astype(jnp.bfloat16)
    row_parts = []
    partials = []
    for branch in range(2):
        query_feat, key_feat, value_rows, gate_vals = open_branch(normed, in_weights[branch])
        partial_state = jnp.einsum(
            "rcha,rchb->rahb", key_feat, value_rows, preferred_element_type=jnp.float32
        )
        partials.append(partial_state.reshape(row_count * HEAD, D))
        row_parts.append((query_feat, gate_vals))
    first_sum, second_sum = (
        lax.psum(partials[0].astype(jnp.bfloat16), "col").astype(jnp.float32),
        lax.psum(partials[1].astype(jnp.bfloat16), "col").astype(jnp.float32),
    )
    first_state = first_sum.astype(jnp.bfloat16)
    second_state = second_sum.astype(jnp.bfloat16)
    row_outputs = []
    for branch, states in enumerate((first_state, second_state)):
        query_feat, gate_vals = row_parts[branch]
        states = states.reshape(row_count, HEAD, HEADS, HEAD)
        head_out = jnp.einsum(
            "rcha,rahb->rchb", query_feat, states, preferred_element_type=jnp.float32
        )
        row_outputs.append(
            close_branch(head_out, gate_vals, head_gain[branch], out_weights[branch])
        )
    regrouped = lax.all_to_all(normed, "row", split_axis=1, concat_axis=0, tiled=True)
    query_feat, key_feat, value_rows, gate_vals = open_branch(regrouped, in_weights[2])
    states = jnp.einsum(
        "rcha,rchb->chab", key_feat, value_rows, preferred_element_type=jnp.float32
    ).astype(jnp.bfloat16)
    head_out = jnp.einsum("rcha,chab->rchb", query_feat, states, preferred_element_type=jnp.float32)
    column_out = close_branch(head_out, gate_vals, head_gain[2], out_weights[2])
    third_out = lax.all_to_all(column_out, "row", split_axis=0, concat_axis=1, tiled=True)
    updated = (
        widened
        + row_outputs[0].astype(jnp.float32)
        + row_outputs[1].astype(jnp.float32)
        + third_out.astype(jnp.float32)
    )
    trans_in = normalize(updated, trans_gain).astype(jnp.bfloat16)
    hidden = jax.nn.silu(
        jnp.dot(trans_in.reshape(-1, D), up_weight, preferred_element_type=jnp.float32)
    ).astype(jnp.bfloat16)
    lowered = jnp.dot(hidden, down_weight, preferred_element_type=jnp.float32).reshape(
        updated.shape
    )
    return (updated + lowered).astype(jnp.bfloat16)


def solution(mesh):
    in_specs = (P("row", "col", None), P(), P(), P(), P(), P(), P(), P())
    out_specs = P("row", "col", None)
    return jax.shard_map(shards, mesh=mesh, in_specs=in_specs, out_specs=out_specs, check_vma=False)
```

profile of v0, /device:TPU:0, one launch (start us, length us, event | category | flops | bytes accessed | tf_op | source)
XLA Modules:
  0.0 150.5 jit_solution(14820503538839783449)
XLA Ops:
  6.5 1.4 fusion.10
  8.0 1.4 fusion.12
  9.4 1.2 copy.109
  10.6 7.3 %all-to-all-start = ((bf16[4,512,128]{2,0,1:T(4,128)(2,1)}), bf16[4,512,128]{2,0,1:T(4,128)(2,1)S(1)}, u32[]{:S(2)}, u32[]{:S(2)}) async-start(bf16[4,512,128]{2,0,1:T(4,128)(2,1)} %copy.109), calls=%async_computation | async-start | bytes 1048576 | tf_op jit(solution)/shard_map/all_to_all | solution.py:74
  17.9 1.6 %fusion.36 = f32[2048,512]{1,0:T(8,128)S(1)} fusion(bf16[2048,128]{1,0:T(8,128)(2,1)S(1)} %bitcast.106, bf16[3,128,512]{2,1,0:T(8,128)(2,1)} %param.10), kind=kOutput, calls=%fused_computation.65 | convolution fusion | flops 268435456 | bytes 4849664 | tf_op jit(solution)/shard_map/dot_general | solution.py:25
  19.5 0.1 slice.169
  19.7 1.8 %copy-done.3 = f32[2048,512]{1,0:T(8,128)} copy-done((f32[2048,512]{1,0:T(8,128)}, f32[2048,512]{1,0:T(8,128)S(1)}, u32[]{:S(2)}) %copy-start.3) | copy-done | bytes 4194328
  21.5 1.3 select_convert_fusion.2
  22.8 1.6 %fusion.38 = f32[2048,512]{1,0:T(8,128)S(1)} fusion(bf16[2048,128]{1,0:T(8,128)(2,1)S(1)} %bitcast.107, bf16[3,128,512]{2,1,0:T(8,128)(2,1)} %param.10), kind=kOutput, calls=%fused_computation.67 | convolution fusion | flops 268435456 | bytes 4849664 | tf_op jit(solution)/shard_map/dot_general | solution.py:25
  24.4 0.1 slice.170
  24.5 1.8 %copy-done.1 = f32[2048,512]{1,0:T(8,128)} copy-done((f32[2048,512]{1,0:T(8,128)}, f32[2048,512]{1,0:T(8,128)S(1)}, u32[]{:S(2)}) %copy-start.1) | copy-done | bytes 4194328
  26.3 1.3 select_convert_fusion.4
  27.6 0.2 copy.101
  27.8 1.2 reshape.154
  29.0 1.3 copy.102
  30.3 1.2 reshape.155
  31.5 0.2 copy.93
  31.7 1.2 reshape.149
  32.9 0.2 copy.94
  33.1 0.4 reshape.150
  33.5 2.2 %fusion.9 = bf16[4,32,4,32]{1,3,2,0:T(8,128)(2,1)} fusion(bf16[4,512,4,32]{1,0,3,2:T(4,128)(2,1)} %reshape.155, bf16[4,512,4,32]{1,0,3,2:T(4,128)(2,1)} %reshape.154), kind=kOutput, calls=%fused_computation.21 | convolution fusion | flops 16793600 | bytes 1081344 | tf_op jit(solution)/shard_map/rcha,rchb->rahb/dot_general | solution.py:53
  35.8 2.1 %fusion.8 = bf16[4,32,4,32]{1,3,2,0:T(8,128)(2,1)} fusion(bf16[4,512,4,32]{1,0,3,2:T(4,128)(2,1)S(1)} %reshape.150, bf16[4,512,4,32]{1,0,3,2:T(4,128)(2,1)} %reshape.149), kind=kOutput, calls=%fused_computation.20 | convolution fusion | flops 16793600 | bytes 1081344 | tf_op jit(solution)/shard_map/rcha,rchb->rahb/dot_general | solution.py:53
  37.9 0.2 copy.105
  38.1 0.4 reshape.157
  38.5 0.2 copy.97
  38.7 0.4 reshape.152
  39.1 32.4 %all-reduce.3.cloned.1.call-done = (bf16[4,32,4,32]{1,3,2,0:T(8,128)(2,1)}, bf16[4,32,4,32]{1,3,2,0:T(8,128)(2,1)}) async-done(((bf16[4,32,4,32]{1,3,2,0:T(8,128)(2,1)}, bf16[4,32,4,32]{1,3,2,0:T(8,128)(2,1)}), (bf16[4,32,4,32]{1,3,2,0:T(8,128)(2,1)}, bf16[4,32,4,32]{1,3,2,0:T(8,128)(2,1)})) %all-reduce.3.cloned.1.call-update) | async-done | bytes 65552 | tf_op jit(solution)/shard_map/psum | solution.py:60
  71.5 1.3 multiply_reduce_fusion.2
  72.8 0.7 copy.107
  73.5 0.3 copy.126
  73.8 1.3 copy.108
  75.2 1.3 multiply_reduce_fusion.3
  76.6 1.6 %fusion.34 = f32[2048,512]{1,0:T(8,128)S(1)} fusion(bf16[2048,128]{1,0:T(8,128)(2,1)S(1)} %bitcast.115, bf16[3,128,512]{2,1,0:T(8,128)(2,1)} %param.10), kind=kOutput, calls=%fused_computation.63 | convolution fusion | flops 268435456 | bytes 4849664 | tf_op jit(solution)/shard_map/dot_general | solution.py:25
  78.2 0.1 slice.168
  78.3 1.8 %copy-done.2 = f32[2048,512]{1,0:T(8,128)} copy-done((f32[2048,512]{1,0:T(8,128)}, f32[2048,512]{1,0:T(8,128)S(1)}, u32[]{:S(2)}) %copy-start.2) | copy-done | bytes 4194328
  80.1 1.5 select_convert_fusion.1
  81.6 0.2 copy.113
  81.8 1.1 reshape.161
  82.9 3.4 %copy.115 = bf16[32,64,4,32]{3,0,2,1:T(8,128)(2,1)S(1)} copy(bf16[32,64,4,32]{1,0,3,2:T(8,128)(2,1)S(1)} %reshape.161) | data formatting | bytes 1048576 | tf_op jit(solution)/shard_map/reshape | solution.py:29
  86.3 2.1 %copy.112 = bf16[2048,128]{0,1:T(8,128)(2,1)} copy(bf16[2048,128]{1,0:T(8,128)(2,1)} %get-tuple-element.11) | data formatting | bytes 1048576 | tf_op jit(solution)/shard_map/convert_element_type | solution.py:28
  88.3 2.1 %reshape.160 = bf16[32,64,4,32]{1,0,3,2:T(8,128)(2,1)S(1)} reshape(bf16[2048,128]{0,1:T(8,128)(2,1)} %copy.112) | data formatting | bytes 1048576 | tf_op jit(solution)/shard_map/reshape | solution.py:28
  90.4 2.0 %copy.116 = bf16[2048,128]{0,1:T(8,128)(2,1)} copy(bf16[2048,128]{1,0:T(8,128)(2,1)} %get-tuple-element.12) | data formatting | bytes 1048576 | tf_op jit(solution)/shard_map/convert_element_type | solution.py:27
  92.5 2.8 %reshape.162 = bf16[32,64,4,32]{1,0,3,2:T(8,128)(2,1)} reshape(bf16[2048,128]{0,1:T(8,128)(2,1)} %copy.116) | data formatting | bytes 1048576 | tf_op jit(solution)/shard_map/reshape | solution.py:27
  95.3 5.4 %copy.118 = bf16[32,64,4,32]{3,0,2,1:T(8,128)(2,1)} copy(bf16[32,64,4,32]{1,0,3,2:T(8,128)(2,1)} %reshape.162) | data formatting | bytes 1048576 | tf_op jit(solution)/shard_map/reshape | solution.py:27
  100.7 3.9 %copy.114 = bf16[32,64,4,32]{0,3,2,1:T(8,128)(2,1)} copy(bf16[32,64,4,32]{1,0,3,2:T(8,128)(2,1)S(1)} %reshape.160) | data formatting | bytes 1048576 | tf_op jit(solution)/shard_map/reshape | solution.py:28
  104.6 5.9 %multiply_reduce_fusion = (f32[32,64]{0,1:T(8,128)S(1)}, f32[32,64,4,32]{0,3,2,1:T(8,128)}) fusion(bf16[32,64,4,32]{3,0,2,1:T(8,128)(2,1)} %copy.118, bf16[32,64,4,32]{0,3,2,1:T(8,128)(2,1)} %copy.114, bf16[32,64,4,32]{3,0,2,1:T(8,128)(2,1)S(1)} %copy.115), kind=kOutput, calls=%fused_computation.1 | convolution fusion | flops 34338816 | bytes 2629632 | tf_op jit(solution)/shard_map/rcha,chab->rchb/dot_general | solution.py:79
  110.6 0.1 rsqrt.55
  110.7 3.7 %copy.119 = f32[32,64,4,32]{1,0,3,2:T(8,128)S(1)} copy(f32[32,64,4,32]{0,3,2,1:T(8,128)} %get-tuple-element.17) | data formatting | bytes 2097152 | tf_op jit(solution)/shard_map/rcha,chab->rchb/transpose | solution.py:79
  114.3 0.7 reshape.163
  115.0 0.3 copy.121
  115.3 2.3 %fusion.26 = (bf16[2048,128]{1,0:T(8,128)(2,1)S(1)}, bf16[2048,128]{1,0:T(8,128)(2,1)S(1)}) fusion(f32[2048,512]{1,0:T(8,128)} %copy-done.3, f32[2048,128]{1,0:T(8,128)} %copy.108, f32[128]{0:T(128)S(1)} %get-tuple-element.15, f32[2048]{0:T(1024)S(1)} %bitcast.120, f32[2048,512]{1,0:T(8,128)} %copy-done.2, f32[128]{0:T(128)S(1)} %get-tuple-element.14, ...), kind=kLoop, calls=%fused_computation.55 | loop fusion | flops 3670016 | bytes 5260288 | tf_op jit(solution)/shard_map/convert_element_type | solution.py:35
  117.7 1.1 convolution_convert_fusion
  118.8 5.5 %all-to-all-start.1 = ((bf16[32,64,128]{2,1,0:T(8,128)(2,1)}), bf16[32,64,128]{2,1,0:T(8,128)(2,1)}, u32[]{:S(2)}, u32[]{:S(2)}) async-start(bf16[32,64,128]{2,1,0:T(8,128)(2,1)} %convolution_convert_fusion), calls=%async_computation.1 | async-start | bytes 1048576 | tf_op jit(solution)/shard_map/all_to_all | solution.py:81
  124.3 0.7 copy.99
  125.0 0.3 copy.124
  125.4 0.3 copy.100
  125.7 2.4 %fusion.25 = bf16[2048,128]{1,0:T(8,128)(2,1)} fusion(f32[2048,512]{1,0:T(8,128)} %copy-done.1, f32[2048,128]{1,0:T(8,128)S(1)} %copy.100, f32[128]{0:T(128)S(1)} %get-tuple-element.13, f32[2048]{0:T(1024)S(1)} %bitcast.121), kind=kLoop, calls=%fused_computation.54 | loop fusion | flops 1835008 | bytes 2630144 | tf_op jit(solution)/shard_map/convert_element_type | solution.py:35
  128.1 0.3 fusion.7
  128.3 9.5 %all-to-all-done.1 = bf16[32,64,128]{2,1,0:T(8,128)(2,1)} async-done(((bf16[32,64,128]{2,1,0:T(8,128)(2,1)}), bf16[32,64,128]{2,1,0:T(8,128)(2,1)}, u32[]{:S(2)}, u32[]{:S(2)}) %all-to-all-start.1) | async-done | bytes 524320 | tf_op jit(solution)/shard_map/all_to_all | solution.py:81
  137.9 1.1 copy.122
  139.0 1.6 %multiply_reduce_fusion.1 = (f32[4,512]{1,0:T(4,128)S(1)}, f32[4,512,128]{2,1,0:T(8,128)S(1)}) fusion(f32[4,512,128]{2,1,0:T(8,128)S(1)} %bitcast.112, f32[4,512,128]{2,1,0:T(8,128)S(1)} %fusion.7, bf16[4,512,128]{2,1,0:T(8,128)(2,1)} %bitcast.117, bf16[3,128,128]{2,1,0:T(8,128)(2,1)S(1)} %copy-done.8, bf16[4,512,128]{2,1,0:T(8,128)(2,1)S(1)} %copy-done.4), kind=kOutput, calls=%fused_computation.45 | convolution fusion | flops 69203968 | bytes 4235264 | tf_op jit(solution)/shard_map/dot_general | solution.py:39
  140.6 0.3 multiply_convert_fusion.1
  141.0 1.8 %fusion.3 = f32[2048,128]{1,0:T(8,128)S(1)} fusion(bf16[512,128]{1,0:T(8,128)(2,1)S(1)} %copy-done, bf16[2048,128]{1,0:T(8,128)(2,1)S(1)} %bitcast.119, bf16[128,512]{1,0:T(8,128)(2,1)S(1)} %copy-done.11), kind=kOutput, calls=%fused_computation.8 | convolution fusion | flops 542113792 | bytes 1835008 | tf_op jit(solution)/shard_map/dot_general | solution.py:92
  142.8 0.9 add_convert_fusion
  (35 shorter events, 0.3 us)
Async XLA Ops:
  6.5 134.4 %copy-start = (bf16[512,128]{1,0:T(8,128)(2,1)S(1)}, bf16[512,128]{1,0:T(8,128)(2,1)}, u32[]{:S(2)}) copy-start(bf16[512,128]{1,0:T(8,128)(2,1)} %param.15) | copy-start | bytes 393220
  10.6 65.8 %all-to-all-start = ((bf16[4,512,128]{2,0,1:T(4,128)(2,1)}), bf16[4,512,128]{2,0,1:T(4,128)(2,1)S(1)}, u32[]{:S(2)}, u32[]{:S(2)}) async-start(bf16[4,512,128]{2,0,1:T(4,128)(2,1)} %copy.109), calls=%async_computation | async-start | bytes 1048576 | tf_op jit(solution)/shard_map/all_to_all | solution.py:74
  17.9 53.6 %all-reduce.3.cloned.1.call-start = ((), (), s32[]{:S(2)}) async-start(), calls=%async_computation.2 | async-start | bytes 524288 | tf_op jit(solution)/shard_map/psum | solution.py:60
  19.5 2.0 %copy-start.3 = (f32[2048,512]{1,0:T(8,128)}, f32[2048,512]{1,0:T(8,128)S(1)}, u32[]{:S(2)}) copy-start(f32[2048,512]{1,0:T(8,128)S(1)} %fusion.36) | copy-start | bytes 12582916
  24.4 2.0 %copy-start.1 = (f32[2048,512]{1,0:T(8,128)}, f32[2048,512]{1,0:T(8,128)S(1)}, u32[]{:S(2)}) copy-start(f32[2048,512]{1,0:T(8,128)S(1)} %fusion.38) | copy-start | bytes 12582916
  29.0 3.9 %copy-start.6 = (bf16[2048,128]{1,0:T(8,128)(2,1)S(1)}, bf16[2048,128]{1,0:T(8,128)(2,1)}, u32[]{:S(2)}) copy-start(bf16[2048,128]{1,0:T(8,128)(2,1)} %get-tuple-element.8) | copy-start | bytes 1572868
  30.3 7.6 %copy-start.9 = (f32[3,128]{1,0:T(4,128)S(1)}, f32[3,128]{1,0:T(4,128)}, u32[]{:S(2)}) copy-start(f32[3,128]{1,0:T(4,128)} %param.11) | copy-start | bytes 4612
  71.5 3.6 %copy-start.7 = (bf16[4,32,4,32]{1,3,2,0:T(8,128)(2,1)S(1)}, bf16[4,32,4,32]{1,3,2,0:T(8,128)(2,1)}, u32[]{:S(2)}) copy-start(bf16[4,32,4,32]{1,3,2,0:T(8,128)(2,1)} %get-tuple-element.6) | copy-start | bytes 98308
  78.1 2.0 %copy-start.2 = (f32[2048,512]{1,0:T(8,128)}, f32[2048,512]{1,0:T(8,128)S(1)}, u32[]{:S(2)}) copy-start(f32[2048,512]{1,0:T(8,128)S(1)} %fusion.34) | copy-start | bytes 12582916
  115.0 2.7 %copy-start.8 = (bf16[3,128,128]{2,1,0:T(8,128)(2,1)S(1)}, bf16[3,128,128]{2,1,0:T(8,128)(2,1)}, u32[]{:S(2)}) copy-start(bf16[3,128,128]{2,1,0:T(8,128)(2,1)} %param.12) | copy-start | bytes 294916
  115.3 9.0 %copy-start.5 = (f32[4,512,4,32]{1,3,2,0:T(8,128)S(1)}, f32[4,512,4,32]{1,3,2,0:T(8,128)}, u32[]{:S(2)}) copy-start(f32[4,512,4,32]{1,3,2,0:T(8,128)} %get-tuple-element.21) | copy-start | bytes 3145732
  118.8 19.1 %all-to-all-start.1 = ((bf16[32,64,128]{2,1,0:T(8,128)(2,1)}), bf16[32,64,128]{2,1,0:T(8,128)(2,1)}, u32[]{:S(2)}, u32[]{:S(2)}) async-start(bf16[32,64,128]{2,1,0:T(8,128)(2,1)} %convolution_convert_fusion), calls=%async_computation.1 | async-start | bytes 1048576 | tf_op jit(solution)/shard_map/all_to_all | solution.py:81
  125.3 13.7 %copy-start.4 = (bf16[4,512,128]{2,1,0:T(8,128)(2,1)S(1)}, bf16[4,512,128]{2,1,0:T(8,128)(2,1)}, u32[]{:S(2)}) copy-start(bf16[4,512,128]{2,1,0:T(8,128)(2,1)} %param.8) | copy-start | bytes 1572868
  128.0 12.6 %copy-start.10 = (f32[128]{0:T(128)S(1)}, f32[128]{0:T(128)}, u32[]{:S(2)}) copy-start(f32[128]{0:T(128)} %param.13) | copy-start | bytes 1540
  128.1 12.9 %copy-start.11 = (bf16[128,512]{1,0:T(8,128)(2,1)S(1)}, bf16[128,512]{1,0:T(8,128)(2,1)}, u32[]{:S(2)}) copy-start(bf16[128,512]{1,0:T(8,128)(2,1)} %param.14) | copy-start | bytes 393220
Sparse Core Ops, SparseCore 0:
  38.0 33.4 all-reduce.2
where the time goes:
time: 151 us
  local copies, waits for them, and re-layouts  46.9 us (31%)
  waiting for transfers between devices  42 us (28%)
  matrix products  22.2 us (15%)
  between operations  13.8 us (9%)
  other arithmetic  12.8 us (8%)
  starting transfers between devices  12.8 us (8%)
    psum x1, waiting for transfers between devices, shards(): lax.psum(partials[1].astype(jnp.bfloat16), 'col').astype(jnp.float32)  32.4 us
    all_to_all x1, waiting for transfers between devices, shards(): lax.all_to_all(column_out, 'row', split_axis=0, concat_axis=1, tiled=True)  9.55 us
    reshape x4, local copies, waits for them, and re-layouts, open_branch(): query_feat = feature(flat[:, :width]).astype(jnp.bfloat16).reshape(shape)  8.99 us
    reshape x4, local copies, waits for them, and re-layouts, open_branch(): feature(flat[:, width:2 * width]).astype(jnp.bfloat16).reshape(shape)  7.51 us
    all_to_all x1, starting transfers between devices, shards(): lax.all_to_all(normed, 'row', split_axis=1, concat_axis=0, tiled=True)  7.28 us
    reshape x4, local copies, waits for them, and re-layouts, open_branch(): flat[:, 2 * width:3 * width].astype(jnp.bfloat16).reshape(shape)  6.85 us
    unnamed x28, local copies, waits for them, and re-layouts  6.15 us
    dot_general x1, matrix products, shards(): jnp.einsum('rcha,chab->rchb', query_feat, states, preferred_element_type=...  5.92 us
  transfers between devices with their start and end apart: 3, of which 2 were waited for; matrix products, arithmetic and copies ran while one was open for 17% of the time, Pallas kernels for 0%

commit v1 on v0

v1 whole, which is shorter than its diff:
```python
import functools

import jax
import jax.numpy as jnp
from jax import lax
from jax.experimental import pallas as pl
from jax.experimental.pallas import tpu as pltpu
from jax.sharding import PartitionSpec as P

HEAD = 32
GROUP = 4
EPSILON = 1e-05
VMEM_LIMIT = 24 * 1024 * 1024

F32 = jnp.float32
BF16 = jnp.bfloat16


def matmul(a, b):
    return jnp.dot(a, b, preferred_element_type=F32)


def matmul_nt(a, b):
    return lax.dot_general(a, b, (((1,), (1,)), ((), ())), preferred_element_type=F32)


def feature(values):
    return jnp.exp(jnp.minimum(values, 0.0)) + jnp.maximum(values, 0.0)


def sigmoid(values):
    return 0.5 * jnp.tanh(0.5 * values) + 0.5


def normalize(values, gain):
    meansq = jnp.mean(values * values, axis=-1, keepdims=True)
    return values * lax.rsqrt(meansq + EPSILON) * gain


def iota(shape, axis):
    return lax.broadcasted_iota(jnp.int32, shape, axis)


def head_mask(rows, width):
    return ((iota((rows, width), 0) % width) // HEAD) == (iota((rows, width), 1) // HEAD)


def interleave(row_count, cols):
    count = row_count * cols
    out = iota((count, count), 0)
    src = iota((count, count), 1)
    hit = (out // row_count == src % cols) & (out % row_count == src // cols)
    return hit.astype(F32).astype(BF16)


def norm_kernel(parts, x_ref, gain_ref, normed_ref, sent_ref):
    row_count, col_count, width = x_ref.shape
    cols = col_count // parts
    order = interleave(row_count, cols)
    gain = gain_ref[...]
    for part in range(parts):
        span = slice(part * cols, (part + 1) * cols)
        block = x_ref[:, span, :].astype(F32).reshape(row_count * cols, width)
        normed = normalize(block, gain).astype(BF16)
        normed_ref[:, span, :] = normed.reshape(row_count, cols, width)
        sent_ref[part] = matmul(order, normed).astype(BF16)


def state_kernel(normed_ref, weight_ref, state_ref):
    row_count, col_count, width = normed_ref.shape
    keep = head_mask(width, width)
    for branch in range(2):
        key_weight = weight_ref[branch, :, width : 2 * width].T
        value_weight = weight_ref[branch, :, 2 * width : 3 * width]
        for row in range(row_count):
            normed = normed_ref[row]
            keys = feature(matmul_nt(key_weight, normed)).astype(BF16)
            values = matmul(normed, value_weight).astype(BF16)
            state = jnp.where(keep, matmul(keys, values), 0.0)
            packed = state[:HEAD]
            for head in range(1, width // HEAD):
                packed = packed + state[head * HEAD : (head + 1) * HEAD]
            state_ref[branch, row] = packed.astype(BF16)


def row_kernel(
    x_ref, normed_ref, state_ref, weight_ref, head_gain_ref, out_weight_ref, updated_ref
):
    row_count, col_count, width = normed_ref.shape
    keep = head_mask(width, width)
    heads = width // HEAD
    for row in range(row_count):
        normed = normed_ref[row]
        total = x_ref[row].astype(F32)
        for branch in range(2):
            packed = state_ref[branch, row].astype(F32)
            state = jnp.where(keep, jnp.concatenate([packed] * heads, axis=0), 0.0).astype(BF16)
            query = feature(matmul(normed, weight_ref[branch, :, :width])).astype(BF16)
            gate = sigmoid(matmul(normed, weight_ref[branch, :, 3 * width :]))
            head_out = matmul(query, state)
            mixed = (normalize(head_out, head_gain_ref[branch : branch + 1]) * gate).astype(BF16)
            total = total + matmul(mixed, out_weight_ref[branch]).astype(BF16).astype(F32)
        updated_ref[row] = total


def column_pass(row_count, got_ref, weight_ref, head_gain_ref, out_weight_ref, sent_ref):
    parts, tokens, width = got_ref.shape
    heads = width // HEAD
    piece = GROUP * row_count
    size = parts * piece
    key_weight = weight_ref[2, :, width : 2 * width].T
    keep = head_mask(GROUP * width, width)
    column_down = (iota((size, width), 0) // row_count) % GROUP
    column_across = (iota((width, size), 1) // row_count) % GROUP
    gain = head_gain_ref[2:3]
    for group in range(tokens // piece):
        span = slice(group * piece, (group + 1) * piece)
        block = jnp.concatenate([got_ref[part, span, :] for part in range(parts)], axis=0)
        keys = feature(matmul_nt(key_weight, block))
        spread_keys = jnp.concatenate(
            [jnp.where(column_across == at, keys, 0.0).astype(BF16) for at in range(GROUP)], axis=0
        )
        values = matmul(block, weight_ref[2, :, 2 * width : 3 * width]).astype(BF16)
        state = jnp.where(keep, matmul(spread_keys, values), 0.0).astype(BF16)
        query = feature(matmul(block, weight_ref[2, :, :width]))
        spread_query = jnp.concatenate(
            [jnp.where(column_down == at, query, 0.0).astype(BF16) for at in range(GROUP)], axis=1
        )
        gate = sigmoid(matmul(block, weight_ref[2, :, 3 * width :]))
        head_out = matmul(spread_query, state)
        mixed = (normalize(head_out, gain) * gate).astype(BF16)
        out = matmul(mixed, out_weight_ref[2]).astype(BF16)
        for part in range(parts):
            sent_ref[part, span, :] = out[part * piece : (part + 1) * piece]


def final_kernel(updated_ref, got_ref, gain_ref, up_ref, down_ref, out_ref):
    row_count, col_count, width = updated_ref.shape
    parts = got_ref.shape[0]
    cols = col_count // parts
    order = interleave(cols, row_count)
    gain = gain_ref[...]
    up = up_ref[...]
    down = down_ref[...]
    for part in range(parts):
        span = slice(part * cols, (part + 1) * cols)
        third = matmul(order, got_ref[part])
        updated = updated_ref[:, span, :].reshape(row_count * cols, width) + third
        trans_in = normalize(updated, gain).astype(BF16)
        hidden = matmul(trans_in, up)
        hidden = (hidden * sigmoid(hidden)).astype(BF16)
        result = (updated + matmul(hidden, down)).astype(BF16)
        out_ref[:, span, :] = result.reshape(row_count, cols, width)


def call(kernel, out_shape, name, flops):
    return pl.pallas_call(
        kernel,
        out_shape=out_shape,
        name=name,
        compiler_params=pltpu.CompilerParams(vmem_limit_bytes=VMEM_LIMIT),
        cost_estimate=pl.CostEstimate(flops=flops, bytes_accessed=1 << 20, transcendentals=0),
    )


def shards(
    parts,
    col_parts,
    pair_map,
    norm_gain,
    in_weights,
    head_gain,
    out_weights,
    trans_gain,
    up_weight,
    down_weight,
):
    row_count, col_count, width = pair_map.shape
    tokens = row_count * (col_count // parts)
    total = row_count * col_count
    struct = jax.ShapeDtypeStruct
    moved = struct((parts, tokens, width), BF16)
    square = total * width * width * 2

    normed, sent = call(
        functools.partial(norm_kernel, parts),
        (struct(pair_map.shape, BF16), moved),
        "norm",
        square,
    )(pair_map, norm_gain.reshape(1, width))
    got = lax.all_to_all(sent, "row", split_axis=0, concat_axis=0, tiled=True)

    state = call(
        state_kernel, struct((2, row_count, HEAD, width), BF16), "row_state", 6 * square
    )(normed, in_weights)
    step = 1
    while step < col_parts:
        pairs = [(at, at ^ step) for at in range(col_parts)]
        state = (state.astype(F32) + lax.ppermute(state, "col", pairs).astype(F32)).astype(BF16)
        step *= 2
    updated = call(row_kernel, struct(pair_map.shape, F32), "row_out", 8 * square)(
        pair_map, normed, state, in_weights, head_gain, out_weights
    )

    column_out = call(
        functools.partial(column_pass, row_count), moved, "column", 10 * square
    )(got, in_weights, head_gain, out_weights)
    third = lax.all_to_all(column_out, "row", split_axis=0, concat_axis=0, tiled=True)

    return call(final_kernel, struct(pair_map.shape, BF16), "final", 9 * square)(
        updated, third, trans_gain.reshape(1, width), up_weight, down_weight
    )


def solution(mesh):
    in_specs = (P("row", "col", None), P(), P(), P(), P(), P(), P(), P())
    out_specs = P("row", "col", None)
    body = functools.partial(shards, mesh.shape["row"], mesh.shape["col"])
    return jax.shard_map(body, mesh=mesh, in_specs=in_specs, out_specs=out_specs, check_vma=False)
```

time: 151 us -> 56.8 us (0.38)
  local copies, waits for them, and re-layouts: 46.9 us -> 1.74 us
  waiting for transfers between devices: 42 us -> 8.46 us
  matrix products: 22.2 us -> 0 us
  blocking collectives: 0 us -> 21.7 us
  Pallas kernels: 0 us -> 19.1 us
  between operations: 13.8 us -> 0.12 us
  other arithmetic: 12.8 us -> 0.04 us
  starting transfers between devices: 12.8 us -> 5.31 us
    psum x1 -> x0, waiting for transfers between devices: 32.4 us -> none  [shards(): lax.psum(partials[1].astype(jnp.bfloat16), 'col').astype(jnp.float32)]
    reshape x16 -> x0, local copies, waits for them, and re-layouts: 26 us -> none  [the longest x4 8.99 us: open_branch(): query_feat = feature(flat[:, :width]).astype(jnp.bfloat16).reshape(shape)]
    dot_general x12 -> x0, matrix products: 22.2 us -> none  [the longest x1 5.92 us: shards(): jnp.einsum('rcha,chab->rchb', query_feat, states, preferred_element_type=...]
    all_to_all x0 -> x1, blocking collectives: none -> 21.7 us  [shards(): got = lax.all_to_all(sent, 'row', split_axis=0, concat_axis=0, tiled=True)]
    pallas_call x0 -> x5, Pallas kernels: none -> 19.1 us  [the longest x1 9.93 us: shards(): call(functools.partial(column_pass, row_count), moved, 'column', 10 * squ...]
    convert_element_type x8 -> x2, other arithmetic: 11.3 us -> 0.04 us  [shards(): (state.astype(F32) + lax.ppermute(state, 'col', pairs).astype(F32)).astyp...]
    all_to_all x2 -> x1, starting transfers between devices: 12.8 us -> 3.67 us  [shards(): lax.all_to_all(column_out, 'row', split_axis=0, concat_axis=0, tiled=True)]
    convert_element_type x8 -> x0, local copies, waits for them, and re-layouts: 8.44 us -> none  [the longest x3 3.59 us: open_branch(): feature(flat[:, width:2 * width]).astype(jnp.bfloat16).reshape(shape)]
  transfers between devices with their start and end apart: 3 -> 3, of which waited for: 2 -> 3; matrix products, arithmetic and copies ran while one was open for 17% -> 0% of each run, Pallas kernels for 0% -> 7%
where the time goes in v1:
time: 56.8 us; the launch traced here: 56.5 us
  blocking collectives  21.7 us (38%)
  Pallas kernels  19.1 us (34%)
  waiting for transfers between devices  8.46 us (15%)
  starting transfers between devices  5.31 us (9%)
  local copies, waits for them, and re-layouts  1.74 us (3%)
    all_to_all x1, blocking collectives, shards(): got = lax.all_to_all(sent, 'row', split_axis=0, concat_axis=0, tiled=True)  21.7 us
    pallas_call x1, Pallas kernels, shards(): call(functools.partial(column_pass, row_count), moved, 'column', 10 * squ...  9.93 us
    pallas_call x1, Pallas kernels, shards(): call(final_kernel, struct(pair_map.shape, BF16), 'final', 9 * square)  4.66 us
    all_to_all x1, waiting for transfers between devices, shards(): lax.all_to_all(column_out, 'row', split_axis=0, concat_axis=0, tiled=True)  4.45 us
    ppermute x2, waiting for transfers between devices, shards(): lax.ppermute(state, 'col', pairs).astype(F32)  4.01 us
    all_to_all x1, starting transfers between devices, shards(): lax.all_to_all(column_out, 'row', split_axis=0, concat_axis=0, tiled=True)  3.67 us
    pallas_call x1, Pallas kernels, shards(): call(row_kernel, struct(pair_map.shape, F32), 'row_out', 8 * square)  2.27 us
    unnamed x18, local copies, waits for them, and re-layouts  1.74 us
  transfers between devices with their start and end apart: 3, of which 3 were waited for; matrix products, arithmetic and copies ran while one was open for 0% of the time, Pallas kernels for 7%

profile of v1, /device:TPU:0, one launch (start us, length us, event | category | flops | bytes accessed | tf_op | source)
XLA Modules:
  0.0 56.5 jit_solution(6708789975235339430)
XLA Ops:
  0.0 0.0 copy-start.7
  0.0 0.7 %copy-done.7 = f32[128]{0:T(128)S(1)} copy-done((f32[128]{0:T(128)S(1)}, f32[128]{0:T(128)}, u32[]{:S(2)}) %copy-start.7) | copy-done | bytes 536
  0.7 0.0 copy-start
  0.7 1.0 %copy-done = bf16[4,512,128]{2,1,0:T(8,128)(2,1)S(1)} copy-done((bf16[4,512,128]{2,1,0:T(8,128)(2,1)S(1)}, bf16[4,512,128]{2,1,0:T(8,128)(2,1)}, u32[]{:S(2)}) %copy-start) | copy-done | bytes 524312
  1.7 0.6 %norm.1 = (bf16[4,512,128]{2,1,0:T(8,128)(2,1)S(1)}, bf16[8,256,128]{2,1,0:T(8,128)(2,1)S(1)}) custom-call(bf16[4,512,128]{2,1,0:T(8,128)(2,1)S(1)} %copy-done, f32[1,128]{1,0:T(1,128)S(1)} %bitcast.2), custom_call_target="tpu_custom_call" | custom-call | flops 67108864 | bytes 1048576 | tf_op jit(solution)/shard_map/norm/pallas_call | solution.py:185
  2.3 0.0 copy-start.2
  2.3 0.0 copy-start.5
  2.3 0.0 copy-start.6
  2.3 21.7 %all_to_all.10.got_ref = bf16[8,256,128]{2,1,0:T(8,128)(2,1)S(1)} all-to-all(bf16[8,256,128]{2,1,0:T(8,128)(2,1)S(1)} %get-tuple-element.8), channel_id=1, replica_groups=mesh['row'=8,'col'=4] {'row'}, dimensions={0} | all-to-all | bytes 1048576 | tf_op jit(solution)/shard_map/all_to_all | solution.py:191
  24.1 0.0 copy-done.2
  24.1 0.0 copy-done.5
  24.1 0.0 copy-done.6
  24.1 9.9 %column.1 = bf16[8,256,128]{2,1,0:T(8,128)(2,1)} custom-call(bf16[8,256,128]{2,1,0:T(8,128)(2,1)S(1)} %all_to_all.10.got_ref, bf16[3,128,512]{2,1,0:T(8,128)(2,1)S(1)} %copy-done.2, f32[3,128]{1,0:T(4,128)S(1)} %copy-done.6, bf16[3,128,128]{2,1,0:T(8,128)(2,1)S(1)} %copy-done.5), custom_call_target="tpu_custom_call" | custom-call | flops 671088640 | bytes 1048576 | tf_op jit(solution)/shard_map/column/pallas_call | solution.py:205
  34.0 3.7 %all-to-all-start.1 = ((bf16[8,256,128]{2,1,0:T(8,128)(2,1)}), bf16[8,256,128]{2,1,0:T(8,128)(2,1)S(1)}, u32[]{:S(2)}, u32[]{:S(2)}) async-start(bf16[8,256,128]{2,1,0:T(8,128)(2,1)} %column.1), calls=%async_computation.1 | async-start | bytes 1048576 | tf_op jit(solution)/shard_map/all_to_all | solution.py:208
  37.7 0.0 copy-start.1
  37.7 1.6 %row_state.1 = bf16[2,4,32,128]{3,2,1,0:T(8,128)(2,1)S(1)} custom-call(bf16[4,512,128]{2,1,0:T(8,128)(2,1)S(1)} %get-tuple-element.7.normed_ref, bf16[3,128,512]{2,1,0:T(8,128)(2,1)S(1)} %copy-done.2), custom_call_target="tpu_custom_call" | custom-call | flops 402653184 | bytes 1048576 | tf_op jit(solution)/shard_map/row_state/pallas_call | solution.py:193
  39.3 0.1 collective-permute-start
  39.4 1.2 %collective-permute-done = bf16[2,4,32,128]{3,2,1,0:T(8,128)(2,1)S(1)} collective-permute-done((bf16[2,4,32,128]{3,2,1,0:T(8,128)(2,1)S(1)}, bf16[2,4,32,128]{3,2,1,0:T(8,128)(2,1)S(1)}, u32[]{:S(2)}, u32[]{:S(2)}) %collective-permute-start) | collective-permute-done | bytes 65568 | tf_op jit(solution)/shard_map/ppermute | solution.py:199
  40.7 1.6 %collective-permute-start.1 = (bf16[2,4,32,128]{3,2,1,0:T(8,128)(2,1)S(1)}, bf16[2,4,32,128]{3,2,1,0:T(8,128)(2,1)S(1)}, u32[]{:S(2)}, u32[]{:S(2)}) collective-permute-start(bf16[2,4,32,128]{3,2,1,0:T(8,128)(2,1)S(1)} %add_convert_fusion.1), channel_id=1, source_target_pairs={{0,2},{1,3},{2,0},{3,1},{4,6},{5,7},{6,4},{7,5},{8,10},{9,11},{10,... | collective-permute-start | bytes 196616 | tf_op jit(solution)/shard_map/ppermute | solution.py:199
  42.2 2.8 %collective-permute-done.1 = bf16[2,4,32,128]{3,2,1,0:T(8,128)(2,1)S(1)} collective-permute-done((bf16[2,4,32,128]{3,2,1,0:T(8,128)(2,1)S(1)}, bf16[2,4,32,128]{3,2,1,0:T(8,128)(2,1)S(1)}, u32[]{:S(2)}, u32[]{:S(2)}) %collective-permute-start.1) | collective-permute-done | bytes 65568 | tf_op jit(solution)/shard_map/ppermute | solution.py:199
  45.0 0.0 copy-done.1
  45.0 0.0 copy-start.3
  45.1 0.0 copy-start.4
  45.1 2.3 %row_out.1.updated_ref = f32[4,512,128]{2,1,0:T(8,128)S(1)} custom-call(bf16[4,512,128]{2,1,0:T(8,128)(2,1)S(1)} %copy-done.1, bf16[4,512,128]{2,1,0:T(8,128)(2,1)S(1)} %get-tuple-element.7.normed_ref, bf16[2,4,32,128]{3,2,1,0:T(8,128)(2,1)S(1)} %add_convert_fusion.state_ref, bf16[3,128,512]{2,1,0:T(8,128)(2,1)S(1)} %copy-done.2, f32[3,128]{1,0:T(4,128)S(1)} %copy-done.6, ...), custom_call_target="tpu_custom_call" | custom-call | flops 536870912 | bytes 1048576 | tf_op jit(solution)/shard_map/row_out/pallas_call | solution.py:201
  47.3 0.0 copy-start.8
  47.4 4.5 %all-to-all-done.1.got_ref = bf16[8,256,128]{2,1,0:T(8,128)(2,1)S(1)} async-done(((bf16[8,256,128]{2,1,0:T(8,128)(2,1)}), bf16[8,256,128]{2,1,0:T(8,128)(2,1)S(1)}, u32[]{:S(2)}, u32[]{:S(2)}) %all-to-all-start.1) | async-done | bytes 524320 | tf_op jit(solution)/shard_map/all_to_all | solution.py:208
  51.8 0.0 copy-done.3
  51.8 0.0 copy-done.4
  51.8 0.0 copy-done.8
  51.8 4.7 %final.1 = bf16[4,512,128]{2,1,0:T(8,128)(2,1)} custom-call(f32[4,512,128]{2,1,0:T(8,128)S(1)} %row_out.1.updated_ref, bf16[8,256,128]{2,1,0:T(8,128)(2,1)S(1)} %all-to-all-done.1.got_ref, f32[1,128]{1,0:T(1,128)S(1)} %bitcast.3, bf16[128,512]{1,0:T(8,128)(2,1)S(1)} %copy-done.3, bf16[512,128]{1,0:T(8,128)(2,1)S(1)} %copy-done.4), custom_call_target="tpu_custom_call" | custom-call | flops 603979776 | bytes 1048576 | tf_op jit(solution)/shard_map/final/pallas_call | solution.py:210
  (2 shorter events, 0.0 us)
Async XLA Ops:
  0.0 0.7 %copy-start.7 = (f32[128]{0:T(128)S(1)}, f32[128]{0:T(128)}, u32[]{:S(2)}) copy-start(f32[128]{0:T(128)} %param.9) | copy-start | bytes 1540
  0.7 1.0 %copy-start = (bf16[4,512,128]{2,1,0:T(8,128)(2,1)S(1)}, bf16[4,512,128]{2,1,0:T(8,128)(2,1)}, u32[]{:S(2)}) copy-start(bf16[4,512,128]{2,1,0:T(8,128)(2,1)} %x_ref.3) | copy-start | bytes 1572868
  2.3 21.8 %copy-start.2 = (bf16[3,128,512]{2,1,0:T(8,128)(2,1)S(1)}, bf16[3,128,512]{2,1,0:T(8,128)(2,1)}, u32[]{:S(2)}) copy-start(bf16[3,128,512]{2,1,0:T(8,128)(2,1)} %weight_ref.5) | copy-start | bytes 1179652
  2.3 21.8 %copy-start.5 = (bf16[3,128,128]{2,1,0:T(8,128)(2,1)S(1)}, bf16[3,128,128]{2,1,0:T(8,128)(2,1)}, u32[]{:S(2)}) copy-start(bf16[3,128,128]{2,1,0:T(8,128)(2,1)} %out_weight_ref.3) | copy-start | bytes 294916
  2.3 21.8 %copy-start.6 = (f32[3,128]{1,0:T(4,128)S(1)}, f32[3,128]{1,0:T(4,128)}, u32[]{:S(2)}) copy-start(f32[3,128]{1,0:T(4,128)} %head_gain_ref.3) | copy-start | bytes 4612
  34.0 17.8 %all-to-all-start.1 = ((bf16[8,256,128]{2,1,0:T(8,128)(2,1)}), bf16[8,256,128]{2,1,0:T(8,128)(2,1)S(1)}, u32[]{:S(2)}, u32[]{:S(2)}) async-start(bf16[8,256,128]{2,1,0:T(8,128)(2,1)} %column.1), calls=%async_computation.1 | async-start | bytes 1048576 | tf_op jit(solution)/shard_map/all_to_all | solution.py:208
  37.7 7.3 %copy-start.1 = (bf16[4,512,128]{2,1,0:T(8,128)(2,1)S(1)}, bf16[4,512,128]{2,1,0:T(8,128)(2,1)}, u32[]{:S(2)}) copy-start(bf16[4,512,128]{2,1,0:T(8,128)(2,1)} %x_ref.3) | copy-start | bytes 1572868
  39.3 1.3 %collective-permute-start = (bf16[2,4,32,128]{3,2,1,0:T(8,128)(2,1)S(1)}, bf16[2,4,32,128]{3,2,1,0:T(8,128)(2,1)S(1)}, u32[]{:S(2)}, u32[]{:S(2)}) collective-permute-start(bf16[2,4,32,128]{3,2,1,0:T(8,128)(2,1)S(1)} %row_state.1), channel_id=1, source_target_pairs={{0,1},{1,0},{2,3},{3,2},{4,5},{5,4},{6,7},{7,6},{8,9},{9,8},{10,11... | collective-permute-start | bytes 196616 | tf_op jit(solution)/shard_map/ppermute | solution.py:199
  40.7 4.3 %collective-permute-start.1 = (bf16[2,4,32,128]{3,2,1,0:T(8,128)(2,1)S(1)}, bf16[2,4,32,128]{3,2,1,0:T(8,128)(2,1)S(1)}, u32[]{:S(2)}, u32[]{:S(2)}) collective-permute-start(bf16[2,4,32,128]{3,2,1,0:T(8,128)(2,1)S(1)} %add_convert_fusion.1), channel_id=1, source_target_pairs={{0,2},{1,3},{2,0},{3,1},{4,6},{5,7},{6,4},{7,5},{8,10},{9,11},{10,... | collective-permute-start | bytes 196616 | tf_op jit(solution)/shard_map/ppermute | solution.py:199
  45.0 6.8 %copy-start.3 = (bf16[128,512]{1,0:T(8,128)(2,1)S(1)}, bf16[128,512]{1,0:T(8,128)(2,1)}, u32[]{:S(2)}) copy-start(bf16[128,512]{1,0:T(8,128)(2,1)} %up_ref.1) | copy-start | bytes 393220
  45.1 6.8 %copy-start.4 = (bf16[512,128]{1,0:T(8,128)(2,1)S(1)}, bf16[512,128]{1,0:T(8,128)(2,1)}, u32[]{:S(2)}) copy-start(bf16[512,128]{1,0:T(8,128)(2,1)} %down_ref.1) | copy-start | bytes 393220
  47.3 4.5 %copy-start.8 = (f32[128]{0:T(128)S(1)}, f32[128]{0:T(128)}, u32[]{:S(2)}) copy-start(f32[128]{0:T(128)} %param.13) | copy-start | bytes 1540

commit v2 on v1

v2 whole, which is shorter than its diff:
```python
import functools

import jax
import jax.numpy as jnp
from jax import lax
from jax.experimental import pallas as pl
from jax.experimental.pallas import tpu as pltpu
from jax.sharding import PartitionSpec as P

HEAD = 32
GROUP = 4
EPSILON = 1e-05
CHUNK = 512
VMEM_LIMIT = 24 * 1024 * 1024

F32 = jnp.float32
BF16 = jnp.bfloat16


def matmul(a, b):
    return jnp.dot(a, b, preferred_element_type=F32)


def matmul_nt(a, b):
    return lax.dot_general(a, b, (((1,), (1,)), ((), ())), preferred_element_type=F32)


def feature(values):
    return jnp.exp(jnp.minimum(values, 0.0)) + jnp.maximum(values, 0.0)


def sigmoid(values):
    return 0.5 * jnp.tanh(0.5 * values) + 0.5


def normalize(values, gain):
    meansq = jnp.mean(values * values, axis=-1, keepdims=True)
    return values * lax.rsqrt(meansq + EPSILON) * gain


def iota(shape, axis):
    return lax.broadcasted_iota(jnp.int32, shape, axis)


def head_mask(rows, width):
    return ((iota((rows, width), 0) % width) // HEAD) == (iota((rows, width), 1) // HEAD)


def interleave(row_count, cols):
    count = row_count * cols
    out = iota((count, count), 0)
    src = iota((count, count), 1)
    hit = (out // row_count == src % cols) & (out % row_count == src // cols)
    return hit.astype(F32).astype(BF16)


def norm_kernel(x_ref, gain_ref, normed_ref, *sent_refs):
    row_count, col_count, width = x_ref.shape
    parts = len(sent_refs)
    cols = col_count // parts
    me = lax.axis_index("row")
    order = interleave(row_count, cols)
    gain = gain_ref[:1]
    for step in range(parts):
        span = pl.ds(pl.multiple_of((me ^ step) * cols, cols), cols)
        block = x_ref[:, span, :].astype(F32).reshape(row_count * cols, width)
        normed = normalize(block, gain).astype(BF16)
        normed_ref[:, span, :] = normed.reshape(row_count, cols, width)
        sent_refs[step][...] = matmul(order, normed).astype(BF16)


def state_kernel(normed_ref, weight_ref, after_ref, state_ref):
    row_count, col_count, width = normed_ref.shape
    keep = head_mask(width, width)
    for branch in range(2):
        key_weight = weight_ref[branch, :, width : 2 * width].T
        value_weight = weight_ref[branch, :, 2 * width : 3 * width]
        for row in range(row_count):
            normed = normed_ref[row]
            keys = feature(matmul_nt(key_weight, normed)).astype(BF16)
            values = matmul(normed, value_weight).astype(BF16)
            state = jnp.where(keep, matmul(keys, values), 0.0)
            packed = state[:HEAD]
            for head in range(1, width // HEAD):
                packed = packed + state[head * HEAD : (head + 1) * HEAD]
            state_ref[branch, row] = packed.astype(BF16)


def row_kernel(
    x_ref, normed_ref, state_ref, weight_ref, head_gain_ref, out_weight_ref, gain_ref, updated_ref, gain_out_ref
):
    row_count, col_count, width = normed_ref.shape
    keep = head_mask(width, width)
    heads = width // HEAD
    gain_out_ref[...] = gain_ref[...]
    for row in range(row_count):
        normed = normed_ref[row]
        total = x_ref[row].astype(F32)
        for branch in range(2):
            packed = state_ref[branch, row].astype(F32)
            state = jnp.where(keep, jnp.concatenate([packed] * heads, axis=0), 0.0).astype(BF16)
            query = feature(matmul(normed, weight_ref[branch, :, :width])).astype(BF16)
            gate = sigmoid(matmul(normed, weight_ref[branch, :, 3 * width :]))
            head_out = matmul(query, state)
            mixed = (normalize(head_out, head_gain_ref[branch : branch + 1]) * gate).astype(BF16)
            total = total + matmul(mixed, out_weight_ref[branch]).astype(BF16).astype(F32)
        updated_ref[row] = total


def column_kernel(row_count, order, weight_ref, head_gain_ref, out_weight_ref, *refs):
    parts = len(order)
    got_refs = refs[:parts]
    sent_refs = refs[parts + 1 : 2 * parts + 1]
    block_ref, query_ref, key_ref, value_ref, gate_ref, head_ref = refs[2 * parts + 1 :]
    tokens, width = got_refs[0].shape
    piece = GROUP * row_count
    size = parts * piece
    groups = tokens // piece
    total = parts * tokens
    for step, got_ref in zip(order, got_refs):
        for group in range(groups):
            start = group * size + step * piece
            block_ref[start : start + piece] = got_ref[group * piece : (group + 1) * piece]
    key_weight = weight_ref[2, :, width : 2 * width].T
    for start in range(0, total, CHUNK):
        span = slice(start, start + CHUNK)
        block = block_ref[span]
        query_ref[span] = feature(matmul(block, weight_ref[2, :, :width])).astype(BF16)
        value_ref[span] = matmul(block, weight_ref[2, :, 2 * width : 3 * width]).astype(BF16)
        gate_ref[span] = sigmoid(matmul(block, weight_ref[2, :, 3 * width :]))
        key_ref[:, span] = feature(matmul_nt(key_weight, block)).astype(BF16)
    keep = head_mask(GROUP * width, width).astype(F32).astype(BF16)
    down = (iota((size, width), 0) // row_count) % GROUP
    across = (iota((width, size), 1) // row_count) % GROUP
    down = [(down == at).astype(F32).astype(BF16) for at in range(GROUP)]
    across = [(across == at).astype(F32).astype(BF16) for at in range(GROUP)]
    for group in range(groups):
        span = slice(group * size, (group + 1) * size)
        keys = key_ref[:, span]
        query = query_ref[span]
        spread_keys = jnp.concatenate([keys * mask for mask in across], axis=0)
        state = matmul(spread_keys, value_ref[span]).astype(BF16) * keep
        spread_query = jnp.concatenate([query * mask for mask in down], axis=1)
        head_ref[span] = matmul(spread_query, state)
    gain = head_gain_ref[2:3]
    for start in range(0, total, CHUNK):
        span = slice(start, start + CHUNK)
        mixed = (normalize(head_ref[span], gain) * gate_ref[span]).astype(BF16)
        query_ref[span] = matmul(mixed, out_weight_ref[2]).astype(BF16)
    for step in range(parts):
        for group in range(groups):
            start = group * size + step * piece
            sent_refs[step][group * piece : (group + 1) * piece] = query_ref[start : start + piece]


def final_kernel(steps, parts, fresh, updated_ref, gain_ref, up_ref, down_ref, *refs):
    row_count, col_count, width = updated_ref.shape
    got_refs = refs[: len(steps)]
    out_hbm, sum_ref, trans_ref, hidden_ref, out_ref, sems = refs[len(steps) + (not fresh) :]
    cols = col_count // parts
    tokens = row_count * cols
    me = lax.axis_index("row")
    order = interleave(cols, row_count)
    gain = gain_ref[...]
    spans = [pl.ds(pl.multiple_of((me ^ step) * cols, cols), cols) for step in steps]
    for at, got_ref in enumerate(got_refs):
        span = slice(at * tokens, (at + 1) * tokens)
        third = matmul(order, got_ref[...])
        updated = updated_ref[:, spans[at], :].reshape(tokens, width) + third
        sum_ref[span] = updated
        trans_ref[span] = normalize(updated, gain).astype(BF16)
    for at in range(len(steps)):
        span = slice(at * tokens, (at + 1) * tokens)
        half = 0.5 * matmul(trans_ref[span], up_ref[...])
        hidden_ref[span] = (half * jnp.tanh(half) + half).astype(BF16)
    stores = []
    for at in range(len(steps)):
        span = slice(at * tokens, (at + 1) * tokens)
        result = (sum_ref[span] + matmul(hidden_ref[span], down_ref[...])).astype(BF16)
        out_ref[at] = result.reshape(row_count, cols, width)
        store = pltpu.make_async_copy(out_ref.at[at], out_hbm.at[:, spans[at], :], sems.at[at])
        store.start()
        stores.append(store)
    for store in stores:
        store.wait()


def send_order(parts):
    first = [0, 1, *range(parts // 2, parts), *range(2, parts // 2)]
    return tuple(dict.fromkeys(first[:parts] if parts < 4 else first))


def exchange(pieces):
    parts = len(pieces)
    moved = list(pieces)
    for step in range(parts - 1, 0, -1):
        pairs = [(at, at ^ step) for at in range(parts)]
        moved[step] = lax.ppermute(pieces[step], "row", pairs)
    return moved


def call(kernel, out_shape, name, flops, vmem_limit=VMEM_LIMIT, **kwargs):
    return pl.pallas_call(
        kernel,
        out_shape=out_shape,
        name=name,
        compiler_params=pltpu.CompilerParams(vmem_limit_bytes=vmem_limit),
        cost_estimate=pl.CostEstimate(flops=0, bytes_accessed=0, transcendentals=0),
        **kwargs,
    )


def shards(
    parts,
    col_parts,
    pair_map,
    norm_gain,
    in_weights,
    head_gain,
    out_weights,
    trans_gain,
    up_weight,
    down_weight,
):
    row_count, col_count, width = pair_map.shape
    cols = col_count // parts
    tokens = row_count * cols
    total = row_count * col_count
    hidden = up_weight.shape[1]
    struct = jax.ShapeDtypeStruct
    square = total * width * width * 2
    vmem = pl.BlockSpec(memory_space=pltpu.VMEM)
    anywhere = pl.BlockSpec(memory_space=pl.ANY)

    normed, *sent = call(
        norm_kernel,
        [struct(pair_map.shape, BF16)] + [struct((tokens, width), BF16)] * parts,
        "norm",
        square,
    )(pair_map, jnp.broadcast_to(norm_gain, (8, width)))
    got = exchange(sent)

    state = call(
        state_kernel,
        struct((2, row_count, HEAD, width), BF16),
        "row_state",
        6 * square,
        in_specs=[vmem] * 2 + [anywhere],
    )(normed, in_weights, got[1])
    state0 = state
    step = 1
    while step < col_parts:
        pairs = [(at, at ^ step) for at in range(col_parts)]
        state = (state.astype(F32) + lax.ppermute(state, "col", pairs).astype(F32)).astype(BF16)
        if step == 1:
            state1 = state
        step *= 2
    updated, gain = call(
        row_kernel,
        (struct(pair_map.shape, F32), struct((1, width), F32)),
        "row_out",
        8 * square,
    )(pair_map, normed, state, in_weights, head_gain, out_weights, trans_gain.reshape(1, width))

    order = send_order(parts)
    column_out = call(
        functools.partial(column_kernel, row_count, order),
        [struct((tokens, width), BF16)] * parts,
        "column",
        10 * square,
        in_specs=[vmem] * (3 + parts) + [anywhere],
        scratch_shapes=[
            pltpu.VMEM((total, width), BF16),
            pltpu.VMEM((total, width), BF16),
            pltpu.VMEM((width, total), BF16),
            pltpu.VMEM((total, width), BF16),
            pltpu.VMEM((total, width), F32),
            pltpu.VMEM((total, width), F32),
        ],
    )(in_weights, head_gain, out_weights, *[got[step] for step in order], normed)

    third = exchange(column_out)

    result = None
    for steps in (order,):
        fresh = result is None
        count = len(steps)
        result = call(
            functools.partial(final_kernel, steps, parts, fresh),
            struct(pair_map.shape, BF16),
            "final",
            9 * square * count // parts,
            in_specs=[vmem] * (4 + count) + [anywhere] * (not fresh),
            out_specs=anywhere,
            input_output_aliases={} if fresh else {4 + count: 0},
            scratch_shapes=[
                pltpu.VMEM((count * tokens, width), F32),
                pltpu.VMEM((count * tokens, width), BF16),
                pltpu.VMEM((count * tokens, hidden), BF16),
                pltpu.VMEM((count, row_count, cols, width), BF16),
                pltpu.SemaphoreType.DMA((count,)),
            ],
        )(
            updated,
            gain,
            up_weight,
            down_weight,
            *[third[step] for step in steps],
            *([] if fresh else [result]),
        )
    return result


def solution(mesh):
    in_specs = (P("row", "col", None), P(), P(), P(), P(), P(), P(), P())
    out_specs = P("row", "col", None)
    body = functools.partial(shards, mesh.shape["row"], mesh.shape["col"])
    return jax.shard_map(body, mesh=mesh, in_specs=in_specs, out_specs=out_specs, check_vma=False)
```

time: 56.8 us -> 42.4 us (0.75)
  blocking collectives: 21.7 us -> 0 us
  starting transfers between devices: 5.31 us -> 25.3 us
  Pallas kernels: 19.1 us -> 9.46 us
  waiting for transfers between devices: 8.46 us -> 4.99 us
  local copies, waits for them, and re-layouts: 1.74 us -> 2.42 us
    ppermute x0 -> x14, starting transfers between devices: none -> 23.7 us  [exchange(): moved[step] = lax.ppermute(pieces[step], 'row', pairs)]
    all_to_all x1 -> x0, blocking collectives: 21.7 us -> none  [shards(): got = lax.all_to_all(sent, 'row', split_axis=0, concat_axis=0, tiled=True)]
    pallas_call x4, Pallas kernels: 17.5 us -> 7.85 us  [the longest x1 2.57 us: shards(): call(functools.partial(final_kernel, steps, parts, fresh), struct(pair_ma...]
    ppermute x0 -> x14, waiting for transfers between devices: none -> 4.98 us  [exchange(): moved[step] = lax.ppermute(pieces[step], 'row', pairs)]
    all_to_all x1 -> x0, waiting for transfers between devices: 4.45 us -> none  [shards(): lax.all_to_all(column_out, 'row', split_axis=0, concat_axis=0, tiled=True)]
    ppermute x2, waiting for transfers between devices: 4.01 us -> 0.01 us  [shards(): lax.ppermute(state, 'col', pairs).astype(F32)]
    all_to_all x1 -> x0, starting transfers between devices: 3.67 us -> none  [shards(): lax.all_to_all(column_out, 'row', split_axis=0, concat_axis=0, tiled=True)]
    broadcast_in_dim x0 -> x1, local copies, waits for them, and re-layouts: none -> 0.71 us  [shards(): jnp.broadcast_to(norm_gain, (8, width))]
  transfers between devices with their start and end apart: 3 -> 16, of which waited for: 3 -> 6; matrix products, arithmetic and copies ran while one was open for 0% -> 0% of each run, Pallas kernels for 7% -> 15%
where the time goes in v2:
time: 42.4 us; the launch traced here: 42.3 us
  starting transfers between devices  25.3 us (60%)
  Pallas kernels  9.46 us (22%)
  waiting for transfers between devices  4.99 us (12%)
  local copies, waits for them, and re-layouts  2.42 us (6%)
    ppermute x14, starting transfers between devices, exchange(): moved[step] = lax.ppermute(pieces[step], 'row', pairs)  23.7 us
    ppermute x14, waiting for transfers between devices, exchange(): moved[step] = lax.ppermute(pieces[step], 'row', pairs)  4.98 us
    pallas_call x1, Pallas kernels, shards(): call(functools.partial(final_kernel, steps, parts, fresh), struct(pair_ma...  2.57 us
    pallas_call x1, Pallas kernels, shards(): call(functools.partial(column_kernel, row_count, order), [struct((tokens,...  2.41 us
    pallas_call x1, Pallas kernels, shards(): call(row_kernel, (struct(pair_map.shape, F32), struct((1, width), F32)),...  2.27 us
    unnamed x14, local copies, waits for them, and re-layouts  1.71 us
    pallas_call x1, Pallas kernels, shards(): call(state_kernel, struct((2, row_count, HEAD, width), BF16), 'row_state'...  1.61 us
    ppermute x2, starting transfers between devices, shards(): lax.ppermute(state, 'col', pairs).astype(F32)  1.56 us
  transfers between devices with their start and end apart: 16, of which 6 were waited for; matrix products, arithmetic and copies ran while one was open for 0% of the time, Pallas kernels for 15%

profile of v2, /device:TPU:0, one launch (start us, length us, event | category | flops | bytes accessed | tf_op | source)
XLA Modules:
  0.0 42.3 jit_solution(13602836001809988804)
XLA Ops:
  0.0 0.0 copy-start
  0.0 0.7 %broadcast_in_dim.3.gain_ref = f32[8,128]{1,0:T(8,128)S(1)} broadcast(f32[128]{0:T(128)} %param.9), dimensions={1} | broadcast | bytes 4608 | tf_op jit(solution)/shard_map/broadcast_in_dim | solution.py:240
  0.7 0.0 copy-start.1
  0.7 1.0 %copy-done.1 = bf16[4,512,128]{2,1,0:T(8,128)(2,1)S(1)} copy-done((bf16[4,512,128]{2,1,0:T(8,128)(2,1)S(1)}, bf16[4,512,128]{2,1,0:T(8,128)(2,1)}, u32[]{:S(2)}) %copy-start.1) | copy-done | bytes 524312
  1.8 0.6 %norm.1 = (bf16[4,512,128]{2,1,0:T(8,128)(2,1)S(1)}, bf16[256,128]{1,0:T(8,128)(2,1)S(1)}, bf16[256,128]{1,0:T(8,128)(2,1)S(1)}, bf16[256,128]{1,0:T(8,128)(2,1)...) custom-call(bf16[4,512,128]{2,1,0:T(8,128)(2,1)S(1)} %copy-done.1, ...), custom_call_target="tpu_custom_call" | custom-call | tf_op jit(solution)/shard_map/norm/pallas_call | solution.py:235
  2.4 3.0 %collective-permute-start = (bf16[256,128]{1,0:T(8,128)(2,1)S(1)}, bf16[256,128]{1,0:T(8,128)(2,1)S(1)}, u32[]{:S(2)}, u32[]{:S(2)}) collective-permute-start(bf16[256,128]{1,0:T(8,128)(2,1)S(1)} %get-tuple-element.25), channel_id=1, source_target_pairs={{0,4},{4,0},{8,12},{12,8},{16,20},{20,16},{24,28},{28,24},{1,5},{5... | collective-permute-start | bytes 196616 | tf_op jit(solution)/shard_map/ppermute | solution.py:198
  5.4 2.6 %collective-permute-start.3 = (bf16[256,128]{1,0:T(8,128)(2,1)S(1)}, bf16[256,128]{1,0:T(8,128)(2,1)S(1)}, u32[]{:S(2)}, u32[]{:S(2)}) collective-permute-start(bf16[256,128]{1,0:T(8,128)(2,1)S(1)} %get-tuple-element.29), channel_id=1, source_target_pairs={{0,16},{4,20},{8,24},{12,28},{16,0},{20,4},{24,8},{28,12},{1,17},{... | collective-permute-start | bytes 196616 | tf_op jit(solution)/shard_map/ppermute | solution.py:198
  8.0 0.0 collective-permute-start.4
  8.0 3.9 %collective-permute-start.5 = (bf16[256,128]{1,0:T(8,128)(2,1)S(1)}, bf16[256,128]{1,0:T(8,128)(2,1)S(1)}, u32[]{:S(2)}, u32[]{:S(2)}) collective-permute-start(bf16[256,128]{1,0:T(8,128)(2,1)S(1)} %get-tuple-element.31), channel_id=1, source_target_pairs={{0,24},{4,28},{8,16},{12,20},{16,8},{20,12},{24,0},{28,4},{1,25},{... | collective-permute-start | bytes 196616 | tf_op jit(solution)/shard_map/ppermute | solution.py:198
  11.9 1.2 %collective-permute-start.6 = (bf16[256,128]{1,0:T(8,128)(2,1)S(1)}, bf16[256,128]{1,0:T(8,128)(2,1)S(1)}, u32[]{:S(2)}, u32[]{:S(2)}) collective-permute-start(bf16[256,128]{1,0:T(8,128)(2,1)S(1)} %get-tuple-element.32), channel_id=1, source_target_pairs={{0,28},{4,24},{8,20},{12,16},{16,12},{20,8},{24,4},{28,0},{1,29},{... | collective-permute-start | bytes 196616 | tf_op jit(solution)/shard_map/ppermute | solution.py:198
  13.0 0.0 collective-permute-done.after_ref.refs_1_
  13.0 0.0 collective-permute-start.7
  13.1 0.1 collective-permute-done.3.refs_2_
  13.2 1.7 %collective-permute-start.8 = (bf16[256,128]{1,0:T(8,128)(2,1)S(1)}, bf16[256,128]{1,0:T(8,128)(2,1)S(1)}, u32[]{:S(2)}, u32[]{:S(2)}) collective-permute-start(bf16[256,128]{1,0:T(8,128)(2,1)S(1)} %get-tuple-element.34), channel_id=1, source_target_pairs={{0,12},{4,8},{8,4},{12,0},{16,28},{20,24},{24,20},{28,16},{1,13},{... | collective-permute-start | bytes 196616 | tf_op jit(solution)/shard_map/ppermute | solution.py:198
  14.9 0.0 copy-done
  14.9 0.0 copy-start.2
  14.9 0.0 copy-start.5
  14.9 1.6 %row_state.1 = bf16[2,4,32,128]{3,2,1,0:T(8,128)(2,1)S(1)} custom-call(bf16[4,512,128]{2,1,0:T(8,128)(2,1)S(1)} %get-tuple-element.24.normed_ref.refs_8_, bf16[3,128,512]{2,1,0:T(8,128)(2,1)S(1)} %copy-done, bf16[256,128]{1,0:T(8,128)(2,1)S(1)} %collective-permute-done.after_ref.refs_1_), custom_call_target="tpu_custom_call" | custom-call | tf_op jit(solution)/shard_map/row_state/pallas_call | solution.py:243
  16.5 1.3 %collective-permute-done.4.refs_3_ = bf16[256,128]{1,0:T(8,128)(2,1)S(1)} collective-permute-done((bf16[256,128]{1,0:T(8,128)(2,1)S(1)}, bf16[256,128]{1,0:T(8,128)(2,1)S(1)}, u32[]{:S(2)}, u32[]{:S(2)}) %collective-permute-start.4) | collective-permute-done | bytes 65568 | tf_op jit(solution)/shard_map/ppermute | solution.py:198
  17.7 0.0 collective-permute-start.1
  17.7 0.0 collective-permute-done.5.refs_4_
  17.7 1.6 %collective-permute-done.6.refs_5_ = bf16[256,128]{1,0:T(8,128)(2,1)S(1)} collective-permute-done((bf16[256,128]{1,0:T(8,128)(2,1)S(1)}, bf16[256,128]{1,0:T(8,128)(2,1)S(1)}, u32[]{:S(2)}, u32[]{:S(2)}) %collective-permute-start.6) | collective-permute-done | bytes 65568 | tf_op jit(solution)/shard_map/ppermute | solution.py:198
  19.4 0.0 collective-permute-done.7.refs_6_
  19.4 0.6 %collective-permute-done.8.refs_7_ = bf16[256,128]{1,0:T(8,128)(2,1)S(1)} collective-permute-done((bf16[256,128]{1,0:T(8,128)(2,1)S(1)}, bf16[256,128]{1,0:T(8,128)(2,1)S(1)}, u32[]{:S(2)}, u32[]{:S(2)}) %collective-permute-start.8) | collective-permute-done | bytes 65568 | tf_op jit(solution)/shard_map/ppermute | solution.py:198
  19.9 0.0 copy-done.2
  19.9 0.0 copy-done.5
  19.9 2.4 %column.1 = (bf16[256,128]{1,0:T(8,128)(2,1)S(1)}, bf16[256,128]{1,0:T(8,128)(2,1)S(1)}, bf16[256,128]{1,0:T(8,128)(2,1)S(1)}, bf16[256,128]{1,0:T(8,128)(2,1)S(...) custom-call(bf16[3,128,512]{2,1,0:T(8,128)(2,1)S(1)} %copy-done, ...), custom_call_target="tpu_custom_call" | custom-call | tf_op jit(solution)/shard_map/column/pallas_call | solution.py:266
  22.3 1.6 %collective-permute-start.9 = (bf16[256,128]{1,0:T(8,128)(2,1)S(1)}, bf16[256,128]{1,0:T(8,128)(2,1)S(1)}, u32[]{:S(2)}, u32[]{:S(2)}) collective-permute-start(bf16[256,128]{1,0:T(8,128)(2,1)S(1)} %get-tuple-element.36), channel_id=1, source_target_pairs={{0,4},{4,0},{8,12},{12,8},{16,20},{20,16},{24,28},{28,24},{1,5},{5... | collective-permute-start | bytes 196616 | tf_op jit(solution)/shard_map/ppermute | solution.py:198
  23.9 3.0 %collective-permute-start.10 = (bf16[256,128]{1,0:T(8,128)(2,1)S(1)}, bf16[256,128]{1,0:T(8,128)(2,1)S(1)}, u32[]{:S(2)}, u32[]{:S(2)}) collective-permute-start(bf16[256,128]{1,0:T(8,128)(2,1)S(1)} %get-tuple-element.37), channel_id=1, source_target_pairs={{0,16},{4,20},{8,24},{12,28},{16,0},{20,4},{24,8},{28,12},{1,17},{... | collective-permute-start | bytes 196616 | tf_op jit(solution)/shard_map/ppermute | solution.py:198
  26.9 0.0 collective-permute-done.1
  26.9 1.6 %collective-permute-start.2 = (bf16[2,4,32,128]{3,2,1,0:T(8,128)(2,1)S(1)}, bf16[2,4,32,128]{3,2,1,0:T(8,128)(2,1)S(1)}, u32[]{:S(2)}, u32[]{:S(2)}) collective-permute-start(bf16[2,4,32,128]{3,2,1,0:T(8,128)(2,1)S(1)} %add_convert_fusion.1), channel_id=1, source_target_pairs={{0,2},{1,3},{2,0},{3,1},{4,6},{5,7},{6,4},{7,5},{8,10},{9,11},{10,... | collective-permute-start | bytes 196616 | tf_op jit(solution)/shard_map/ppermute | solution.py:254
  28.5 0.0 collective-permute-start.11
  28.5 3.2 %collective-permute-start.12 = (bf16[256,128]{1,0:T(8,128)(2,1)S(1)}, bf16[256,128]{1,0:T(8,128)(2,1)S(1)}, u32[]{:S(2)}, u32[]{:S(2)}) collective-permute-start(bf16[256,128]{1,0:T(8,128)(2,1)S(1)} %get-tuple-element.39), channel_id=1, source_target_pairs={{0,24},{4,28},{8,16},{12,20},{16,8},{20,12},{24,0},{28,4},{1,25},{... | collective-permute-start | bytes 196616 | tf_op jit(solution)/shard_map/ppermute | solution.py:198
  31.7 0.0 collective-permute-done.9.refs_1_
  31.7 1.5 %collective-permute-start.13 = (bf16[256,128]{1,0:T(8,128)(2,1)S(1)}, bf16[256,128]{1,0:T(8,128)(2,1)S(1)}, u32[]{:S(2)}, u32[]{:S(2)}) collective-permute-start(bf16[256,128]{1,0:T(8,128)(2,1)S(1)} %get-tuple-element.40), channel_id=1, source_target_pairs={{0,28},{4,24},{8,20},{12,16},{16,12},{20,8},{24,4},{28,0},{1,29},{... | collective-permute-start | bytes 196616 | tf_op jit(solution)/shard_map/ppermute | solution.py:198
  33.2 0.0 collective-permute-done.10.refs_2_
  33.2 0.0 collective-permute-start.14
  33.2 0.0 collective-permute-done.2
  33.2 2.0 %collective-permute-start.15 = (bf16[256,128]{1,0:T(8,128)(2,1)S(1)}, bf16[256,128]{1,0:T(8,128)(2,1)S(1)}, u32[]{:S(2)}, u32[]{:S(2)}) collective-permute-start(bf16[256,128]{1,0:T(8,128)(2,1)S(1)} %get-tuple-element.42), channel_id=1, source_target_pairs={{0,12},{4,8},{8,4},{12,0},{16,28},{20,24},{24,20},{28,16},{1,13},{... | collective-permute-start | bytes 196616 | tf_op jit(solution)/shard_map/ppermute | solution.py:198
  35.3 0.0 copy-start.6
  35.3 0.6 %copy-done.6 = f32[128]{0:T(128)S(1)} copy-done((f32[128]{0:T(128)S(1)}, f32[128]{0:T(128)}, u32[]{:S(2)}) %copy-start.6) | copy-done | bytes 536
  35.9 0.0 copy-start.3
  35.9 0.0 copy-start.4
  35.9 2.3 %row_out.1 = (f32[4,512,128]{2,1,0:T(8,128)S(1)}, f32[1,128]{1,0:T(1,128)S(1)}) custom-call(bf16[4,512,128]{2,1,0:T(8,128)(2,1)S(1)} %copy-done.1, bf16[4,512,128]{2,1,0:T(8,128)(2,1)S(1)} %get-tuple-element.24.normed_ref.refs_8_, bf16[2,4,32,128]{3,2,1,0:T(8,128)(2,1)S(1)} %add_convert_fusion.state_ref, bf16[3,128,512]{2,1,0:T(8,128)(2,1)S(1)} %copy-done, ...), custom_call_target="tpu_custom_call" | custom-call | tf_op jit(solution)/shard_map/row_out/pallas_call | solution.py:258
  38.2 0.0 collective-permute-done.11.refs_3_
  38.2 0.0 collective-permute-done.12.refs_4_
  38.2 1.2 %collective-permute-done.13.refs_5_ = bf16[256,128]{1,0:T(8,128)(2,1)S(1)} collective-permute-done((bf16[256,128]{1,0:T(8,128)(2,1)S(1)}, bf16[256,128]{1,0:T(8,128)(2,1)S(1)}, u32[]{:S(2)}, u32[]{:S(2)}) %collective-permute-start.13) | collective-permute-done | bytes 65568 | tf_op jit(solution)/shard_map/ppermute | solution.py:198
  39.4 0.0 collective-permute-done.14.refs_6_
  39.4 0.3 collective-permute-done.15.refs_7_
  39.7 0.0 copy-done.3
  39.7 0.0 copy-done.4
  39.7 2.6 %final.1 = bf16[4,512,128]{2,1,0:T(8,128)(2,1)} custom-call(f32[4,512,128]{2,1,0:T(8,128)S(1)} %get-tuple-element.26.updated_ref, f32[1,128]{1,0:T(1,128)S(1)} %get-tuple-element.27.gain_ref, bf16[128,512]{1,0:T(8,128)(2,1)S(1)} %copy-done.3, bf16[512,128]{1,0:T(8,128)(2,1)S(1)} %copy-done.4, bf16[256,128]{1,0:T(8,128)(2,1)S(1)} %get-tuple-element.35.refs_0_, ...), custom_call_target="tpu_custom_call" | custom-call | tf_op jit(solution)/shard_map/final/pallas_call | solution.py:288
  (2 shorter events, 0.0 us)
Async XLA Ops:
  0.0 14.9 %copy-start = (bf16[3,128,512]{2,1,0:T(8,128)(2,1)S(1)}, bf16[3,128,512]{2,1,0:T(8,128)(2,1)}, u32[]{:S(2)}) copy-start(bf16[3,128,512]{2,1,0:T(8,128)(2,1)} %weight_ref.5) | copy-start | bytes 1179652
  0.7 1.0 %copy-start.1 = (bf16[4,512,128]{2,1,0:T(8,128)(2,1)S(1)}, bf16[4,512,128]{2,1,0:T(8,128)(2,1)}, u32[]{:S(2)}) copy-start(bf16[4,512,128]{2,1,0:T(8,128)(2,1)} %x_ref.3) | copy-start | bytes 1572868
  2.4 10.7 %collective-permute-start = (bf16[256,128]{1,0:T(8,128)(2,1)S(1)}, bf16[256,128]{1,0:T(8,128)(2,1)S(1)}, u32[]{:S(2)}, u32[]{:S(2)}) collective-permute-start(bf16[256,128]{1,0:T(8,128)(2,1)S(1)} %get-tuple-element.25), channel_id=1, source_target_pairs={{0,4},{4,0},{8,12},{12,8},{16,20},{20,16},{24,28},{28,24},{1,5},{5... | collective-permute-start | bytes 196616 | tf_op jit(solution)/shard_map/ppermute | solution.py:198
  5.4 7.8 %collective-permute-start.3 = (bf16[256,128]{1,0:T(8,128)(2,1)S(1)}, bf16[256,128]{1,0:T(8,128)(2,1)S(1)}, u32[]{:S(2)}, u32[]{:S(2)}) collective-permute-start(bf16[256,128]{1,0:T(8,128)(2,1)S(1)} %get-tuple-element.29), channel_id=1, source_target_pairs={{0,16},{4,20},{8,24},{12,28},{16,0},{20,4},{24,8},{28,12},{1,17},{... | collective-permute-start | bytes 196616 | tf_op jit(solution)/shard_map/ppermute | solution.py:198
  8.0 9.8 %collective-permute-start.4 = (bf16[256,128]{1,0:T(8,128)(2,1)S(1)}, bf16[256,128]{1,0:T(8,128)(2,1)S(1)}, u32[]{:S(2)}, u32[]{:S(2)}) collective-permute-start(bf16[256,128]{1,0:T(8,128)(2,1)S(1)} %get-tuple-element.30), channel_id=1, source_target_pairs={{0,20},{4,16},{8,28},{12,24},{16,4},{20,0},{24,12},{28,8},{1,21},{... | collective-permute-start | bytes 196616 | tf_op jit(solution)/shard_map/ppermute | solution.py:198
  8.0 9.8 %collective-permute-start.5 = (bf16[256,128]{1,0:T(8,128)(2,1)S(1)}, bf16[256,128]{1,0:T(8,128)(2,1)S(1)}, u32[]{:S(2)}, u32[]{:S(2)}) collective-permute-start(bf16[256,128]{1,0:T(8,128)(2,1)S(1)} %get-tuple-element.31), channel_id=1, source_target_pairs={{0,24},{4,28},{8,16},{12,20},{16,8},{20,12},{24,0},{28,4},{1,25},{... | collective-permute-start | bytes 196616 | tf_op jit(solution)/shard_map/ppermute | solution.py:198
  11.9 7.5 %collective-permute-start.6 = (bf16[256,128]{1,0:T(8,128)(2,1)S(1)}, bf16[256,128]{1,0:T(8,128)(2,1)S(1)}, u32[]{:S(2)}, u32[]{:S(2)}) collective-permute-start(bf16[256,128]{1,0:T(8,128)(2,1)S(1)} %get-tuple-element.32), channel_id=1, source_target_pairs={{0,28},{4,24},{8,20},{12,16},{16,12},{20,8},{24,4},{28,0},{1,29},{... | collective-permute-start | bytes 196616 | tf_op jit(solution)/shard_map/ppermute | solution.py:198
  13.0 6.3 %collective-permute-start.7 = (bf16[256,128]{1,0:T(8,128)(2,1)S(1)}, bf16[256,128]{1,0:T(8,128)(2,1)S(1)}, u32[]{:S(2)}, u32[]{:S(2)}) collective-permute-start(bf16[256,128]{1,0:T(8,128)(2,1)S(1)} %get-tuple-element.33), channel_id=1, source_target_pairs={{0,8},{4,12},{8,0},{12,4},{16,24},{20,28},{24,16},{28,20},{1,9},{5... | collective-permute-start | bytes 196616 | tf_op jit(solution)/shard_map/ppermute | solution.py:198
  13.2 6.8 %collective-permute-start.8 = (bf16[256,128]{1,0:T(8,128)(2,1)S(1)}, bf16[256,128]{1,0:T(8,128)(2,1)S(1)}, u32[]{:S(2)}, u32[]{:S(2)}) collective-permute-start(bf16[256,128]{1,0:T(8,128)(2,1)S(1)} %get-tuple-element.34), channel_id=1, source_target_pairs={{0,12},{4,8},{8,4},{12,0},{16,28},{20,24},{24,20},{28,16},{1,13},{... | collective-permute-start | bytes 196616 | tf_op jit(solution)/shard_map/ppermute | solution.py:198
  14.9 5.1 %copy-start.2 = (bf16[3,128,128]{2,1,0:T(8,128)(2,1)S(1)}, bf16[3,128,128]{2,1,0:T(8,128)(2,1)}, u32[]{:S(2)}) copy-start(bf16[3,128,128]{2,1,0:T(8,128)(2,1)} %out_weight_ref.3) | copy-start | bytes 294916
  14.9 5.1 %copy-start.5 = (f32[3,128]{1,0:T(4,128)S(1)}, f32[3,128]{1,0:T(4,128)}, u32[]{:S(2)}) copy-start(f32[3,128]{1,0:T(4,128)} %head_gain_ref.3) | copy-start | bytes 4612
  17.7 9.2 %collective-permute-start.1 = (bf16[2,4,32,128]{3,2,1,0:T(8,128)(2,1)S(1)}, bf16[2,4,32,128]{3,2,1,0:T(8,128)(2,1)S(1)}, u32[]{:S(2)}, u32[]{:S(2)}) collective-permute-start(bf16[2,4,32,128]{3,2,1,0:T(8,128)(2,1)S(1)} %row_state.1), channel_id=1, source_target_pairs={{0,1},{1,0},{2,3},{3,2},{4,5},{5,4},{6,7},{7,6},{8,9},{9,8},{10,11... | collective-permute-start | bytes 196616 | tf_op jit(solution)/shard_map/ppermute | solution.py:254
  22.3 9.4 %collective-permute-start.9 = (bf16[256,128]{1,0:T(8,128)(2,1)S(1)}, bf16[256,128]{1,0:T(8,128)(2,1)S(1)}, u32[]{:S(2)}, u32[]{:S(2)}) collective-permute-start(bf16[256,128]{1,0:T(8,128)(2,1)S(1)} %get-tuple-element.36), channel_id=1, source_target_pairs={{0,4},{4,0},{8,12},{12,8},{16,20},{20,16},{24,28},{28,24},{1,5},{5... | collective-permute-start | bytes 196616 | tf_op jit(solution)/shard_map/ppermute | solution.py:198
  23.9 9.3 %collective-permute-start.10 = (bf16[256,128]{1,0:T(8,128)(2,1)S(1)}, bf16[256,128]{1,0:T(8,128)(2,1)S(1)}, u32[]{:S(2)}, u32[]{:S(2)}) collective-permute-start(bf16[256,128]{1,0:T(8,128)(2,1)S(1)} %get-tuple-element.37), channel_id=1, source_target_pairs={{0,16},{4,20},{8,24},{12,28},{16,0},{20,4},{24,8},{28,12},{1,17},{... | collective-permute-start | bytes 196616 | tf_op jit(solution)/shard_map/ppermute | solution.py:198
  26.9 6.3 %collective-permute-start.2 = (bf16[2,4,32,128]{3,2,1,0:T(8,128)(2,1)S(1)}, bf16[2,4,32,128]{3,2,1,0:T(8,128)(2,1)S(1)}, u32[]{:S(2)}, u32[]{:S(2)}) collective-permute-start(bf16[2,4,32,128]{3,2,1,0:T(8,128)(2,1)S(1)} %add_convert_fusion.1), channel_id=1, source_target_pairs={{0,2},{1,3},{2,0},{3,1},{4,6},{5,7},{6,4},{7,5},{8,10},{9,11},{10,... | collective-permute-start | bytes 196616 | tf_op jit(solution)/shard_map/ppermute | solution.py:254
  28.5 9.7 %collective-permute-start.11 = (bf16[256,128]{1,0:T(8,128)(2,1)S(1)}, bf16[256,128]{1,0:T(8,128)(2,1)S(1)}, u32[]{:S(2)}, u32[]{:S(2)}) collective-permute-start(bf16[256,128]{1,0:T(8,128)(2,1)S(1)} %get-tuple-element.38), channel_id=1, source_target_pairs={{0,20},{4,16},{8,28},{12,24},{16,4},{20,0},{24,12},{28,8},{1,21},{... | collective-permute-start | bytes 196616 | tf_op jit(solution)/shard_map/ppermute | solution.py:198
  28.5 9.7 %collective-permute-start.12 = (bf16[256,128]{1,0:T(8,128)(2,1)S(1)}, bf16[256,128]{1,0:T(8,128)(2,1)S(1)}, u32[]{:S(2)}, u32[]{:S(2)}) collective-permute-start(bf16[256,128]{1,0:T(8,128)(2,1)S(1)} %get-tuple-element.39), channel_id=1, source_target_pairs={{0,24},{4,28},{8,16},{12,20},{16,8},{20,12},{24,0},{28,4},{1,25},{... | collective-permute-start | bytes 196616 | tf_op jit(solution)/shard_map/ppermute | solution.py:198
  31.7 7.7 %collective-permute-start.13 = (bf16[256,128]{1,0:T(8,128)(2,1)S(1)}, bf16[256,128]{1,0:T(8,128)(2,1)S(1)}, u32[]{:S(2)}, u32[]{:S(2)}) collective-permute-start(bf16[256,128]{1,0:T(8,128)(2,1)S(1)} %get-tuple-element.40), channel_id=1, source_target_pairs={{0,28},{4,24},{8,20},{12,16},{16,12},{20,8},{24,4},{28,0},{1,29},{... | collective-permute-start | bytes 196616 | tf_op jit(solution)/shard_map/ppermute | solution.py:198
  33.2 6.2 %collective-permute-start.14 = (bf16[256,128]{1,0:T(8,128)(2,1)S(1)}, bf16[256,128]{1,0:T(8,128)(2,1)S(1)}, u32[]{:S(2)}, u32[]{:S(2)}) collective-permute-start(bf16[256,128]{1,0:T(8,128)(2,1)S(1)} %get-tuple-element.41), channel_id=1, source_target_pairs={{0,8},{4,12},{8,0},{12,4},{16,24},{20,28},{24,16},{28,20},{1,9},{5... | collective-permute-start | bytes 196616 | tf_op jit(solution)/shard_map/ppermute | solution.py:198
  33.2 6.5 %collective-permute-start.15 = (bf16[256,128]{1,0:T(8,128)(2,1)S(1)}, bf16[256,128]{1,0:T(8,128)(2,1)S(1)}, u32[]{:S(2)}, u32[]{:S(2)}) collective-permute-start(bf16[256,128]{1,0:T(8,128)(2,1)S(1)} %get-tuple-element.42), channel_id=1, source_target_pairs={{0,12},{4,8},{8,4},{12,0},{16,28},{20,24},{24,20},{28,16},{1,13},{... | collective-permute-start | bytes 196616 | tf_op jit(solution)/shard_map/ppermute | solution.py:198
  35.3 0.7 %copy-start.6 = (f32[128]{0:T(128)S(1)}, f32[128]{0:T(128)}, u32[]{:S(2)}) copy-start(f32[128]{0:T(128)} %param.13) | copy-start | bytes 1540
  35.9 3.8 %copy-start.3 = (bf16[128,512]{1,0:T(8,128)(2,1)S(1)}, bf16[128,512]{1,0:T(8,128)(2,1)}, u32[]{:S(2)}) copy-start(bf16[128,512]{1,0:T(8,128)(2,1)} %up_ref.1) | copy-start | bytes 393220
  35.9 3.8 %copy-start.4 = (bf16[512,128]{1,0:T(8,128)(2,1)S(1)}, bf16[512,128]{1,0:T(8,128)(2,1)}, u32[]{:S(2)}) copy-start(bf16[512,128]{1,0:T(8,128)(2,1)} %down_ref.1) | copy-start | bytes 393220

commit v3 on v2

--- a/solution.py
+++ b/solution.py
@@ -11,6 +11,7 @@
 GROUP = 4
 EPSILON = 1e-05
 CHUNK = 512
+PIECES_FLOPS = 10**10
 VMEM_LIMIT = 24 * 1024 * 1024
 
 F32 = jnp.float32
@@ -54,60 +55,59 @@
     return hit.astype(F32).astype(BF16)
 
 
-def norm_kernel(x_ref, gain_ref, normed_ref, *sent_refs):
+def piece_kernel(x_ref, *sent_refs):
     row_count, col_count, width = x_ref.shape
     parts = len(sent_refs)
     cols = col_count // parts
     me = lax.axis_index("row")
     order = interleave(row_count, cols)
-    gain = gain_ref[:1]
     for step in range(parts):
         span = pl.ds(pl.multiple_of((me ^ step) * cols, cols), cols)
-        block = x_ref[:, span, :].astype(F32).reshape(row_count * cols, width)
-        normed = normalize(block, gain).astype(BF16)
-        normed_ref[:, span, :] = normed.reshape(row_count, cols, width)
-        sent_refs[step][...] = matmul(order, normed).astype(BF16)
-
-
-def state_kernel(normed_ref, weight_ref, after_ref, state_ref):
-    row_count, col_count, width = normed_ref.shape
+        block = x_ref[:, span, :].reshape(row_count * cols, width)
+        sent_refs[step][...] = matmul(order, block).astype(BF16)
+
+
+def state_kernel(x_ref, gain_ref, weight_ref, after_ref, state_ref, query_ref, gate_ref):
+    row_count, col_count, width = x_ref.shape
     keep = head_mask(width, width)
-    for branch in range(2):
-        key_weight = weight_ref[branch, :, width : 2 * width].T
-        value_weight = weight_ref[branch, :, 2 * width : 3 * width]
-        for row in range(row_count):
-            normed = normed_ref[row]
-            keys = feature(matmul_nt(key_weight, normed)).astype(BF16)
-            values = matmul(normed, value_weight).astype(BF16)
+    gain = gain_ref[...]
+    for row in range(row_count):
+        normed = normalize(x_ref[row].astype(F32), gain).astype(BF16)
+        for branch in range(2):
+            weight = weight_ref[branch]
+            keys = feature(matmul_nt(weight[:, width : 2 * width].T, normed)).astype(BF16)
+            values = matmul(normed, weight[:, 2 * width : 3 * width]).astype(BF16)
             state = jnp.where(keep, matmul(keys, values), 0.0)
             packed = state[:HEAD]
             for head in range(1, width // HEAD):
                 packed = packed + state[head * HEAD : (head + 1) * HEAD]
             state_ref[branch, row] = packed.astype(BF16)
+            query_ref[branch, row] = feature(matmul(normed, weight[:, :width])).astype(BF16)
+            gate_ref[branch, row] = sigmoid(matmul(normed, weight[:, 3 * width :]))
 
 
 def row_kernel(
-    x_ref, normed_ref, state_ref, weight_ref, head_gain_ref, out_weight_ref, gain_ref, updated_ref, gain_out_ref
+    x_ref, query_ref, gate_ref, state_ref, head_gain_ref, out_weight_ref, gain_ref, updated_ref, gain_out_ref
 ):
-    row_count, col_count, width = normed_ref.shape
+    row_count, col_count, width = x_ref.shape
     keep = head_mask(width, width)
     heads = width // HEAD
     gain_out_ref[...] = gain_ref[...]
     for row in range(row_count):
-        normed = normed_ref[row]
         total = x_ref[row].astype(F32)
         for branch in range(2):
             packed = state_ref[branch, row].astype(F32)
             state = jnp.where(keep, jnp.concatenate([packed] * heads, axis=0), 0.0).astype(BF16)
-            query = feature(matmul(normed, weight_ref[branch, :, :width])).astype(BF16)
-            gate = sigmoid(matmul(normed, weight_ref[branch, :, 3 * width :]))
-            head_out = matmul(query, state)
-            mixed = (normalize(head_out, head_gain_ref[branch : branch + 1]) * gate).astype(BF16)
-            total = total + matmul(mixed, out_weight_ref[branch]).astype(BF16).astype(F32)
+            head_out = matmul(query_ref[branch, row], state)
+            mixed = normalize(head_out, head_gain_ref[branch : branch + 1]) * gate_ref[branch, row]
+            out = matmul(mixed.astype(BF16), out_weight_ref[branch])
+            total = total + out.astype(BF16).astype(F32)
         updated_ref[row] = total
 
 
-def column_kernel(row_count, order, weight_ref, head_gain_ref, out_weight_ref, *refs):
+def column_kernel(
+    row_count, order, norm_gain_ref, weight_ref, head_gain_ref, out_weight_ref, *refs
+):
     parts = len(order)
     got_refs = refs[:parts]
     sent_refs = refs[parts + 1 : 2 * parts + 1]
@@ -124,7 +124,7 @@
     key_weight = weight_ref[2, :, width : 2 * width].T
     for start in range(0, total, CHUNK):
         span = slice(start, start + CHUNK)
-        block = block_ref[span]
+        block = normalize(block_ref[span].astype(F32), norm_gain_ref[...]).astype(BF16)
         query_ref[span] = feature(matmul(block, weight_ref[2, :, :width])).astype(BF16)
         value_ref[span] = matmul(block, weight_ref[2, :, 2 * width : 3 * width]).astype(BF16)
         gate_ref[span] = sigmoid(matmul(block, weight_ref[2, :, 3 * width :]))
@@ -185,9 +185,17 @@
         store.wait()
 
 
-def send_order(parts):
-    first = [0, 1, *range(parts // 2, parts), *range(2, parts // 2)]
-    return tuple(dict.fromkeys(first[:parts] if parts < 4 else first))
+def inward_order(parts):
+    half = parts // 2
+    steps = (0, half, half - 1, *range(half + 1, parts), *range(1, half - 1))
+    return tuple(dict.fromkeys(steps))
+
+
+def outward_orders(parts):
+    half = parts // 2
+    early = tuple(dict.fromkeys((0, half, 1)))
+    late = (*range(half + 1, parts), *range(2, half))
+    return (early, late) if late else (early,)
 
 
 def exchange(pieces):
@@ -199,13 +207,13 @@
     return moved
 
 
-def call(kernel, out_shape, name, flops, vmem_limit=VMEM_LIMIT, **kwargs):
+def call(kernel, out_shape, name, flops=0, **kwargs):
     return pl.pallas_call(
         kernel,
         out_shape=out_shape,
         name=name,
-        compiler_params=pltpu.CompilerParams(vmem_limit_bytes=vmem_limit),
-        cost_estimate=pl.CostEstimate(flops=0, bytes_accessed=0, transcendentals=0),
+        compiler_params=pltpu.CompilerParams(vmem_limit_bytes=VMEM_LIMIT),
+        cost_estimate=pl.CostEstimate(flops=flops, bytes_accessed=0, transcendentals=0),
         **kwargs,
     )
 
@@ -228,47 +236,38 @@
     total = row_count * col_count
     hidden = up_weight.shape[1]
     struct = jax.ShapeDtypeStruct
-    square = total * width * width * 2
     vmem = pl.BlockSpec(memory_space=pltpu.VMEM)
     anywhere = pl.BlockSpec(memory_space=pl.ANY)
 
-    normed, *sent = call(
-        norm_kernel,
-        [struct(pair_map.shape, BF16)] + [struct((tokens, width), BF16)] * parts,
-        "norm",
-        square,
-    )(pair_map, jnp.broadcast_to(norm_gain, (8, width)))
+    sent = call(
+        piece_kernel, [struct((tokens, width), BF16)] * parts, "pieces", PIECES_FLOPS
+    )(pair_map)
     got = exchange(sent)
 
-    state = call(
+    gain_row = norm_gain.reshape(1, width)
+    both = (2, *pair_map.shape)
+    state, query, gate = call(
         state_kernel,
-        struct((2, row_count, HEAD, width), BF16),
+        (struct((2, row_count, HEAD, width), BF16), struct(both, BF16), struct(both, F32)),
         "row_state",
-        6 * square,
-        in_specs=[vmem] * 2 + [anywhere],
-    )(normed, in_weights, got[1])
-    state0 = state
+        in_specs=[vmem] * 3 + [anywhere],
+    )(pair_map, gain_row, in_weights, got[parts // 2])
     step = 1
     while step < col_parts:
         pairs = [(at, at ^ step) for at in range(col_parts)]
         state = (state.astype(F32) + lax.ppermute(state, "col", pairs).astype(F32)).astype(BF16)
-        if step == 1:
-            state1 = state
         step *= 2
     updated, gain = call(
         row_kernel,
         (struct(pair_map.shape, F32), struct((1, width), F32)),
         "row_out",
-        8 * square,
-    )(pair_map, normed, state, in_weights, head_gain, out_weights, trans_gain.reshape(1, width))
-
-    order = send_order(parts)
+    )(pair_map, query, gate, state, head_gain, out_weights, trans_gain.reshape(1, width))
+    order = inward_order(parts)
     column_out = call(
         functools.partial(column_kernel, row_count, order),
         [struct((tokens, width), BF16)] * parts,
         "column",
-        10 * square,
-        in_specs=[vmem] * (3 + parts) + [anywhere],
+        in_specs=[vmem] * (4 + parts) + [anywhere],
         scratch_shapes=[
             pltpu.VMEM((total, width), BF16),
             pltpu.VMEM((total, width), BF16),
@@ -277,19 +276,20 @@
             pltpu.VMEM((total, width), F32),
             pltpu.VMEM((total, width), F32),
         ],
-    )(in_weights, head_gain, out_weights, *[got[step] for step in order], normed)
+    )(
+        gain_row, in_weights, head_gain, out_weights, *[got[step] for step in order], gate
+    )
 
     third = exchange(column_out)
 
     result = None
-    for steps in (order,):
+    for steps in outward_orders(parts):
         fresh = result is None
         count = len(steps)
         result = call(
             functools.partial(final_kernel, steps, parts, fresh),
             struct(pair_map.shape, BF16),
             "final",
-            9 * square * count // parts,
             in_specs=[vmem] * (4 + count) + [anywhere] * (not fresh),
             out_specs=anywhere,
             input_output_aliases={} if fresh else {4 + count: 0},

time: 42.4 us -> 40 us (0.943)
  waiting for transfers between devices: 4.99 us -> 3.48 us
  local copies, waits for them, and re-layouts: 2.42 us -> 1.08 us
  Pallas kernels: 9.46 us -> 10.1 us
    ppermute x14, waiting for transfers between devices: 4.98 us -> 3.47 us  [exchange(): moved[step] = lax.ppermute(pieces[step], 'row', pairs)]
    pallas_call x1, Pallas kernels: 2.27 us -> 1.11 us  [shards(): call(row_kernel, (struct(pair_map.shape, F32), struct((1, width), F32)),...]
    pallas_call x1 -> x2, Pallas kernels: 2.57 us -> 3.62 us  [shards(): call(functools.partial(final_kernel, steps, parts, fresh), struct(pair_ma...]
    broadcast_in_dim x1 -> x0, local copies, waits for them, and re-layouts: 0.71 us -> none  [shards(): jnp.broadcast_to(norm_gain, (8, width))]
    unnamed x14 -> x18, local copies, waits for them, and re-layouts: 1.71 us -> 1.08 us
    pallas_call x2, Pallas kernels: 2.21 us -> 2.77 us  [the longest x1 2.34 us: shards(): call(state_kernel, (struct((2, row_count, HEAD, width), BF16), struct(bot...]
  transfers between devices with their start and end apart: 16 -> 16, of which waited for: 6 -> 5; matrix products, arithmetic and copies ran while one was open for 0% -> 0% of each run, Pallas kernels for 15% -> 19%
where the time goes in v3:
time: 40 us; the launch traced here: 39.8 us
  starting transfers between devices  25 us (62%)
  Pallas kernels  10.1 us (25%)
  waiting for transfers between devices  3.48 us (9%)
  local copies, waits for them, and re-layouts  1.08 us (3%)
    ppermute x14, starting transfers between devices, exchange(): moved[step] = lax.ppermute(pieces[step], 'row', pairs)  23.4 us
    pallas_call x2, Pallas kernels, shards(): call(functools.partial(final_kernel, steps, parts, fresh), struct(pair_ma...  3.62 us
    ppermute x14, waiting for transfers between devices, exchange(): moved[step] = lax.ppermute(pieces[step], 'row', pairs)  3.47 us
    pallas_call x1, Pallas kernels, shards(): call(functools.partial(column_kernel, row_count, order), [struct((tokens,...  2.6 us
    pallas_call x1, Pallas kernels, shards(): call(state_kernel, (struct((2, row_count, HEAD, width), BF16), struct(bot...  2.34 us
    ppermute x2, starting transfers between devices, shards(): lax.ppermute(state, 'col', pairs).astype(F32)  1.56 us
    pallas_call x1, Pallas kernels, shards(): call(row_kernel, (struct(pair_map.shape, F32), struct((1, width), F32)),...  1.11 us
    unnamed x18, local copies, waits for them, and re-layouts  1.08 us
  transfers between devices with their start and end apart: 16, of which 5 were waited for; matrix products, arithmetic and copies ran while one was open for 0% of the time, Pallas kernels for 19%

profile of v3, /device:TPU:0, one launch (start us, length us, event | category | flops | bytes accessed | tf_op | source)
XLA Modules:
  0.0 39.8 jit_solution(10866824163101849937)
XLA Ops:
  0.0 0.0 copy-start
  0.0 1.0 %copy-done = bf16[4,512,128]{2,1,0:T(8,128)(2,1)S(1)} copy-done((bf16[4,512,128]{2,1,0:T(8,128)(2,1)S(1)}, bf16[4,512,128]{2,1,0:T(8,128)(2,1)}, u32[]{:S(2)}) %copy-start) | copy-done | bytes 524312
  1.0 0.0 copy-start.2
  1.0 0.0 copy-start.7
  1.0 0.0 copy-start.5
  1.0 0.0 copy-start.6
  1.1 0.4 %pieces.1 = (bf16[256,128]{1,0:T(8,128)(2,1)S(1)}, bf16[256,128]{1,0:T(8,128)(2,1)S(1)}, bf16[256,128]{1,0:T(8,128)(2,1)S(1)}, bf16[256,128]{1,0:T(8,128)(2,1)S(...) custom-call(bf16[4,512,128]{2,1,0:T(8,128)(2,1)S(1)} %copy-done), custom_call_target="tpu_custom_call" | custom-call | flops 10000000000 | tf_op jit(solution)/shard_map/pieces/pallas_call | solution.py:242
  1.5 4.1 %collective-permute-start = (bf16[256,128]{1,0:T(8,128)(2,1)S(1)}, bf16[256,128]{1,0:T(8,128)(2,1)S(1)}, u32[]{:S(2)}, u32[]{:S(2)}) collective-permute-start(bf16[256,128]{1,0:T(8,128)(2,1)S(1)} %get-tuple-element.26), channel_id=1, source_target_pairs={{0,16},{4,20},{8,24},{12,28},{16,0},{20,4},{24,8},{28,12},{1,17},{... | collective-permute-start | bytes 196616 | tf_op jit(solution)/shard_map/ppermute | solution.py:206
  5.6 2.5 %collective-permute-start.3 = (bf16[256,128]{1,0:T(8,128)(2,1)S(1)}, bf16[256,128]{1,0:T(8,128)(2,1)S(1)}, u32[]{:S(2)}, u32[]{:S(2)}) collective-permute-start(bf16[256,128]{1,0:T(8,128)(2,1)S(1)} %get-tuple-element.33), channel_id=1, source_target_pairs={{0,12},{4,8},{8,4},{12,0},{16,28},{20,24},{24,20},{28,16},{1,13},{... | collective-permute-start | bytes 196616 | tf_op jit(solution)/shard_map/ppermute | solution.py:206
  8.1 0.3 collective-permute-start.4
  8.4 2.5 %collective-permute-start.5 = (bf16[256,128]{1,0:T(8,128)(2,1)S(1)}, bf16[256,128]{1,0:T(8,128)(2,1)S(1)}, u32[]{:S(2)}, u32[]{:S(2)}) collective-permute-start(bf16[256,128]{1,0:T(8,128)(2,1)S(1)} %get-tuple-element.35), channel_id=1, source_target_pairs={{0,24},{4,28},{8,16},{12,20},{16,8},{20,12},{24,0},{28,4},{1,25},{... | collective-permute-start | bytes 196616 | tf_op jit(solution)/shard_map/ppermute | solution.py:206
  10.9 2.3 %collective-permute-start.6 = (bf16[256,128]{1,0:T(8,128)(2,1)S(1)}, bf16[256,128]{1,0:T(8,128)(2,1)S(1)}, u32[]{:S(2)}, u32[]{:S(2)}) collective-permute-start(bf16[256,128]{1,0:T(8,128)(2,1)S(1)} %get-tuple-element.36), channel_id=1, source_target_pairs={{0,28},{4,24},{8,20},{12,16},{16,12},{20,8},{24,4},{28,0},{1,29},{... | collective-permute-start | bytes 196616 | tf_op jit(solution)/shard_map/ppermute | solution.py:206
  13.2 0.0 collective-permute-done.after_ref.refs_1_
  13.2 0.5 %collective-permute-start.7 = (bf16[256,128]{1,0:T(8,128)(2,1)S(1)}, bf16[256,128]{1,0:T(8,128)(2,1)S(1)}, u32[]{:S(2)}, u32[]{:S(2)}) collective-permute-start(bf16[256,128]{1,0:T(8,128)(2,1)S(1)} %get-tuple-element.37), channel_id=1, source_target_pairs={{0,4},{4,0},{8,12},{12,8},{16,20},{20,16},{24,28},{28,24},{1,5},{5... | collective-permute-start | bytes 196616 | tf_op jit(solution)/shard_map/ppermute | solution.py:206
  13.7 0.0 collective-permute-done.3.refs_2_
  13.7 0.0 collective-permute-start.8
  13.7 0.0 copy-done.2
  13.7 0.0 copy-done.7
  13.7 0.0 copy-start.1
  13.7 0.0 copy-start.8
  13.7 2.3 %row_state.1 = (bf16[2,4,32,128]{3,2,1,0:T(8,128)(2,1)S(1)}, bf16[2,4,512,128]{3,2,1,0:T(8,128)(2,1)S(1)}, f32[2,4,512,128]{3,2,1,0:T(8,128)S(1)}) custom-call(bf16[4,512,128]{2,1,0:T(8,128)(2,1)S(1)} %copy-done, f32[1,128]{1,0:T(1,128)S(1)} %bitcast.2, bf16[3,128,512]{2,1,0:T(8,128)(2,1)S(1)} %copy-done.2, ...), custom_call_target="tpu_custom_call" | custom-call | tf_op jit(solution)/shard_map/row_state/pallas_call | solution.py:249
  16.1 1.0 %collective-permute-done.4.refs_3_ = bf16[256,128]{1,0:T(8,128)(2,1)S(1)} collective-permute-done((bf16[256,128]{1,0:T(8,128)(2,1)S(1)}, bf16[256,128]{1,0:T(8,128)(2,1)S(1)}, u32[]{:S(2)}, u32[]{:S(2)}) %collective-permute-start.4) | collective-permute-done | bytes 65568 | tf_op jit(solution)/shard_map/ppermute | solution.py:206
  17.1 0.0 collective-permute-start.1
  17.1 0.0 collective-permute-done.5.refs_4_
  17.1 1.0 %collective-permute-done.6.refs_5_ = bf16[256,128]{1,0:T(8,128)(2,1)S(1)} collective-permute-done((bf16[256,128]{1,0:T(8,128)(2,1)S(1)}, bf16[256,128]{1,0:T(8,128)(2,1)S(1)}, u32[]{:S(2)}, u32[]{:S(2)}) %collective-permute-start.6) | collective-permute-done | bytes 65568 | tf_op jit(solution)/shard_map/ppermute | solution.py:206
  18.0 0.3 collective-permute-done.7.refs_6_
  18.3 0.4 collective-permute-done.8.refs_7_
  18.7 0.0 copy-done.5
  18.7 0.0 copy-done.6
  18.7 2.6 %column.1 = (bf16[256,128]{1,0:T(8,128)(2,1)S(1)}, bf16[256,128]{1,0:T(8,128)(2,1)S(1)}, bf16[256,128]{1,0:T(8,128)(2,1)S(1)}, bf16[256,128]{1,0:T(8,128)(2,1)S(...) custom-call(f32[1,128]{1,0:T(1,128)S(1)} %bitcast.3, ...), custom_call_target="tpu_custom_call" | custom-call | tf_op jit(solution)/shard_map/column/pallas_call | solution.py:266
  21.3 2.5 %collective-permute-start.14 = (bf16[256,128]{1,0:T(8,128)(2,1)S(1)}, bf16[256,128]{1,0:T(8,128)(2,1)S(1)}, u32[]{:S(2)}, u32[]{:S(2)}) collective-permute-start(bf16[256,128]{1,0:T(8,128)(2,1)S(1)} %get-tuple-element.45), channel_id=1, source_target_pairs={{0,16},{4,20},{8,24},{12,28},{16,0},{20,4},{24,8},{28,12},{1,17},{... | collective-permute-start | bytes 196616 | tf_op jit(solution)/shard_map/ppermute | solution.py:206
  23.8 0.0 copy-start.3
  23.8 0.0 copy-start.4
  23.8 0.6 %collective-permute-start.15 = (bf16[256,128]{1,0:T(8,128)(2,1)S(1)}, bf16[256,128]{1,0:T(8,128)(2,1)S(1)}, u32[]{:S(2)}, u32[]{:S(2)}) collective-permute-start(bf16[256,128]{1,0:T(8,128)(2,1)S(1)} %get-tuple-element.46), channel_id=1, source_target_pairs={{0,4},{4,0},{8,12},{12,8},{16,20},{20,16},{24,28},{28,24},{1,5},{5... | collective-permute-start | bytes 196616 | tf_op jit(solution)/shard_map/ppermute | solution.py:206
  24.4 0.0 collective-permute-done.1
  24.4 1.6 %collective-permute-start.2 = (bf16[2,4,32,128]{3,2,1,0:T(8,128)(2,1)S(1)}, bf16[2,4,32,128]{3,2,1,0:T(8,128)(2,1)S(1)}, u32[]{:S(2)}, u32[]{:S(2)}) collective-permute-start(bf16[2,4,32,128]{3,2,1,0:T(8,128)(2,1)S(1)} %add_convert_fusion.1), channel_id=1, source_target_pairs={{0,2},{1,3},{2,0},{3,1},{4,6},{5,7},{6,4},{7,5},{8,10},{9,11},{10,... | collective-permute-start | bytes 196616 | tf_op jit(solution)/shard_map/ppermute | solution.py:258
  26.0 1.4 %collective-permute-start.9 = (bf16[256,128]{1,0:T(8,128)(2,1)S(1)}, bf16[256,128]{1,0:T(8,128)(2,1)S(1)}, u32[]{:S(2)}, u32[]{:S(2)}) collective-permute-start(bf16[256,128]{1,0:T(8,128)(2,1)S(1)} %get-tuple-element.39), channel_id=1, source_target_pairs={{0,20},{4,16},{8,28},{12,24},{16,4},{20,0},{24,12},{28,8},{1,21},{... | collective-permute-start | bytes 196616 | tf_op jit(solution)/shard_map/ppermute | solution.py:206
  27.3 2.3 %collective-permute-start.10 = (bf16[256,128]{1,0:T(8,128)(2,1)S(1)}, bf16[256,128]{1,0:T(8,128)(2,1)S(1)}, u32[]{:S(2)}, u32[]{:S(2)}) collective-permute-start(bf16[256,128]{1,0:T(8,128)(2,1)S(1)} %get-tuple-element.40), channel_id=1, source_target_pairs={{0,24},{4,28},{8,16},{12,20},{16,8},{20,12},{24,0},{28,4},{1,25},{... | collective-permute-start | bytes 196616 | tf_op jit(solution)/shard_map/ppermute | solution.py:206
  29.6 0.0 collective-permute-done.14.refs_1_
  29.6 1.9 %collective-permute-start.11 = (bf16[256,128]{1,0:T(8,128)(2,1)S(1)}, bf16[256,128]{1,0:T(8,128)(2,1)S(1)}, u32[]{:S(2)}, u32[]{:S(2)}) collective-permute-start(bf16[256,128]{1,0:T(8,128)(2,1)S(1)} %get-tuple-element.41), channel_id=1, source_target_pairs={{0,28},{4,24},{8,20},{12,16},{16,12},{20,8},{24,4},{28,0},{1,29},{... | collective-permute-start | bytes 196616 | tf_op jit(solution)/shard_map/ppermute | solution.py:206
  31.5 0.0 collective-permute-done.15.refs_2_
  31.5 0.0 collective-permute-start.12
  31.5 0.0 collective-permute-done.2
  31.5 2.5 %collective-permute-start.13 = (bf16[256,128]{1,0:T(8,128)(2,1)S(1)}, bf16[256,128]{1,0:T(8,128)(2,1)S(1)}, u32[]{:S(2)}, u32[]{:S(2)}) collective-permute-start(bf16[256,128]{1,0:T(8,128)(2,1)S(1)} %get-tuple-element.43), channel_id=1, source_target_pairs={{0,12},{4,8},{8,4},{12,0},{16,28},{20,24},{24,20},{28,16},{1,13},{... | collective-permute-start | bytes 196616 | tf_op jit(solution)/shard_map/ppermute | solution.py:206
  34.1 0.0 copy-done.1
  34.1 0.0 copy-done.8
  34.1 1.1 %row_out.1 = (f32[4,512,128]{2,1,0:T(8,128)S(1)}, f32[1,128]{1,0:T(1,128)S(1)}) custom-call(bf16[4,512,128]{2,1,0:T(8,128)(2,1)S(1)} %copy-done.1, bf16[2,4,512,128]{3,2,1,0:T(8,128)(2,1)S(1)} %get-tuple-element.27.query_ref, f32[2,4,512,128]{3,2,1,0:T(8,128)S(1)} %get-tuple-element.28.gate_ref.refs_8_, ...), custom_call_target="tpu_custom_call" | custom-call | tf_op jit(solution)/shard_map/row_out/pallas_call | solution.py:260
  35.2 0.0 copy-done.3
  35.2 0.0 copy-done.4
  35.3 1.6 %final.2.refs_5_ = bf16[4,512,128]{2,1,0:T(8,128)(2,1)} custom-call(f32[4,512,128]{2,1,0:T(8,128)S(1)} %get-tuple-element.30.updated_ref, f32[1,128]{1,0:T(1,128)S(1)} %get-tuple-element.31.gain_ref, bf16[128,512]{1,0:T(8,128)(2,1)S(1)} %copy-done.3, bf16[512,128]{1,0:T(8,128)(2,1)S(1)} %copy-done.4, bf16[256,128]{1,0:T(8,128)(2,1)S(1)} %get-tuple-element.44.refs_0_, ...), custom_call_target="tpu_custom_call" | custom-call | tf_op jit(solution)/shard_map/final/pallas_call | solution.py:289
  36.9 0.0 collective-permute-done.9.refs_0_
  36.9 0.0 collective-permute-done.10.refs_1_
  36.9 0.0 collective-permute-done.11.refs_2_
  36.9 0.0 collective-permute-done.12.refs_3_
  36.9 0.9 %collective-permute-done.13.refs_4_ = bf16[256,128]{1,0:T(8,128)(2,1)S(1)} collective-permute-done((bf16[256,128]{1,0:T(8,128)(2,1)S(1)}, bf16[256,128]{1,0:T(8,128)(2,1)S(1)}, u32[]{:S(2)}, u32[]{:S(2)}) %collective-permute-start.13) | collective-permute-done | bytes 65568 | tf_op jit(solution)/shard_map/ppermute | solution.py:206
  37.8 2.0 %final.3 = bf16[4,512,128]{2,1,0:T(8,128)(2,1)} custom-call(f32[4,512,128]{2,1,0:T(8,128)S(1)} %get-tuple-element.30.updated_ref, f32[1,128]{1,0:T(1,128)S(1)} %get-tuple-element.31.gain_ref, bf16[128,512]{1,0:T(8,128)(2,1)S(1)} %copy-done.3, bf16[512,128]{1,0:T(8,128)(2,1)S(1)} %copy-done.4, ...), custom_call_target="tpu_custom_call", output_to_operand_aliasing={{}: (9, {})} | custom-call | tf_op jit(solution)/shard_map/final/pallas_call | solution.py:289
  (2 shorter events, 0.0 us)
Async XLA Ops:
  0.0 1.0 %copy-start = (bf16[4,512,128]{2,1,0:T(8,128)(2,1)S(1)}, bf16[4,512,128]{2,1,0:T(8,128)(2,1)}, u32[]{:S(2)}) copy-start(bf16[4,512,128]{2,1,0:T(8,128)(2,1)} %x_ref.5) | copy-start | bytes 1572868
  1.0 12.7 %copy-start.2 = (bf16[3,128,512]{2,1,0:T(8,128)(2,1)S(1)}, bf16[3,128,512]{2,1,0:T(8,128)(2,1)}, u32[]{:S(2)}) copy-start(bf16[3,128,512]{2,1,0:T(8,128)(2,1)} %weight_ref.3) | copy-start | bytes 1179652
  1.0 12.7 %copy-start.7 = (f32[128]{0:T(128)S(1)}, f32[128]{0:T(128)}, u32[]{:S(2)}) copy-start(f32[128]{0:T(128)} %param.9) | copy-start | bytes 1540
  1.0 17.6 %copy-start.5 = (bf16[3,128,128]{2,1,0:T(8,128)(2,1)S(1)}, bf16[3,128,128]{2,1,0:T(8,128)(2,1)}, u32[]{:S(2)}) copy-start(bf16[3,128,128]{2,1,0:T(8,128)(2,1)} %out_weight_ref.3) | copy-start | bytes 294916
  1.0 17.6 %copy-start.6 = (f32[3,128]{1,0:T(4,128)S(1)}, f32[3,128]{1,0:T(4,128)}, u32[]{:S(2)}) copy-start(f32[3,128]{1,0:T(4,128)} %head_gain_ref.3) | copy-start | bytes 4612
  1.5 11.7 %collective-permute-start = (bf16[256,128]{1,0:T(8,128)(2,1)S(1)}, bf16[256,128]{1,0:T(8,128)(2,1)S(1)}, u32[]{:S(2)}, u32[]{:S(2)}) collective-permute-start(bf16[256,128]{1,0:T(8,128)(2,1)S(1)} %get-tuple-element.26), channel_id=1, source_target_pairs={{0,16},{4,20},{8,24},{12,28},{16,0},{20,4},{24,8},{28,12},{1,17},{... | collective-permute-start | bytes 196616 | tf_op jit(solution)/shard_map/ppermute | solution.py:206
  5.6 8.1 %collective-permute-start.3 = (bf16[256,128]{1,0:T(8,128)(2,1)S(1)}, bf16[256,128]{1,0:T(8,128)(2,1)S(1)}, u32[]{:S(2)}, u32[]{:S(2)}) collective-permute-start(bf16[256,128]{1,0:T(8,128)(2,1)S(1)} %get-tuple-element.33), channel_id=1, source_target_pairs={{0,12},{4,8},{8,4},{12,0},{16,28},{20,24},{24,20},{28,16},{1,13},{... | collective-permute-start | bytes 196616 | tf_op jit(solution)/shard_map/ppermute | solution.py:206
  8.1 8.9 %collective-permute-start.4 = (bf16[256,128]{1,0:T(8,128)(2,1)S(1)}, bf16[256,128]{1,0:T(8,128)(2,1)S(1)}, u32[]{:S(2)}, u32[]{:S(2)}) collective-permute-start(bf16[256,128]{1,0:T(8,128)(2,1)S(1)} %get-tuple-element.34), channel_id=1, source_target_pairs={{0,20},{4,16},{8,28},{12,24},{16,4},{20,0},{24,12},{28,8},{1,21},{... | collective-permute-start | bytes 196616 | tf_op jit(solution)/shard_map/ppermute | solution.py:206
  8.4 8.7 %collective-permute-start.5 = (bf16[256,128]{1,0:T(8,128)(2,1)S(1)}, bf16[256,128]{1,0:T(8,128)(2,1)S(1)}, u32[]{:S(2)}, u32[]{:S(2)}) collective-permute-start(bf16[256,128]{1,0:T(8,128)(2,1)S(1)} %get-tuple-element.35), channel_id=1, source_target_pairs={{0,24},{4,28},{8,16},{12,20},{16,8},{20,12},{24,0},{28,4},{1,25},{... | collective-permute-start | bytes 196616 | tf_op jit(solution)/shard_map/ppermute | solution.py:206
  10.9 7.1 %collective-permute-start.6 = (bf16[256,128]{1,0:T(8,128)(2,1)S(1)}, bf16[256,128]{1,0:T(8,128)(2,1)S(1)}, u32[]{:S(2)}, u32[]{:S(2)}) collective-permute-start(bf16[256,128]{1,0:T(8,128)(2,1)S(1)} %get-tuple-element.36), channel_id=1, source_target_pairs={{0,28},{4,24},{8,20},{12,16},{16,12},{20,8},{24,4},{28,0},{1,29},{... | collective-permute-start | bytes 196616 | tf_op jit(solution)/shard_map/ppermute | solution.py:206
  13.2 5.1 %collective-permute-start.7 = (bf16[256,128]{1,0:T(8,128)(2,1)S(1)}, bf16[256,128]{1,0:T(8,128)(2,1)S(1)}, u32[]{:S(2)}, u32[]{:S(2)}) collective-permute-start(bf16[256,128]{1,0:T(8,128)(2,1)S(1)} %get-tuple-element.37), channel_id=1, source_target_pairs={{0,4},{4,0},{8,12},{12,8},{16,20},{20,16},{24,28},{28,24},{1,5},{5... | collective-permute-start | bytes 196616 | tf_op jit(solution)/shard_map/ppermute | solution.py:206
  13.7 5.0 %collective-permute-start.8 = (bf16[256,128]{1,0:T(8,128)(2,1)S(1)}, bf16[256,128]{1,0:T(8,128)(2,1)S(1)}, u32[]{:S(2)}, u32[]{:S(2)}) collective-permute-start(bf16[256,128]{1,0:T(8,128)(2,1)S(1)} %get-tuple-element.38), channel_id=1, source_target_pairs={{0,8},{4,12},{8,0},{12,4},{16,24},{20,28},{24,16},{28,20},{1,9},{5... | collective-permute-start | bytes 196616 | tf_op jit(solution)/shard_map/ppermute | solution.py:206
  13.7 20.4 %copy-start.1 = (bf16[4,512,128]{2,1,0:T(8,128)(2,1)S(1)}, bf16[4,512,128]{2,1,0:T(8,128)(2,1)}, u32[]{:S(2)}) copy-start(bf16[4,512,128]{2,1,0:T(8,128)(2,1)} %x_ref.5) | copy-start | bytes 1572868
  13.7 20.4 %copy-start.8 = (f32[128]{0:T(128)S(1)}, f32[128]{0:T(128)}, u32[]{:S(2)}) copy-start(f32[128]{0:T(128)} %param.13) | copy-start | bytes 1540
  17.1 7.3 %collective-permute-start.1 = (bf16[2,4,32,128]{3,2,1,0:T(8,128)(2,1)S(1)}, bf16[2,4,32,128]{3,2,1,0:T(8,128)(2,1)S(1)}, u32[]{:S(2)}, u32[]{:S(2)}) collective-permute-start(bf16[2,4,32,128]{3,2,1,0:T(8,128)(2,1)S(1)} %get-tuple-element.29), channel_id=1, source_target_pairs={{0,1},{1,0},{2,3},{3,2},{4,5},{5,4},{6,7},{7,6},{8,9},{9,8},{10,11... | collective-permute-start | bytes 196616 | tf_op jit(solution)/shard_map/ppermute | solution.py:258
  21.3 8.4 %collective-permute-start.14 = (bf16[256,128]{1,0:T(8,128)(2,1)S(1)}, bf16[256,128]{1,0:T(8,128)(2,1)S(1)}, u32[]{:S(2)}, u32[]{:S(2)}) collective-permute-start(bf16[256,128]{1,0:T(8,128)(2,1)S(1)} %get-tuple-element.45), channel_id=1, source_target_pairs={{0,16},{4,20},{8,24},{12,28},{16,0},{20,4},{24,8},{28,12},{1,17},{... | collective-permute-start | bytes 196616 | tf_op jit(solution)/shard_map/ppermute | solution.py:206
  23.8 11.4 %copy-start.3 = (bf16[128,512]{1,0:T(8,128)(2,1)S(1)}, bf16[128,512]{1,0:T(8,128)(2,1)}, u32[]{:S(2)}) copy-start(bf16[128,512]{1,0:T(8,128)(2,1)} %up_ref.3) | copy-start | bytes 393220
  23.8 11.4 %copy-start.4 = (bf16[512,128]{1,0:T(8,128)(2,1)S(1)}, bf16[512,128]{1,0:T(8,128)(2,1)}, u32[]{:S(2)}) copy-start(bf16[512,128]{1,0:T(8,128)(2,1)} %down_ref.3) | copy-start | bytes 393220
  23.8 7.7 %collective-permute-start.15 = (bf16[256,128]{1,0:T(8,128)(2,1)S(1)}, bf16[256,128]{1,0:T(8,128)(2,1)S(1)}, u32[]{:S(2)}, u32[]{:S(2)}) collective-permute-start(bf16[256,128]{1,0:T(8,128)(2,1)S(1)} %get-tuple-element.46), channel_id=1, source_target_pairs={{0,4},{4,0},{8,12},{12,8},{16,20},{20,16},{24,28},{28,24},{1,5},{5... | collective-permute-start | bytes 196616 | tf_op jit(solution)/shard_map/ppermute | solution.py:206
  24.4 7.1 %collective-permute-start.2 = (bf16[2,4,32,128]{3,2,1,0:T(8,128)(2,1)S(1)}, bf16[2,4,32,128]{3,2,1,0:T(8,128)(2,1)S(1)}, u32[]{:S(2)}, u32[]{:S(2)}) collective-permute-start(bf16[2,4,32,128]{3,2,1,0:T(8,128)(2,1)S(1)} %add_convert_fusion.1), channel_id=1, source_target_pairs={{0,2},{1,3},{2,0},{3,1},{4,6},{5,7},{6,4},{7,5},{8,10},{9,11},{10,... | collective-permute-start | bytes 196616 | tf_op jit(solution)/shard_map/ppermute | solution.py:258
  26.0 10.9 %collective-permute-start.9 = (bf16[256,128]{1,0:T(8,128)(2,1)S(1)}, bf16[256,128]{1,0:T(8,128)(2,1)S(1)}, u32[]{:S(2)}, u32[]{:S(2)}) collective-permute-start(bf16[256,128]{1,0:T(8,128)(2,1)S(1)} %get-tuple-element.39), channel_id=1, source_target_pairs={{0,20},{4,16},{8,28},{12,24},{16,4},{20,0},{24,12},{28,8},{1,21},{... | collective-permute-start | bytes 196616 | tf_op jit(solution)/shard_map/ppermute | solution.py:206
  27.3 9.6 %collective-permute-start.10 = (bf16[256,128]{1,0:T(8,128)(2,1)S(1)}, bf16[256,128]{1,0:T(8,128)(2,1)S(1)}, u32[]{:S(2)}, u32[]{:S(2)}) collective-permute-start(bf16[256,128]{1,0:T(8,128)(2,1)S(1)} %get-tuple-element.40), channel_id=1, source_target_pairs={{0,24},{4,28},{8,16},{12,20},{16,8},{20,12},{24,0},{28,4},{1,25},{... | collective-permute-start | bytes 196616 | tf_op jit(solution)/shard_map/ppermute | solution.py:206
  29.6 7.3 %collective-permute-start.11 = (bf16[256,128]{1,0:T(8,128)(2,1)S(1)}, bf16[256,128]{1,0:T(8,128)(2,1)S(1)}, u32[]{:S(2)}, u32[]{:S(2)}) collective-permute-start(bf16[256,128]{1,0:T(8,128)(2,1)S(1)} %get-tuple-element.41), channel_id=1, source_target_pairs={{0,28},{4,24},{8,20},{12,16},{16,12},{20,8},{24,4},{28,0},{1,29},{... | collective-permute-start | bytes 196616 | tf_op jit(solution)/shard_map/ppermute | solution.py:206
  31.5 5.4 %collective-permute-start.12 = (bf16[256,128]{1,0:T(8,128)(2,1)S(1)}, bf16[256,128]{1,0:T(8,128)(2,1)S(1)}, u32[]{:S(2)}, u32[]{:S(2)}) collective-permute-start(bf16[256,128]{1,0:T(8,128)(2,1)S(1)} %get-tuple-element.42), channel_id=1, source_target_pairs={{0,8},{4,12},{8,0},{12,4},{16,24},{20,28},{24,16},{28,20},{1,9},{5... | collective-permute-start | bytes 196616 | tf_op jit(solution)/shard_map/ppermute | solution.py:206
  31.5 6.3 %collective-permute-start.13 = (bf16[256,128]{1,0:T(8,128)(2,1)S(1)}, bf16[256,128]{1,0:T(8,128)(2,1)S(1)}, u32[]{:S(2)}, u32[]{:S(2)}) collective-permute-start(bf16[256,128]{1,0:T(8,128)(2,1)S(1)} %get-tuple-element.43), channel_id=1, source_target_pairs={{0,12},{4,8},{8,4},{12,0},{16,28},{20,24},{24,20},{28,16},{1,13},{... | collective-permute-start | bytes 196616 | tf_op jit(solution)/shard_map/ppermute | solution.py:206

commit v4 on v3

--- a/solution.py
+++ b/solution.py
@@ -193,8 +193,8 @@
 
 def outward_orders(parts):
     half = parts // 2
-    early = tuple(dict.fromkeys((0, half, 1)))
-    late = (*range(half + 1, parts), *range(2, half))
+    early = tuple(dict.fromkeys((0, half, half - 1)))
+    late = (*range(half + 1, parts), *range(half - 2, 0, -1))
     return (early, late) if late else (early,)
 
 
@@ -252,11 +252,11 @@
         "row_state",
         in_specs=[vmem] * 3 + [anywhere],
     )(pair_map, gain_row, in_weights, got[parts // 2])
-    step = 1
-    while step < col_parts:
+    step = col_parts // 2
+    while step > 0:
         pairs = [(at, at ^ step) for at in range(col_parts)]
         state = (state.astype(F32) + lax.ppermute(state, "col", pairs).astype(F32)).astype(BF16)
-        step *= 2
+        step //= 2
     updated, gain = call(
         row_kernel,
         (struct(pair_map.shape, F32), struct((1, width), F32)),

time: 40 us -> 39 us (0.975)
  waiting for transfers between devices: 3.48 us -> 2.32 us
    ppermute x14, waiting for transfers between devices: 3.47 us -> 2.32 us  [exchange(): moved[step] = lax.ppermute(pieces[step], 'row', pairs)]
  transfers between devices with their start and end apart: 16 -> 16, of which waited for: 5 -> 4; matrix products, arithmetic and copies ran while one was open for 0% -> 0% of each run, Pallas kernels for 19% -> 20%
where the time goes in v4:
time: 39 us; the launch traced here: 38.8 us
  starting transfers between devices  25.1 us (64%)
  Pallas kernels  10.1 us (26%)
  waiting for transfers between devices  2.32 us (6%)
  local copies, waits for them, and re-layouts  1.08 us (3%)
    ppermute x14, starting transfers between devices, exchange(): moved[step] = lax.ppermute(pieces[step], 'row', pairs)  23.5 us
    pallas_call x2, Pallas kernels, shards(): call(functools.partial(final_kernel, steps, parts, fresh), struct(pair_ma...  3.63 us
    pallas_call x1, Pallas kernels, shards(): call(functools.partial(column_kernel, row_count, order), [struct((tokens,...  2.6 us
    pallas_call x1, Pallas kernels, shards(): call(state_kernel, (struct((2, row_count, HEAD, width), BF16), struct(bot...  2.34 us
    ppermute x14, waiting for transfers between devices, exchange(): moved[step] = lax.ppermute(pieces[step], 'row', pairs)  2.32 us
    ppermute x2, starting transfers between devices, shards(): lax.ppermute(state, 'col', pairs).astype(F32)  1.56 us
    pallas_call x1, Pallas kernels, shards(): call(row_kernel, (struct(pair_map.shape, F32), struct((1, width), F32)),...  1.11 us
    unnamed x18, local copies, waits for them, and re-layouts  1.08 us
  transfers between devices with their start and end apart: 16, of which 4 were waited for; matrix products, arithmetic and copies ran while one was open for 0% of the time, Pallas kernels for 20%

profile of v4, /device:TPU:0, one launch (start us, length us, event | category | flops | bytes accessed | tf_op | source)
XLA Modules:
  0.0 38.8 jit_solution(15194780109079958038)
XLA Ops:
  0.0 0.0 copy-start
  0.0 1.0 %copy-done = bf16[4,512,128]{2,1,0:T(8,128)(2,1)S(1)} copy-done((bf16[4,512,128]{2,1,0:T(8,128)(2,1)S(1)}, bf16[4,512,128]{2,1,0:T(8,128)(2,1)}, u32[]{:S(2)}) %copy-start) | copy-done | bytes 524312
  1.0 0.0 copy-start.2
  1.0 0.0 copy-start.7
  1.0 0.0 copy-start.5
  1.0 0.0 copy-start.6
  1.1 0.4 %pieces.1 = (bf16[256,128]{1,0:T(8,128)(2,1)S(1)}, bf16[256,128]{1,0:T(8,128)(2,1)S(1)}, bf16[256,128]{1,0:T(8,128)(2,1)S(1)}, bf16[256,128]{1,0:T(8,128)(2,1)S(...) custom-call(bf16[4,512,128]{2,1,0:T(8,128)(2,1)S(1)} %copy-done), custom_call_target="tpu_custom_call" | custom-call | flops 10000000000 | tf_op jit(solution)/shard_map/pieces/pallas_call | solution.py:242
  1.5 4.1 %collective-permute-start = (bf16[256,128]{1,0:T(8,128)(2,1)S(1)}, bf16[256,128]{1,0:T(8,128)(2,1)S(1)}, u32[]{:S(2)}, u32[]{:S(2)}) collective-permute-start(bf16[256,128]{1,0:T(8,128)(2,1)S(1)} %get-tuple-element.26), channel_id=1, source_target_pairs={{0,16},{4,20},{8,24},{12,28},{16,0},{20,4},{24,8},{28,12},{1,17},{... | collective-permute-start | bytes 196616 | tf_op jit(solution)/shard_map/ppermute | solution.py:206
  5.6 2.5 %collective-permute-start.3 = (bf16[256,128]{1,0:T(8,128)(2,1)S(1)}, bf16[256,128]{1,0:T(8,128)(2,1)S(1)}, u32[]{:S(2)}, u32[]{:S(2)}) collective-permute-start(bf16[256,128]{1,0:T(8,128)(2,1)S(1)} %get-tuple-element.33), channel_id=1, source_target_pairs={{0,12},{4,8},{8,4},{12,0},{16,28},{20,24},{24,20},{28,16},{1,13},{... | collective-permute-start | bytes 196616 | tf_op jit(solution)/shard_map/ppermute | solution.py:206
  8.1 0.3 collective-permute-start.4
  8.4 2.5 %collective-permute-start.5 = (bf16[256,128]{1,0:T(8,128)(2,1)S(1)}, bf16[256,128]{1,0:T(8,128)(2,1)S(1)}, u32[]{:S(2)}, u32[]{:S(2)}) collective-permute-start(bf16[256,128]{1,0:T(8,128)(2,1)S(1)} %get-tuple-element.35), channel_id=1, source_target_pairs={{0,24},{4,28},{8,16},{12,20},{16,8},{20,12},{24,0},{28,4},{1,25},{... | collective-permute-start | bytes 196616 | tf_op jit(solution)/shard_map/ppermute | solution.py:206
  10.9 2.3 %collective-permute-start.6 = (bf16[256,128]{1,0:T(8,128)(2,1)S(1)}, bf16[256,128]{1,0:T(8,128)(2,1)S(1)}, u32[]{:S(2)}, u32[]{:S(2)}) collective-permute-start(bf16[256,128]{1,0:T(8,128)(2,1)S(1)} %get-tuple-element.36), channel_id=1, source_target_pairs={{0,28},{4,24},{8,20},{12,16},{16,12},{20,8},{24,4},{28,0},{1,29},{... | collective-permute-start | bytes 196616 | tf_op jit(solution)/shard_map/ppermute | solution.py:206
  13.2 0.0 collective-permute-done.after_ref.refs_1_
  13.2 0.5 %collective-permute-start.7 = (bf16[256,128]{1,0:T(8,128)(2,1)S(1)}, bf16[256,128]{1,0:T(8,128)(2,1)S(1)}, u32[]{:S(2)}, u32[]{:S(2)}) collective-permute-start(bf16[256,128]{1,0:T(8,128)(2,1)S(1)} %get-tuple-element.37), channel_id=1, source_target_pairs={{0,4},{4,0},{8,12},{12,8},{16,20},{20,16},{24,28},{28,24},{1,5},{5... | collective-permute-start | bytes 196616 | tf_op jit(solution)/shard_map/ppermute | solution.py:206
  13.7 0.0 collective-permute-done.3.refs_2_
  13.7 0.0 collective-permute-start.8
  13.7 0.0 copy-done.2
  13.7 0.0 copy-done.7
  13.7 0.0 copy-start.1
  13.7 0.0 copy-start.8
  13.7 2.3 %row_state.1 = (bf16[2,4,32,128]{3,2,1,0:T(8,128)(2,1)S(1)}, bf16[2,4,512,128]{3,2,1,0:T(8,128)(2,1)S(1)}, f32[2,4,512,128]{3,2,1,0:T(8,128)S(1)}) custom-call(bf16[4,512,128]{2,1,0:T(8,128)(2,1)S(1)} %copy-done, f32[1,128]{1,0:T(1,128)S(1)} %bitcast.2, bf16[3,128,512]{2,1,0:T(8,128)(2,1)S(1)} %copy-done.2, ...), custom_call_target="tpu_custom_call" | custom-call | tf_op jit(solution)/shard_map/row_state/pallas_call | solution.py:249
  16.1 1.0 %collective-permute-done.4.refs_3_ = bf16[256,128]{1,0:T(8,128)(2,1)S(1)} collective-permute-done((bf16[256,128]{1,0:T(8,128)(2,1)S(1)}, bf16[256,128]{1,0:T(8,128)(2,1)S(1)}, u32[]{:S(2)}, u32[]{:S(2)}) %collective-permute-start.4) | collective-permute-done | bytes 65568 | tf_op jit(solution)/shard_map/ppermute | solution.py:206
  17.1 1.5 %collective-permute-start.1 = (bf16[2,4,32,128]{3,2,1,0:T(8,128)(2,1)S(1)}, bf16[2,4,32,128]{3,2,1,0:T(8,128)(2,1)S(1)}, u32[]{:S(2)}, u32[]{:S(2)}) collective-permute-start(bf16[2,4,32,128]{3,2,1,0:T(8,128)(2,1)S(1)} %get-tuple-element.29), channel_id=1, source_target_pairs={{0,2},{1,3},{2,0},{3,1},{4,6},{5,7},{6,4},{7,5},{8,10},{9,11},{10,... | collective-permute-start | bytes 196616 | tf_op jit(solution)/shard_map/ppermute | solution.py:258
  18.5 0.0 collective-permute-done.5.refs_4_
  18.5 0.0 collective-permute-done.6.refs_5_
  18.6 0.0 collective-permute-done.7.refs_6_
  18.6 0.1 collective-permute-done.8.refs_7_
  18.7 0.0 copy-done.5
  18.7 0.0 copy-done.6
  18.7 2.6 %column.1 = (bf16[256,128]{1,0:T(8,128)(2,1)S(1)}, bf16[256,128]{1,0:T(8,128)(2,1)S(1)}, bf16[256,128]{1,0:T(8,128)(2,1)S(1)}, bf16[256,128]{1,0:T(8,128)(2,1)S(...) custom-call(f32[1,128]{1,0:T(1,128)S(1)} %bitcast.3, ...), custom_call_target="tpu_custom_call" | custom-call | tf_op jit(solution)/shard_map/column/pallas_call | solution.py:266
  21.3 2.7 %collective-permute-start.14 = (bf16[256,128]{1,0:T(8,128)(2,1)S(1)}, bf16[256,128]{1,0:T(8,128)(2,1)S(1)}, u32[]{:S(2)}, u32[]{:S(2)}) collective-permute-start(bf16[256,128]{1,0:T(8,128)(2,1)S(1)} %get-tuple-element.45), channel_id=1, source_target_pairs={{0,16},{4,20},{8,24},{12,28},{16,0},{20,4},{24,8},{28,12},{1,17},{... | collective-permute-start | bytes 196616 | tf_op jit(solution)/shard_map/ppermute | solution.py:206
  23.9 0.0 copy-start.3
  23.9 0.0 copy-start.4
  23.9 0.7 %collective-permute-start.15 = (bf16[256,128]{1,0:T(8,128)(2,1)S(1)}, bf16[256,128]{1,0:T(8,128)(2,1)S(1)}, u32[]{:S(2)}, u32[]{:S(2)}) collective-permute-start(bf16[256,128]{1,0:T(8,128)(2,1)S(1)} %get-tuple-element.46), channel_id=1, source_target_pairs={{0,12},{4,8},{8,4},{12,0},{16,28},{20,24},{24,20},{28,16},{1,13},{... | collective-permute-start | bytes 196616 | tf_op jit(solution)/shard_map/ppermute | solution.py:206
  24.6 0.0 collective-permute-done.1
  24.7 0.1 collective-permute-start.2
  24.8 2.6 %collective-permute-start.9 = (bf16[256,128]{1,0:T(8,128)(2,1)S(1)}, bf16[256,128]{1,0:T(8,128)(2,1)S(1)}, u32[]{:S(2)}, u32[]{:S(2)}) collective-permute-start(bf16[256,128]{1,0:T(8,128)(2,1)S(1)} %get-tuple-element.39), channel_id=1, source_target_pairs={{0,20},{4,16},{8,28},{12,24},{16,4},{20,0},{24,12},{28,8},{1,21},{... | collective-permute-start | bytes 196616 | tf_op jit(solution)/shard_map/ppermute | solution.py:206
  27.4 2.0 %collective-permute-start.10 = (bf16[256,128]{1,0:T(8,128)(2,1)S(1)}, bf16[256,128]{1,0:T(8,128)(2,1)S(1)}, u32[]{:S(2)}, u32[]{:S(2)}) collective-permute-start(bf16[256,128]{1,0:T(8,128)(2,1)S(1)} %get-tuple-element.40), channel_id=1, source_target_pairs={{0,24},{4,28},{8,16},{12,20},{16,8},{20,12},{24,0},{28,4},{1,25},{... | collective-permute-start | bytes 196616 | tf_op jit(solution)/shard_map/ppermute | solution.py:206
  29.4 0.0 collective-permute-done.14.refs_1_
  29.4 1.8 %collective-permute-start.11 = (bf16[256,128]{1,0:T(8,128)(2,1)S(1)}, bf16[256,128]{1,0:T(8,128)(2,1)S(1)}, u32[]{:S(2)}, u32[]{:S(2)}) collective-permute-start(bf16[256,128]{1,0:T(8,128)(2,1)S(1)} %get-tuple-element.41), channel_id=1, source_target_pairs={{0,28},{4,24},{8,20},{12,16},{16,12},{20,8},{24,4},{28,0},{1,29},{... | collective-permute-start | bytes 196616 | tf_op jit(solution)/shard_map/ppermute | solution.py:206
  31.2 0.0 collective-permute-done.15.refs_2_
  31.2 0.0 collective-permute-start.12
  31.2 0.0 collective-permute-done.2
  31.2 1.6 %collective-permute-start.13 = (bf16[256,128]{1,0:T(8,128)(2,1)S(1)}, bf16[256,128]{1,0:T(8,128)(2,1)S(1)}, u32[]{:S(2)}, u32[]{:S(2)}) collective-permute-start(bf16[256,128]{1,0:T(8,128)(2,1)S(1)} %get-tuple-element.43), channel_id=1, source_target_pairs={{0,4},{4,0},{8,12},{12,8},{16,20},{20,16},{24,28},{28,24},{1,5},{5... | collective-permute-start | bytes 196616 | tf_op jit(solution)/shard_map/ppermute | solution.py:206
  32.8 0.0 copy-done.1
  32.8 0.0 copy-done.8
  32.8 1.1 %row_out.1 = (f32[4,512,128]{2,1,0:T(8,128)S(1)}, f32[1,128]{1,0:T(1,128)S(1)}) custom-call(bf16[4,512,128]{2,1,0:T(8,128)(2,1)S(1)} %copy-done.1, bf16[2,4,512,128]{3,2,1,0:T(8,128)(2,1)S(1)} %get-tuple-element.27.query_ref, f32[2,4,512,128]{3,2,1,0:T(8,128)S(1)} %get-tuple-element.28.gate_ref.refs_8_, ...), custom_call_target="tpu_custom_call" | custom-call | tf_op jit(solution)/shard_map/row_out/pallas_call | solution.py:260
  33.9 0.0 copy-done.3
  33.9 0.0 copy-done.4
  33.9 1.6 %final.2.refs_5_ = bf16[4,512,128]{2,1,0:T(8,128)(2,1)} custom-call(f32[4,512,128]{2,1,0:T(8,128)S(1)} %get-tuple-element.30.updated_ref, f32[1,128]{1,0:T(1,128)S(1)} %get-tuple-element.31.gain_ref, bf16[128,512]{1,0:T(8,128)(2,1)S(1)} %copy-done.3, bf16[512,128]{1,0:T(8,128)(2,1)S(1)} %copy-done.4, bf16[256,128]{1,0:T(8,128)(2,1)S(1)} %get-tuple-element.44.refs_0_, ...), custom_call_target="tpu_custom_call" | custom-call | tf_op jit(solution)/shard_map/final/pallas_call | solution.py:289
  35.5 0.0 collective-permute-done.9.refs_0_
  35.5 0.0 collective-permute-done.10.refs_1_
  35.6 1.2 %collective-permute-done.11.refs_2_ = bf16[256,128]{1,0:T(8,128)(2,1)S(1)} collective-permute-done((bf16[256,128]{1,0:T(8,128)(2,1)S(1)}, bf16[256,128]{1,0:T(8,128)(2,1)S(1)}, u32[]{:S(2)}, u32[]{:S(2)}) %collective-permute-start.11) | collective-permute-done | bytes 65568 | tf_op jit(solution)/shard_map/ppermute | solution.py:206
  36.7 0.0 collective-permute-done.12.refs_3_
  36.7 0.1 collective-permute-done.13.refs_4_
  36.8 2.0 %final.3 = bf16[4,512,128]{2,1,0:T(8,128)(2,1)} custom-call(f32[4,512,128]{2,1,0:T(8,128)S(1)} %get-tuple-element.30.updated_ref, f32[1,128]{1,0:T(1,128)S(1)} %get-tuple-element.31.gain_ref, bf16[128,512]{1,0:T(8,128)(2,1)S(1)} %copy-done.3, bf16[512,128]{1,0:T(8,128)(2,1)S(1)} %copy-done.4, ...), custom_call_target="tpu_custom_call", output_to_operand_aliasing={{}: (9, {})} | custom-call | tf_op jit(solution)/shard_map/final/pallas_call | solution.py:289
  (2 shorter events, 0.0 us)
Async XLA Ops:
  0.0 1.0 %copy-start = (bf16[4,512,128]{2,1,0:T(8,128)(2,1)S(1)}, bf16[4,512,128]{2,1,0:T(8,128)(2,1)}, u32[]{:S(2)}) copy-start(bf16[4,512,128]{2,1,0:T(8,128)(2,1)} %x_ref.5) | copy-start | bytes 1572868
  1.0 12.7 %copy-start.2 = (bf16[3,128,512]{2,1,0:T(8,128)(2,1)S(1)}, bf16[3,128,512]{2,1,0:T(8,128)(2,1)}, u32[]{:S(2)}) copy-start(bf16[3,128,512]{2,1,0:T(8,128)(2,1)} %weight_ref.3) | copy-start | bytes 1179652
  1.0 12.7 %copy-start.7 = (f32[128]{0:T(128)S(1)}, f32[128]{0:T(128)}, u32[]{:S(2)}) copy-start(f32[128]{0:T(128)} %param.9) | copy-start | bytes 1540
  1.0 17.6 %copy-start.5 = (bf16[3,128,128]{2,1,0:T(8,128)(2,1)S(1)}, bf16[3,128,128]{2,1,0:T(8,128)(2,1)}, u32[]{:S(2)}) copy-start(bf16[3,128,128]{2,1,0:T(8,128)(2,1)} %out_weight_ref.3) | copy-start | bytes 294916
  1.0 17.6 %copy-start.6 = (f32[3,128]{1,0:T(4,128)S(1)}, f32[3,128]{1,0:T(4,128)}, u32[]{:S(2)}) copy-start(f32[3,128]{1,0:T(4,128)} %head_gain_ref.3) | copy-start | bytes 4612
  1.5 11.7 %collective-permute-start = (bf16[256,128]{1,0:T(8,128)(2,1)S(1)}, bf16[256,128]{1,0:T(8,128)(2,1)S(1)}, u32[]{:S(2)}, u32[]{:S(2)}) collective-permute-start(bf16[256,128]{1,0:T(8,128)(2,1)S(1)} %get-tuple-element.26), channel_id=1, source_target_pairs={{0,16},{4,20},{8,24},{12,28},{16,0},{20,4},{24,8},{28,12},{1,17},{... | collective-permute-start | bytes 196616 | tf_op jit(solution)/shard_map/ppermute | solution.py:206
  5.6 8.1 %collective-permute-start.3 = (bf16[256,128]{1,0:T(8,128)(2,1)S(1)}, bf16[256,128]{1,0:T(8,128)(2,1)S(1)}, u32[]{:S(2)}, u32[]{:S(2)}) collective-permute-start(bf16[256,128]{1,0:T(8,128)(2,1)S(1)} %get-tuple-element.33), channel_id=1, source_target_pairs={{0,12},{4,8},{8,4},{12,0},{16,28},{20,24},{24,20},{28,16},{1,13},{... | collective-permute-start | bytes 196616 | tf_op jit(solution)/shard_map/ppermute | solution.py:206
  8.1 8.9 %collective-permute-start.4 = (bf16[256,128]{1,0:T(8,128)(2,1)S(1)}, bf16[256,128]{1,0:T(8,128)(2,1)S(1)}, u32[]{:S(2)}, u32[]{:S(2)}) collective-permute-start(bf16[256,128]{1,0:T(8,128)(2,1)S(1)} %get-tuple-element.34), channel_id=1, source_target_pairs={{0,20},{4,16},{8,28},{12,24},{16,4},{20,0},{24,12},{28,8},{1,21},{... | collective-permute-start | bytes 196616 | tf_op jit(solution)/shard_map/ppermute | solution.py:206
  8.4 10.1 %collective-permute-start.5 = (bf16[256,128]{1,0:T(8,128)(2,1)S(1)}, bf16[256,128]{1,0:T(8,128)(2,1)S(1)}, u32[]{:S(2)}, u32[]{:S(2)}) collective-permute-start(bf16[256,128]{1,0:T(8,128)(2,1)S(1)} %get-tuple-element.35), channel_id=1, source_target_pairs={{0,24},{4,28},{8,16},{12,20},{16,8},{20,12},{24,0},{28,4},{1,25},{... | collective-permute-start | bytes 196616 | tf_op jit(solution)/shard_map/ppermute | solution.py:206
  10.9 7.7 %collective-permute-start.6 = (bf16[256,128]{1,0:T(8,128)(2,1)S(1)}, bf16[256,128]{1,0:T(8,128)(2,1)S(1)}, u32[]{:S(2)}, u32[]{:S(2)}) collective-permute-start(bf16[256,128]{1,0:T(8,128)(2,1)S(1)} %get-tuple-element.36), channel_id=1, source_target_pairs={{0,28},{4,24},{8,20},{12,16},{16,12},{20,8},{24,4},{28,0},{1,29},{... | collective-permute-start | bytes 196616 | tf_op jit(solution)/shard_map/ppermute | solution.py:206
  13.2 5.4 %collective-permute-start.7 = (bf16[256,128]{1,0:T(8,128)(2,1)S(1)}, bf16[256,128]{1,0:T(8,128)(2,1)S(1)}, u32[]{:S(2)}, u32[]{:S(2)}) collective-permute-start(bf16[256,128]{1,0:T(8,128)(2,1)S(1)} %get-tuple-element.37), channel_id=1, source_target_pairs={{0,4},{4,0},{8,12},{12,8},{16,20},{20,16},{24,28},{28,24},{1,5},{5... | collective-permute-start | bytes 196616 | tf_op jit(solution)/shard_map/ppermute | solution.py:206
  13.7 5.0 %collective-permute-start.8 = (bf16[256,128]{1,0:T(8,128)(2,1)S(1)}, bf16[256,128]{1,0:T(8,128)(2,1)S(1)}, u32[]{:S(2)}, u32[]{:S(2)}) collective-permute-start(bf16[256,128]{1,0:T(8,128)(2,1)S(1)} %get-tuple-element.38), channel_id=1, source_target_pairs={{0,8},{4,12},{8,0},{12,4},{16,24},{20,28},{24,16},{28,20},{1,9},{5... | collective-permute-start | bytes 196616 | tf_op jit(solution)/shard_map/ppermute | solution.py:206
  13.7 19.0 %copy-start.1 = (bf16[4,512,128]{2,1,0:T(8,128)(2,1)S(1)}, bf16[4,512,128]{2,1,0:T(8,128)(2,1)}, u32[]{:S(2)}) copy-start(bf16[4,512,128]{2,1,0:T(8,128)(2,1)} %x_ref.5) | copy-start | bytes 1572868
  13.7 19.0 %copy-start.8 = (f32[128]{0:T(128)S(1)}, f32[128]{0:T(128)}, u32[]{:S(2)}) copy-start(f32[128]{0:T(128)} %param.13) | copy-start | bytes 1540
  17.1 7.6 %collective-permute-start.1 = (bf16[2,4,32,128]{3,2,1,0:T(8,128)(2,1)S(1)}, bf16[2,4,32,128]{3,2,1,0:T(8,128)(2,1)S(1)}, u32[]{:S(2)}, u32[]{:S(2)}) collective-permute-start(bf16[2,4,32,128]{3,2,1,0:T(8,128)(2,1)S(1)} %get-tuple-element.29), channel_id=1, source_target_pairs={{0,2},{1,3},{2,0},{3,1},{4,6},{5,7},{6,4},{7,5},{8,10},{9,11},{10,... | collective-permute-start | bytes 196616 | tf_op jit(solution)/shard_map/ppermute | solution.py:258
  21.3 8.1 %collective-permute-start.14 = (bf16[256,128]{1,0:T(8,128)(2,1)S(1)}, bf16[256,128]{1,0:T(8,128)(2,1)S(1)}, u32[]{:S(2)}, u32[]{:S(2)}) collective-permute-start(bf16[256,128]{1,0:T(8,128)(2,1)S(1)} %get-tuple-element.45), channel_id=1, source_target_pairs={{0,16},{4,20},{8,24},{12,28},{16,0},{20,4},{24,8},{28,12},{1,17},{... | collective-permute-start | bytes 196616 | tf_op jit(solution)/shard_map/ppermute | solution.py:206
  23.9 10.0 %copy-start.3 = (bf16[128,512]{1,0:T(8,128)(2,1)S(1)}, bf16[128,512]{1,0:T(8,128)(2,1)}, u32[]{:S(2)}) copy-start(bf16[128,512]{1,0:T(8,128)(2,1)} %up_ref.3) | copy-start | bytes 393220
  23.9 10.0 %copy-start.4 = (bf16[512,128]{1,0:T(8,128)(2,1)S(1)}, bf16[512,128]{1,0:T(8,128)(2,1)}, u32[]{:S(2)}) copy-start(bf16[512,128]{1,0:T(8,128)(2,1)} %down_ref.3) | copy-start | bytes 393220
  23.9 7.2 %collective-permute-start.15 = (bf16[256,128]{1,0:T(8,128)(2,1)S(1)}, bf16[256,128]{1,0:T(8,128)(2,1)S(1)}, u32[]{:S(2)}, u32[]{:S(2)}) collective-permute-start(bf16[256,128]{1,0:T(8,128)(2,1)S(1)} %get-tuple-element.46), channel_id=1, source_target_pairs={{0,12},{4,8},{8,4},{12,0},{16,28},{20,24},{24,20},{28,16},{1,13},{... | collective-permute-start | bytes 196616 | tf_op jit(solution)/shard_map/ppermute | solution.py:206
  24.7 6.5 %collective-permute-start.2 = (bf16[2,4,32,128]{3,2,1,0:T(8,128)(2,1)S(1)}, bf16[2,4,32,128]{3,2,1,0:T(8,128)(2,1)S(1)}, u32[]{:S(2)}, u32[]{:S(2)}) collective-permute-start(bf16[2,4,32,128]{3,2,1,0:T(8,128)(2,1)S(1)} %add_convert_fusion.1), channel_id=1, source_target_pairs={{0,1},{1,0},{2,3},{3,2},{4,5},{5,4},{6,7},{7,6},{8,9},{9,8},{10,11... | collective-permute-start | bytes 196616 | tf_op jit(solution)/shard_map/ppermute | solution.py:258
  24.8 10.8 %collective-permute-start.9 = (bf16[256,128]{1,0:T(8,128)(2,1)S(1)}, bf16[256,128]{1,0:T(8,128)(2,1)S(1)}, u32[]{:S(2)}, u32[]{:S(2)}) collective-permute-start(bf16[256,128]{1,0:T(8,128)(2,1)S(1)} %get-tuple-element.39), channel_id=1, source_target_pairs={{0,20},{4,16},{8,28},{12,24},{16,4},{20,0},{24,12},{28,8},{1,21},{... | collective-permute-start | bytes 196616 | tf_op jit(solution)/shard_map/ppermute | solution.py:206
  27.4 8.2 %collective-permute-start.10 = (bf16[256,128]{1,0:T(8,128)(2,1)S(1)}, bf16[256,128]{1,0:T(8,128)(2,1)S(1)}, u32[]{:S(2)}, u32[]{:S(2)}) collective-permute-start(bf16[256,128]{1,0:T(8,128)(2,1)S(1)} %get-tuple-element.40), channel_id=1, source_target_pairs={{0,24},{4,28},{8,16},{12,20},{16,8},{20,12},{24,0},{28,4},{1,25},{... | collective-permute-start | bytes 196616 | tf_op jit(solution)/shard_map/ppermute | solution.py:206
  29.4 7.3 %collective-permute-start.11 = (bf16[256,128]{1,0:T(8,128)(2,1)S(1)}, bf16[256,128]{1,0:T(8,128)(2,1)S(1)}, u32[]{:S(2)}, u32[]{:S(2)}) collective-permute-start(bf16[256,128]{1,0:T(8,128)(2,1)S(1)} %get-tuple-element.41), channel_id=1, source_target_pairs={{0,28},{4,24},{8,20},{12,16},{16,12},{20,8},{24,4},{28,0},{1,29},{... | collective-permute-start | bytes 196616 | tf_op jit(solution)/shard_map/ppermute | solution.py:206
  31.2 5.6 %collective-permute-start.12 = (bf16[256,128]{1,0:T(8,128)(2,1)S(1)}, bf16[256,128]{1,0:T(8,128)(2,1)S(1)}, u32[]{:S(2)}, u32[]{:S(2)}) collective-permute-start(bf16[256,128]{1,0:T(8,128)(2,1)S(1)} %get-tuple-element.42), channel_id=1, source_target_pairs={{0,8},{4,12},{8,0},{12,4},{16,24},{20,28},{24,16},{28,20},{1,9},{5... | collective-permute-start | bytes 196616 | tf_op jit(solution)/shard_map/ppermute | solution.py:206
  31.2 5.6 %collective-permute-start.13 = (bf16[256,128]{1,0:T(8,128)(2,1)S(1)}, bf16[256,128]{1,0:T(8,128)(2,1)S(1)}, u32[]{:S(2)}, u32[]{:S(2)}) collective-permute-start(bf16[256,128]{1,0:T(8,128)(2,1)S(1)} %get-tuple-element.43), channel_id=1, source_target_pairs={{0,4},{4,0},{8,12},{12,8},{16,20},{20,16},{24,28},{28,24},{1,5},{5... | collective-permute-start | bytes 196616 | tf_op jit(solution)/shard_map/ppermute | solution.py:206

commit v5 on v4

--- a/solution.py
+++ b/solution.py
@@ -87,8 +87,20 @@
 
 
 def row_kernel(
-    x_ref, query_ref, gate_ref, state_ref, head_gain_ref, out_weight_ref, gain_ref, updated_ref, gain_out_ref
+    steps,
+    parts,
+    x_ref,
+    query_ref,
+    gate_ref,
+    state_ref,
+    head_gain_ref,
+    out_weight_ref,
+    gain_ref,
+    up_ref,
+    down_ref,
+    *refs,
 ):
+    updated_ref, gain_out_ref, out_hbm, *scratch = refs[len(steps) :]
     row_count, col_count, width = x_ref.shape
     keep = head_mask(width, width)
     heads = width // HEAD
@@ -103,6 +115,7 @@
             out = matmul(mixed.astype(BF16), out_weight_ref[branch])
             total = total + out.astype(BF16).astype(F32)
         updated_ref[row] = total
+    finish(steps, parts, updated_ref, gain_ref, up_ref, down_ref, refs[: len(steps)], out_hbm, *scratch)
 
 
 def column_kernel(
@@ -153,10 +166,22 @@
             sent_refs[step][group * piece : (group + 1) * piece] = query_ref[start : start + piece]
 
 
-def final_kernel(steps, parts, fresh, updated_ref, gain_ref, up_ref, down_ref, *refs):
+def finish(
+    steps,
+    parts,
+    updated_ref,
+    gain_ref,
+    up_ref,
+    down_ref,
+    got_refs,
+    out_hbm,
+    sum_ref,
+    trans_ref,
+    hidden_ref,
+    out_ref,
+    sems,
+):
     row_count, col_count, width = updated_ref.shape
-    got_refs = refs[: len(steps)]
-    out_hbm, sum_ref, trans_ref, hidden_ref, out_ref, sems = refs[len(steps) + (not fresh) :]
     cols = col_count // parts
     tokens = row_count * cols
     me = lax.axis_index("row")
@@ -169,10 +194,8 @@
         updated = updated_ref[:, spans[at], :].reshape(tokens, width) + third
         sum_ref[span] = updated
         trans_ref[span] = normalize(updated, gain).astype(BF16)
-    for at in range(len(steps)):
-        span = slice(at * tokens, (at + 1) * tokens)
-        half = 0.5 * matmul(trans_ref[span], up_ref[...])
-        hidden_ref[span] = (half * jnp.tanh(half) + half).astype(BF16)
+    half = 0.5 * matmul(trans_ref[...], up_ref[...])
+    hidden_ref[...] = (half * jnp.tanh(half) + half).astype(BF16)
     stores = []
     for at in range(len(steps)):
         span = slice(at * tokens, (at + 1) * tokens)
@@ -185,17 +208,27 @@
         store.wait()
 
 
+def final_kernel(steps, parts, updated_ref, gain_ref, up_ref, down_ref, *refs):
+    got_refs = refs[: len(steps)]
+    finish(steps, parts, updated_ref, gain_ref, up_ref, down_ref, got_refs, *refs[len(steps) + 1 :])
+
+
+def far_steps(parts):
+    half = parts // 2
+    return (*range(half + 1, min(half + 2, parts)), *range(parts - 1, half + 1, -1))
+
+
 def inward_order(parts):
     half = parts // 2
-    steps = (0, half, half - 1, *range(half + 1, parts), *range(1, half - 1))
+    steps = (0, half, half - 1, *far_steps(parts), *range(1, half - 1))
     return tuple(dict.fromkeys(steps))
 
 
 def outward_orders(parts):
     half = parts // 2
     early = tuple(dict.fromkeys((0, half, half - 1)))
-    late = (*range(half + 1, parts), *range(half - 2, 0, -1))
-    return (early, late) if late else (early,)
+    late = (*far_steps(parts), *range(half - 2, 0, -1))
+    return early, late
 
 
 def exchange(pieces):
@@ -257,11 +290,6 @@
         pairs = [(at, at ^ step) for at in range(col_parts)]
         state = (state.astype(F32) + lax.ppermute(state, "col", pairs).astype(F32)).astype(BF16)
         step //= 2
-    updated, gain = call(
-        row_kernel,
-        (struct(pair_map.shape, F32), struct((1, width), F32)),
-        "row_out",
-    )(pair_map, query, gate, state, head_gain, out_weights, trans_gain.reshape(1, width))
     order = inward_order(parts)
     column_out = call(
         functools.partial(column_kernel, row_count, order),
@@ -282,33 +310,51 @@
 
     third = exchange(column_out)
 
-    result = None
-    for steps in outward_orders(parts):
-        fresh = result is None
+    def scratch(steps):
         count = len(steps)
-        result = call(
-            functools.partial(final_kernel, steps, parts, fresh),
+        return [
+            pltpu.VMEM((count * tokens, width), F32),
+            pltpu.VMEM((count * tokens, width), BF16),
+            pltpu.VMEM((count * tokens, hidden), BF16),
+            pltpu.VMEM((count, row_count, cols, width), BF16),
+            pltpu.SemaphoreType.DMA((count,)),
+        ]
+
+    early, late = outward_orders(parts)
+    updated, gain, result = call(
+        functools.partial(row_kernel, early, parts),
+        (
+            struct(pair_map.shape, F32),
+            struct((1, width), F32),
             struct(pair_map.shape, BF16),
-            "final",
-            in_specs=[vmem] * (4 + count) + [anywhere] * (not fresh),
-            out_specs=anywhere,
-            input_output_aliases={} if fresh else {4 + count: 0},
-            scratch_shapes=[
-                pltpu.VMEM((count * tokens, width), F32),
-                pltpu.VMEM((count * tokens, width), BF16),
-                pltpu.VMEM((count * tokens, hidden), BF16),
-                pltpu.VMEM((count, row_count, cols, width), BF16),
-                pltpu.SemaphoreType.DMA((count,)),
-            ],
-        )(
-            updated,
-            gain,
-            up_weight,
-            down_weight,
-            *[third[step] for step in steps],
-            *([] if fresh else [result]),
-        )
-    return result
+        ),
+        "row_out",
+        in_specs=[vmem] * (9 + len(early)),
+        out_specs=(vmem, vmem, anywhere),
+        scratch_shapes=scratch(early),
+    )(
+        pair_map,
+        query,
+        gate,
+        state,
+        head_gain,
+        out_weights,
+        trans_gain.reshape(1, width),
+        up_weight,
+        down_weight,
+        *[third[step] for step in early],
+    )
+    if not late:
+        return result
+    return call(
+        functools.partial(final_kernel, late, parts),
+        struct(pair_map.shape, BF16),
+        "final",
+        in_specs=[vmem] * (4 + len(late)) + [anywhere],
+        out_specs=anywhere,
+        input_output_aliases={4 + len(late): 0},
+        scratch_shapes=scratch(late),
+    )(updated, gain, up_weight, down_weight, *[third[step] for step in late], result)
 
 
 def solution(mesh):

time: 39 us -> 38.7 us (level)
  starting transfers between devices: 25.1 us -> 24.1 us
  waiting for transfers between devices: 2.32 us -> 3.18 us
    ppermute x14, starting transfers between devices: 23.5 us -> 22.6 us  [exchange(): moved[step] = lax.ppermute(pieces[step], 'row', pairs)]
    ppermute x14, waiting for transfers between devices: 2.32 us -> 3.17 us  [exchange(): moved[step] = lax.ppermute(pieces[step], 'row', pairs)]
    pallas_call x3 -> x2, Pallas kernels: 4.73 us -> 4.58 us  [the longest x1 2.61 us: shards(): call(functools.partial(row_kernel, early, parts), (struct(pair_map.shape,...]
where the time goes in v5:
time: 38.7 us; the launch traced here: 38.6 us
  starting transfers between devices  24.1 us (62%)
  Pallas kernels  9.95 us (26%)
  waiting for transfers between devices  3.18 us (8%)
  local copies, waits for them, and re-layouts  1.08 us (3%)
    ppermute x14, starting transfers between devices, exchange(): moved[step] = lax.ppermute(pieces[step], 'row', pairs)  22.6 us
    ppermute x14, waiting for transfers between devices, exchange(): moved[step] = lax.ppermute(pieces[step], 'row', pairs)  3.17 us
    pallas_call x1, Pallas kernels, shards(): call(functools.partial(row_kernel, early, parts), (struct(pair_map.shape,...  2.61 us
    pallas_call x1, Pallas kernels, shards(): call(functools.partial(column_kernel, row_count, order), [struct((tokens,...  2.61 us
    pallas_call x1, Pallas kernels, shards(): call(state_kernel, (struct((2, row_count, HEAD, width), BF16), struct(bot...  2.33 us
    pallas_call x1, Pallas kernels, shards(): call(functools.partial(final_kernel, late, parts), struct(pair_map.shape,...  1.96 us
    ppermute x2, starting transfers between devices, shards(): lax.ppermute(state, 'col', pairs).astype(F32)  1.56 us
    unnamed x18, local copies, waits for them, and re-layouts  1.08 us
  transfers between devices with their start and end apart: 16, of which 4 were waited for; matrix products, arithmetic and copies ran while one was open for 0% of the time, Pallas kernels for 20%

profile of v5, /device:TPU:0, one launch (start us, length us, event | category | flops | bytes accessed | tf_op | source)
XLA Modules:
  0.0 38.6 jit_solution(6262035021896329685)
XLA Ops:
  0.0 0.0 copy-start
  0.0 1.0 %copy-done = bf16[4,512,128]{2,1,0:T(8,128)(2,1)S(1)} copy-done((bf16[4,512,128]{2,1,0:T(8,128)(2,1)S(1)}, bf16[4,512,128]{2,1,0:T(8,128)(2,1)}, u32[]{:S(2)}) %copy-start) | copy-done | bytes 524312
  1.0 0.0 copy-start.2
  1.0 0.0 copy-start.7
  1.0 0.0 copy-start.5
  1.0 0.0 copy-start.6
  1.1 0.4 %pieces.1 = (bf16[256,128]{1,0:T(8,128)(2,1)S(1)}, bf16[256,128]{1,0:T(8,128)(2,1)S(1)}, bf16[256,128]{1,0:T(8,128)(2,1)S(1)}, bf16[256,128]{1,0:T(8,128)(2,1)S(...) custom-call(bf16[4,512,128]{2,1,0:T(8,128)(2,1)S(1)} %copy-done), custom_call_target="tpu_custom_call" | custom-call | flops 10000000000 | tf_op jit(solution)/shard_map/pieces/pallas_call | solution.py:275
  1.5 4.1 %collective-permute-start = (bf16[256,128]{1,0:T(8,128)(2,1)S(1)}, bf16[256,128]{1,0:T(8,128)(2,1)S(1)}, u32[]{:S(2)}, u32[]{:S(2)}) collective-permute-start(bf16[256,128]{1,0:T(8,128)(2,1)S(1)} %get-tuple-element.27), channel_id=1, source_target_pairs={{0,16},{4,20},{8,24},{12,28},{16,0},{20,4},{24,8},{28,12},{1,17},{... | collective-permute-start | bytes 196616 | tf_op jit(solution)/shard_map/ppermute | solution.py:239
  5.6 2.5 %collective-permute-start.3 = (bf16[256,128]{1,0:T(8,128)(2,1)S(1)}, bf16[256,128]{1,0:T(8,128)(2,1)S(1)}, u32[]{:S(2)}, u32[]{:S(2)}) collective-permute-start(bf16[256,128]{1,0:T(8,128)(2,1)S(1)} %get-tuple-element.32), channel_id=1, source_target_pairs={{0,12},{4,8},{8,4},{12,0},{16,28},{20,24},{24,20},{28,16},{1,13},{... | collective-permute-start | bytes 196616 | tf_op jit(solution)/shard_map/ppermute | solution.py:239
  8.1 0.3 collective-permute-start.4
  8.4 3.4 %collective-permute-start.5 = (bf16[256,128]{1,0:T(8,128)(2,1)S(1)}, bf16[256,128]{1,0:T(8,128)(2,1)S(1)}, u32[]{:S(2)}, u32[]{:S(2)}) collective-permute-start(bf16[256,128]{1,0:T(8,128)(2,1)S(1)} %get-tuple-element.34), channel_id=1, source_target_pairs={{0,28},{4,24},{8,20},{12,16},{16,12},{20,8},{24,4},{28,0},{1,29},{... | collective-permute-start | bytes 196616 | tf_op jit(solution)/shard_map/ppermute | solution.py:239
  11.8 1.3 %collective-permute-start.6 = (bf16[256,128]{1,0:T(8,128)(2,1)S(1)}, bf16[256,128]{1,0:T(8,128)(2,1)S(1)}, u32[]{:S(2)}, u32[]{:S(2)}) collective-permute-start(bf16[256,128]{1,0:T(8,128)(2,1)S(1)} %get-tuple-element.35), channel_id=1, source_target_pairs={{0,24},{4,28},{8,16},{12,20},{16,8},{20,12},{24,0},{28,4},{1,25},{... | collective-permute-start | bytes 196616 | tf_op jit(solution)/shard_map/ppermute | solution.py:239
  13.2 0.0 collective-permute-done.after_ref.refs_1_
  13.2 0.5 %collective-permute-start.7 = (bf16[256,128]{1,0:T(8,128)(2,1)S(1)}, bf16[256,128]{1,0:T(8,128)(2,1)S(1)}, u32[]{:S(2)}, u32[]{:S(2)}) collective-permute-start(bf16[256,128]{1,0:T(8,128)(2,1)S(1)} %get-tuple-element.36), channel_id=1, source_target_pairs={{0,4},{4,0},{8,12},{12,8},{16,20},{20,16},{24,28},{28,24},{1,5},{5... | collective-permute-start | bytes 196616 | tf_op jit(solution)/shard_map/ppermute | solution.py:239
  13.7 0.0 collective-permute-done.3.refs_2_
  13.7 0.0 collective-permute-start.8
  13.7 0.0 copy-done.2
  13.7 0.0 copy-done.7
  13.7 0.0 copy-start.1
  13.7 0.0 copy-start.3
  13.7 0.0 copy-start.4
  13.8 0.0 copy-start.8
  13.8 2.3 %row_state.1 = (bf16[2,4,32,128]{3,2,1,0:T(8,128)(2,1)S(1)}, bf16[2,4,512,128]{3,2,1,0:T(8,128)(2,1)S(1)}, f32[2,4,512,128]{3,2,1,0:T(8,128)S(1)}) custom-call(bf16[4,512,128]{2,1,0:T(8,128)(2,1)S(1)} %copy-done, f32[1,128]{1,0:T(1,128)S(1)} %bitcast.2, bf16[3,128,512]{2,1,0:T(8,128)(2,1)S(1)} %copy-done.2, ...), custom_call_target="tpu_custom_call" | custom-call | tf_op jit(solution)/shard_map/row_state/pallas_call | solution.py:282
  16.1 0.8 %collective-permute-done.4.refs_3_ = bf16[256,128]{1,0:T(8,128)(2,1)S(1)} collective-permute-done((bf16[256,128]{1,0:T(8,128)(2,1)S(1)}, bf16[256,128]{1,0:T(8,128)(2,1)S(1)}, u32[]{:S(2)}, u32[]{:S(2)}) %collective-permute-start.4) | collective-permute-done | bytes 65568 | tf_op jit(solution)/shard_map/ppermute | solution.py:239
  16.9 1.5 %collective-permute-start.1 = (bf16[2,4,32,128]{3,2,1,0:T(8,128)(2,1)S(1)}, bf16[2,4,32,128]{3,2,1,0:T(8,128)(2,1)S(1)}, u32[]{:S(2)}, u32[]{:S(2)}) collective-permute-start(bf16[2,4,32,128]{3,2,1,0:T(8,128)(2,1)S(1)} %get-tuple-element.30), channel_id=1, source_target_pairs={{0,2},{1,3},{2,0},{3,1},{4,6},{5,7},{6,4},{7,5},{8,10},{9,11},{10,... | collective-permute-start | bytes 196616 | tf_op jit(solution)/shard_map/ppermute | solution.py:291
  18.4 0.0 collective-permute-done.5.refs_4_
  18.4 0.0 collective-permute-done.6.refs_5_
  18.4 0.0 collective-permute-done.7.refs_6_
  18.4 0.2 collective-permute-done.8.refs_7_
  18.7 0.0 copy-done.5
  18.7 0.0 copy-done.6
  18.7 2.6 %column.1 = (bf16[256,128]{1,0:T(8,128)(2,1)S(1)}, bf16[256,128]{1,0:T(8,128)(2,1)S(1)}, bf16[256,128]{1,0:T(8,128)(2,1)S(1)}, bf16[256,128]{1,0:T(8,128)(2,1)S(...) custom-call(f32[1,128]{1,0:T(1,128)S(1)} %bitcast.3, ...), custom_call_target="tpu_custom_call" | custom-call | tf_op jit(solution)/shard_map/column/pallas_call | solution.py:294
  21.3 2.7 %collective-permute-start.9 = (bf16[256,128]{1,0:T(8,128)(2,1)S(1)}, bf16[256,128]{1,0:T(8,128)(2,1)S(1)}, u32[]{:S(2)}, u32[]{:S(2)}) collective-permute-start(bf16[256,128]{1,0:T(8,128)(2,1)S(1)} %get-tuple-element.39), channel_id=1, source_target_pairs={{0,16},{4,20},{8,24},{12,28},{16,0},{20,4},{24,8},{28,12},{1,17},{... | collective-permute-start | bytes 196616 | tf_op jit(solution)/shard_map/ppermute | solution.py:239
  24.0 0.7 %collective-permute-start.10 = (bf16[256,128]{1,0:T(8,128)(2,1)S(1)}, bf16[256,128]{1,0:T(8,128)(2,1)S(1)}, u32[]{:S(2)}, u32[]{:S(2)}) collective-permute-start(bf16[256,128]{1,0:T(8,128)(2,1)S(1)} %get-tuple-element.40), channel_id=1, source_target_pairs={{0,12},{4,8},{8,4},{12,0},{16,28},{20,24},{24,20},{28,16},{1,13},{... | collective-permute-start | bytes 196616 | tf_op jit(solution)/shard_map/ppermute | solution.py:239
  24.6 0.0 collective-permute-done.1
  24.7 0.1 collective-permute-start.2
  24.8 1.7 %collective-permute-start.11 = (bf16[256,128]{1,0:T(8,128)(2,1)S(1)}, bf16[256,128]{1,0:T(8,128)(2,1)S(1)}, u32[]{:S(2)}, u32[]{:S(2)}) collective-permute-start(bf16[256,128]{1,0:T(8,128)(2,1)S(1)} %get-tuple-element.43), channel_id=1, source_target_pairs={{0,20},{4,16},{8,28},{12,24},{16,4},{20,0},{24,12},{28,8},{1,21},{... | collective-permute-start | bytes 196616 | tf_op jit(solution)/shard_map/ppermute | solution.py:239
  26.4 3.4 %collective-permute-start.12 = (bf16[256,128]{1,0:T(8,128)(2,1)S(1)}, bf16[256,128]{1,0:T(8,128)(2,1)S(1)}, u32[]{:S(2)}, u32[]{:S(2)}) collective-permute-start(bf16[256,128]{1,0:T(8,128)(2,1)S(1)} %get-tuple-element.44), channel_id=1, source_target_pairs={{0,28},{4,24},{8,20},{12,16},{16,12},{20,8},{24,4},{28,0},{1,29},{... | collective-permute-start | bytes 196616 | tf_op jit(solution)/shard_map/ppermute | solution.py:239
  29.8 0.0 collective-permute-done.9.refs_1_
  29.8 1.4 %collective-permute-start.13 = (bf16[256,128]{1,0:T(8,128)(2,1)S(1)}, bf16[256,128]{1,0:T(8,128)(2,1)S(1)}, u32[]{:S(2)}, u32[]{:S(2)}) collective-permute-start(bf16[256,128]{1,0:T(8,128)(2,1)S(1)} %get-tuple-element.45), channel_id=1, source_target_pairs={{0,24},{4,28},{8,16},{12,20},{16,8},{20,12},{24,0},{28,4},{1,25},{... | collective-permute-start | bytes 196616 | tf_op jit(solution)/shard_map/ppermute | solution.py:239
  31.2 0.0 collective-permute-done.10.refs_2_
  31.2 0.0 collective-permute-start.14
  31.2 0.0 collective-permute-done.2
  31.2 0.6 %collective-permute-start.15 = (bf16[256,128]{1,0:T(8,128)(2,1)S(1)}, bf16[256,128]{1,0:T(8,128)(2,1)S(1)}, u32[]{:S(2)}, u32[]{:S(2)}) collective-permute-start(bf16[256,128]{1,0:T(8,128)(2,1)S(1)} %get-tuple-element.47), channel_id=1, source_target_pairs={{0,4},{4,0},{8,12},{12,8},{16,20},{20,16},{24,28},{28,24},{1,5},{5... | collective-permute-start | bytes 196616 | tf_op jit(solution)/shard_map/ppermute | solution.py:239
  31.8 0.0 copy-done.1
  31.8 0.0 copy-done.3
  31.8 0.0 copy-done.4
  31.8 0.0 copy-done.8
  31.8 2.6 %row_out.1 = (f32[4,512,128]{2,1,0:T(8,128)S(1)}, f32[1,128]{1,0:T(1,128)S(1)}, bf16[4,512,128]{2,1,0:T(8,128)(2,1)}) custom-call(bf16[4,512,128]{2,1,0:T(8,128)(2,1)S(1)} %copy-done.1, bf16[2,4,512,128]{3,2,1,0:T(8,128)(2,1)S(1)} %get-tuple-element.28.query_ref, f32[2,4,512,128]{3,2,1,0:T(8,128)S(1)} %get-tuple-element.29.refs_8_.gate_ref, ...), custom_call_target="tpu_custom_call" | custom-call | tf_op jit(solution)/shard_map/row_out/pallas_call | solution.py:324
  34.5 0.0 collective-permute-done.11.refs_0_
  34.5 0.0 collective-permute-done.12.refs_1_
  34.5 1.8 %collective-permute-done.13.refs_2_ = bf16[256,128]{1,0:T(8,128)(2,1)S(1)} collective-permute-done((bf16[256,128]{1,0:T(8,128)(2,1)S(1)}, bf16[256,128]{1,0:T(8,128)(2,1)S(1)}, u32[]{:S(2)}, u32[]{:S(2)}) %collective-permute-start.13) | collective-permute-done | bytes 65568 | tf_op jit(solution)/shard_map/ppermute | solution.py:239
  36.3 0.3 collective-permute-done.14.refs_3_
  36.6 0.0 collective-permute-done.15.refs_4_
  36.6 2.0 %final.1 = bf16[4,512,128]{2,1,0:T(8,128)(2,1)} custom-call(f32[4,512,128]{2,1,0:T(8,128)S(1)} %get-tuple-element.41.updated_ref, f32[1,128]{1,0:T(1,128)S(1)} %get-tuple-element.42.gain_ref, bf16[128,512]{1,0:T(8,128)(2,1)S(1)} %copy-done.3, bf16[512,128]{1,0:T(8,128)(2,1)S(1)} %copy-done.4, ...), custom_call_target="tpu_custom_call", output_to_operand_aliasing={{}: (9, {})} | custom-call | tf_op jit(solution)/shard_map/final/pallas_call | solution.py:349
  (2 shorter events, 0.0 us)
Async XLA Ops:
  0.0 1.0 %copy-start = (bf16[4,512,128]{2,1,0:T(8,128)(2,1)S(1)}, bf16[4,512,128]{2,1,0:T(8,128)(2,1)}, u32[]{:S(2)}) copy-start(bf16[4,512,128]{2,1,0:T(8,128)(2,1)} %x_ref.5) | copy-start | bytes 1572868
  1.0 12.7 %copy-start.2 = (bf16[3,128,512]{2,1,0:T(8,128)(2,1)S(1)}, bf16[3,128,512]{2,1,0:T(8,128)(2,1)}, u32[]{:S(2)}) copy-start(bf16[3,128,512]{2,1,0:T(8,128)(2,1)} %weight_ref.3) | copy-start | bytes 1179652
  1.0 12.7 %copy-start.7 = (f32[128]{0:T(128)S(1)}, f32[128]{0:T(128)}, u32[]{:S(2)}) copy-start(f32[128]{0:T(128)} %param.9) | copy-start | bytes 1540
  1.0 17.6 %copy-start.5 = (bf16[3,128,128]{2,1,0:T(8,128)(2,1)S(1)}, bf16[3,128,128]{2,1,0:T(8,128)(2,1)}, u32[]{:S(2)}) copy-start(bf16[3,128,128]{2,1,0:T(8,128)(2,1)} %out_weight_ref.3) | copy-start | bytes 294916
  1.0 17.6 %copy-start.6 = (f32[3,128]{1,0:T(4,128)S(1)}, f32[3,128]{1,0:T(4,128)}, u32[]{:S(2)}) copy-start(f32[3,128]{1,0:T(4,128)} %head_gain_ref.3) | copy-start | bytes 4612
  1.5 11.7 %collective-permute-start = (bf16[256,128]{1,0:T(8,128)(2,1)S(1)}, bf16[256,128]{1,0:T(8,128)(2,1)S(1)}, u32[]{:S(2)}, u32[]{:S(2)}) collective-permute-start(bf16[256,128]{1,0:T(8,128)(2,1)S(1)} %get-tuple-element.27), channel_id=1, source_target_pairs={{0,16},{4,20},{8,24},{12,28},{16,0},{20,4},{24,8},{28,12},{1,17},{... | collective-permute-start | bytes 196616 | tf_op jit(solution)/shard_map/ppermute | solution.py:239
  5.6 8.1 %collective-permute-start.3 = (bf16[256,128]{1,0:T(8,128)(2,1)S(1)}, bf16[256,128]{1,0:T(8,128)(2,1)S(1)}, u32[]{:S(2)}, u32[]{:S(2)}) collective-permute-start(bf16[256,128]{1,0:T(8,128)(2,1)S(1)} %get-tuple-element.32), channel_id=1, source_target_pairs={{0,12},{4,8},{8,4},{12,0},{16,28},{20,24},{24,20},{28,16},{1,13},{... | collective-permute-start | bytes 196616 | tf_op jit(solution)/shard_map/ppermute | solution.py:239
  8.1 8.8 %collective-permute-start.4 = (bf16[256,128]{1,0:T(8,128)(2,1)S(1)}, bf16[256,128]{1,0:T(8,128)(2,1)S(1)}, u32[]{:S(2)}, u32[]{:S(2)}) collective-permute-start(bf16[256,128]{1,0:T(8,128)(2,1)S(1)} %get-tuple-element.33), channel_id=1, source_target_pairs={{0,20},{4,16},{8,28},{12,24},{16,4},{20,0},{24,12},{28,8},{1,21},{... | collective-permute-start | bytes 196616 | tf_op jit(solution)/shard_map/ppermute | solution.py:239
  8.4 10.0 %collective-permute-start.5 = (bf16[256,128]{1,0:T(8,128)(2,1)S(1)}, bf16[256,128]{1,0:T(8,128)(2,1)S(1)}, u32[]{:S(2)}, u32[]{:S(2)}) collective-permute-start(bf16[256,128]{1,0:T(8,128)(2,1)S(1)} %get-tuple-element.34), channel_id=1, source_target_pairs={{0,28},{4,24},{8,20},{12,16},{16,12},{20,8},{24,4},{28,0},{1,29},{... | collective-permute-start | bytes 196616 | tf_op jit(solution)/shard_map/ppermute | solution.py:239
  11.8 6.6 %collective-permute-start.6 = (bf16[256,128]{1,0:T(8,128)(2,1)S(1)}, bf16[256,128]{1,0:T(8,128)(2,1)S(1)}, u32[]{:S(2)}, u32[]{:S(2)}) collective-permute-start(bf16[256,128]{1,0:T(8,128)(2,1)S(1)} %get-tuple-element.35), channel_id=1, source_target_pairs={{0,24},{4,28},{8,16},{12,20},{16,8},{20,12},{24,0},{28,4},{1,25},{... | collective-permute-start | bytes 196616 | tf_op jit(solution)/shard_map/ppermute | solution.py:239
  13.2 5.2 %collective-permute-start.7 = (bf16[256,128]{1,0:T(8,128)(2,1)S(1)}, bf16[256,128]{1,0:T(8,128)(2,1)S(1)}, u32[]{:S(2)}, u32[]{:S(2)}) collective-permute-start(bf16[256,128]{1,0:T(8,128)(2,1)S(1)} %get-tuple-element.36), channel_id=1, source_target_pairs={{0,4},{4,0},{8,12},{12,8},{16,20},{20,16},{24,28},{28,24},{1,5},{5... | collective-permute-start | bytes 196616 | tf_op jit(solution)/shard_map/ppermute | solution.py:239
  13.7 5.0 %collective-permute-start.8 = (bf16[256,128]{1,0:T(8,128)(2,1)S(1)}, bf16[256,128]{1,0:T(8,128)(2,1)S(1)}, u32[]{:S(2)}, u32[]{:S(2)}) collective-permute-start(bf16[256,128]{1,0:T(8,128)(2,1)S(1)} %get-tuple-element.37), channel_id=1, source_target_pairs={{0,8},{4,12},{8,0},{12,4},{16,24},{20,28},{24,16},{28,20},{1,9},{5... | collective-permute-start | bytes 196616 | tf_op jit(solution)/shard_map/ppermute | solution.py:239
  13.7 18.1 %copy-start.1 = (bf16[4,512,128]{2,1,0:T(8,128)(2,1)S(1)}, bf16[4,512,128]{2,1,0:T(8,128)(2,1)}, u32[]{:S(2)}) copy-start(bf16[4,512,128]{2,1,0:T(8,128)(2,1)} %x_ref.5) | copy-start | bytes 1572868
  13.7 18.1 %copy-start.3 = (bf16[128,512]{1,0:T(8,128)(2,1)S(1)}, bf16[128,512]{1,0:T(8,128)(2,1)}, u32[]{:S(2)}) copy-start(bf16[128,512]{1,0:T(8,128)(2,1)} %up_ref.3) | copy-start | bytes 393220
  13.7 18.1 %copy-start.4 = (bf16[512,128]{1,0:T(8,128)(2,1)S(1)}, bf16[512,128]{1,0:T(8,128)(2,1)}, u32[]{:S(2)}) copy-start(bf16[512,128]{1,0:T(8,128)(2,1)} %down_ref.3) | copy-start | bytes 393220
  13.8 18.1 %copy-start.8 = (f32[128]{0:T(128)S(1)}, f32[128]{0:T(128)}, u32[]{:S(2)}) copy-start(f32[128]{0:T(128)} %param.13) | copy-start | bytes 1540
  16.9 7.7 %collective-permute-start.1 = (bf16[2,4,32,128]{3,2,1,0:T(8,128)(2,1)S(1)}, bf16[2,4,32,128]{3,2,1,0:T(8,128)(2,1)S(1)}, u32[]{:S(2)}, u32[]{:S(2)}) collective-permute-start(bf16[2,4,32,128]{3,2,1,0:T(8,128)(2,1)S(1)} %get-tuple-element.30), channel_id=1, source_target_pairs={{0,2},{1,3},{2,0},{3,1},{4,6},{5,7},{6,4},{7,5},{8,10},{9,11},{10,... | collective-permute-start | bytes 196616 | tf_op jit(solution)/shard_map/ppermute | solution.py:291
  21.3 8.6 %collective-permute-start.9 = (bf16[256,128]{1,0:T(8,128)(2,1)S(1)}, bf16[256,128]{1,0:T(8,128)(2,1)S(1)}, u32[]{:S(2)}, u32[]{:S(2)}) collective-permute-start(bf16[256,128]{1,0:T(8,128)(2,1)S(1)} %get-tuple-element.39), channel_id=1, source_target_pairs={{0,16},{4,20},{8,24},{12,28},{16,0},{20,4},{24,8},{28,12},{1,17},{... | collective-permute-start | bytes 196616 | tf_op jit(solution)/shard_map/ppermute | solution.py:239
  24.0 7.2 %collective-permute-start.10 = (bf16[256,128]{1,0:T(8,128)(2,1)S(1)}, bf16[256,128]{1,0:T(8,128)(2,1)S(1)}, u32[]{:S(2)}, u32[]{:S(2)}) collective-permute-start(bf16[256,128]{1,0:T(8,128)(2,1)S(1)} %get-tuple-element.40), channel_id=1, source_target_pairs={{0,12},{4,8},{8,4},{12,0},{16,28},{20,24},{24,20},{28,16},{1,13},{... | collective-permute-start | bytes 196616 | tf_op jit(solution)/shard_map/ppermute | solution.py:239
  24.7 6.5 %collective-permute-start.2 = (bf16[2,4,32,128]{3,2,1,0:T(8,128)(2,1)S(1)}, bf16[2,4,32,128]{3,2,1,0:T(8,128)(2,1)S(1)}, u32[]{:S(2)}, u32[]{:S(2)}) collective-permute-start(bf16[2,4,32,128]{3,2,1,0:T(8,128)(2,1)S(1)} %add_convert_fusion.1), channel_id=1, source_target_pairs={{0,1},{1,0},{2,3},{3,2},{4,5},{5,4},{6,7},{7,6},{8,9},{9,8},{10,11... | collective-permute-start | bytes 196616 | tf_op jit(solution)/shard_map/ppermute | solution.py:291
  24.8 9.7 %collective-permute-start.11 = (bf16[256,128]{1,0:T(8,128)(2,1)S(1)}, bf16[256,128]{1,0:T(8,128)(2,1)S(1)}, u32[]{:S(2)}, u32[]{:S(2)}) collective-permute-start(bf16[256,128]{1,0:T(8,128)(2,1)S(1)} %get-tuple-element.43), channel_id=1, source_target_pairs={{0,20},{4,16},{8,28},{12,24},{16,4},{20,0},{24,12},{28,8},{1,21},{... | collective-permute-start | bytes 196616 | tf_op jit(solution)/shard_map/ppermute | solution.py:239
  26.4 8.1 %collective-permute-start.12 = (bf16[256,128]{1,0:T(8,128)(2,1)S(1)}, bf16[256,128]{1,0:T(8,128)(2,1)S(1)}, u32[]{:S(2)}, u32[]{:S(2)}) collective-permute-start(bf16[256,128]{1,0:T(8,128)(2,1)S(1)} %get-tuple-element.44), channel_id=1, source_target_pairs={{0,28},{4,24},{8,20},{12,16},{16,12},{20,8},{24,4},{28,0},{1,29},{... | collective-permute-start | bytes 196616 | tf_op jit(solution)/shard_map/ppermute | solution.py:239
  29.8 6.4 %collective-permute-start.13 = (bf16[256,128]{1,0:T(8,128)(2,1)S(1)}, bf16[256,128]{1,0:T(8,128)(2,1)S(1)}, u32[]{:S(2)}, u32[]{:S(2)}) collective-permute-start(bf16[256,128]{1,0:T(8,128)(2,1)S(1)} %get-tuple-element.45), channel_id=1, source_target_pairs={{0,24},{4,28},{8,16},{12,20},{16,8},{20,12},{24,0},{28,4},{1,25},{... | collective-permute-start | bytes 196616 | tf_op jit(solution)/shard_map/ppermute | solution.py:239
  31.2 5.4 %collective-permute-start.14 = (bf16[256,128]{1,0:T(8,128)(2,1)S(1)}, bf16[256,128]{1,0:T(8,128)(2,1)S(1)}, u32[]{:S(2)}, u32[]{:S(2)}) collective-permute-start(bf16[256,128]{1,0:T(8,128)(2,1)S(1)} %get-tuple-element.46), channel_id=1, source_target_pairs={{0,8},{4,12},{8,0},{12,4},{16,24},{20,28},{24,16},{28,20},{1,9},{5... | collective-permute-start | bytes 196616 | tf_op jit(solution)/shard_map/ppermute | solution.py:239
  31.2 5.4 %collective-permute-start.15 = (bf16[256,128]{1,0:T(8,128)(2,1)S(1)}, bf16[256,128]{1,0:T(8,128)(2,1)S(1)}, u32[]{:S(2)}, u32[]{:S(2)}) collective-permute-start(bf16[256,128]{1,0:T(8,128)(2,1)S(1)} %get-tuple-element.47), channel_id=1, source_target_pairs={{0,4},{4,0},{8,12},{12,8},{16,20},{20,16},{24,28},{28,24},{1,5},{5... | collective-permute-start | bytes 196616 | tf_op jit(solution)/shard_map/ppermute | solution.py:239

commit v6 on v5

--- a/solution.py
+++ b/solution.py
@@ -105,15 +105,16 @@
     keep = head_mask(width, width)
     heads = width // HEAD
     gain_out_ref[...] = gain_ref[...]
+    project = out_weight_ref[:2].reshape(2 * width, width)
     for row in range(row_count):
-        total = x_ref[row].astype(F32)
+        mixed = []
         for branch in range(2):
             packed = state_ref[branch, row].astype(F32)
             state = jnp.where(keep, jnp.concatenate([packed] * heads, axis=0), 0.0).astype(BF16)
             head_out = matmul(query_ref[branch, row], state)
-            mixed = normalize(head_out, head_gain_ref[branch : branch + 1]) * gate_ref[branch, row]
-            out = matmul(mixed.astype(BF16), out_weight_ref[branch])
-            total = total + out.astype(BF16).astype(F32)
+            head_out = normalize(head_out, head_gain_ref[branch : branch + 1])
+            mixed.append((head_out * gate_ref[branch, row]).astype(BF16))
+        total = x_ref[row].astype(F32) + matmul(jnp.concatenate(mixed, axis=1), project)
         updated_ref[row] = total
     finish(steps, parts, updated_ref, gain_ref, up_ref, down_ref, refs[: len(steps)], out_hbm, *scratch)
 

time: 38.7 us -> 38.7 us (level)
  transfers between devices with their start and end apart: 16 -> 16, of which waited for: 4 -> 4; matrix products, arithmetic and copies ran while one was open for 0% -> 0% of each run, Pallas kernels for 20% -> 19%
where the time goes in v6:
time: 38.7 us; the launch traced here: 38.6 us
  starting transfers between devices  24.1 us (62%)
  Pallas kernels  9.86 us (25%)
  waiting for transfers between devices  3.27 us (8%)
  local copies, waits for them, and re-layouts  1.08 us (3%)
    ppermute x14, starting transfers between devices, exchange(): moved[step] = lax.ppermute(pieces[step], 'row', pairs)  22.6 us
    ppermute x14, waiting for transfers between devices, exchange(): moved[step] = lax.ppermute(pieces[step], 'row', pairs)  3.26 us
    pallas_call x1, Pallas kernels, shards(): call(functools.partial(column_kernel, row_count, order), [struct((tokens,...  2.61 us
    pallas_call x1, Pallas kernels, shards(): call(functools.partial(row_kernel, early, parts), (struct(pair_map.shape,...  2.52 us
    pallas_call x1, Pallas kernels, shards(): call(state_kernel, (struct((2, row_count, HEAD, width), BF16), struct(bot...  2.33 us
    pallas_call x1, Pallas kernels, shards(): call(functools.partial(final_kernel, late, parts), struct(pair_map.shape,...  1.96 us
    ppermute x2, starting transfers between devices, shards(): lax.ppermute(state, 'col', pairs).astype(F32)  1.56 us
    unnamed x18, local copies, waits for them, and re-layouts  1.08 us
  transfers between devices with their start and end apart: 16, of which 4 were waited for; matrix products, arithmetic and copies ran while one was open for 0% of the time, Pallas kernels for 19%

profile of v6, /device:TPU:0, one launch (start us, length us, event | category | flops | bytes accessed | tf_op | source)
XLA Modules:
  0.0 38.6 jit_solution(9026758513893146452)
XLA Ops:
  0.0 0.0 copy-start
  0.0 1.0 %copy-done = bf16[4,512,128]{2,1,0:T(8,128)(2,1)S(1)} copy-done((bf16[4,512,128]{2,1,0:T(8,128)(2,1)S(1)}, bf16[4,512,128]{2,1,0:T(8,128)(2,1)}, u32[]{:S(2)}) %copy-start) | copy-done | bytes 524312
  1.0 0.0 copy-start.2
  1.0 0.0 copy-start.7
  1.0 0.0 copy-start.5
  1.0 0.0 copy-start.6
  1.1 0.4 %pieces.1 = (bf16[256,128]{1,0:T(8,128)(2,1)S(1)}, bf16[256,128]{1,0:T(8,128)(2,1)S(1)}, bf16[256,128]{1,0:T(8,128)(2,1)S(1)}, bf16[256,128]{1,0:T(8,128)(2,1)S(...) custom-call(bf16[4,512,128]{2,1,0:T(8,128)(2,1)S(1)} %copy-done), custom_call_target="tpu_custom_call" | custom-call | flops 10000000000 | tf_op jit(solution)/shard_map/pieces/pallas_call | solution.py:276
  1.5 4.1 %collective-permute-start = (bf16[256,128]{1,0:T(8,128)(2,1)S(1)}, bf16[256,128]{1,0:T(8,128)(2,1)S(1)}, u32[]{:S(2)}, u32[]{:S(2)}) collective-permute-start(bf16[256,128]{1,0:T(8,128)(2,1)S(1)} %get-tuple-element.27), channel_id=1, source_target_pairs={{0,16},{4,20},{8,24},{12,28},{16,0},{20,4},{24,8},{28,12},{1,17},{... | collective-permute-start | bytes 196616 | tf_op jit(solution)/shard_map/ppermute | solution.py:240
  5.6 2.5 %collective-permute-start.3 = (bf16[256,128]{1,0:T(8,128)(2,1)S(1)}, bf16[256,128]{1,0:T(8,128)(2,1)S(1)}, u32[]{:S(2)}, u32[]{:S(2)}) collective-permute-start(bf16[256,128]{1,0:T(8,128)(2,1)S(1)} %get-tuple-element.32), channel_id=1, source_target_pairs={{0,12},{4,8},{8,4},{12,0},{16,28},{20,24},{24,20},{28,16},{1,13},{... | collective-permute-start | bytes 196616 | tf_op jit(solution)/shard_map/ppermute | solution.py:240
  8.1 0.3 collective-permute-start.4
  8.4 3.4 %collective-permute-start.5 = (bf16[256,128]{1,0:T(8,128)(2,1)S(1)}, bf16[256,128]{1,0:T(8,128)(2,1)S(1)}, u32[]{:S(2)}, u32[]{:S(2)}) collective-permute-start(bf16[256,128]{1,0:T(8,128)(2,1)S(1)} %get-tuple-element.34), channel_id=1, source_target_pairs={{0,28},{4,24},{8,20},{12,16},{16,12},{20,8},{24,4},{28,0},{1,29},{... | collective-permute-start | bytes 196616 | tf_op jit(solution)/shard_map/ppermute | solution.py:240
  11.8 1.3 %collective-permute-start.6 = (bf16[256,128]{1,0:T(8,128)(2,1)S(1)}, bf16[256,128]{1,0:T(8,128)(2,1)S(1)}, u32[]{:S(2)}, u32[]{:S(2)}) collective-permute-start(bf16[256,128]{1,0:T(8,128)(2,1)S(1)} %get-tuple-element.35), channel_id=1, source_target_pairs={{0,24},{4,28},{8,16},{12,20},{16,8},{20,12},{24,0},{28,4},{1,25},{... | collective-permute-start | bytes 196616 | tf_op jit(solution)/shard_map/ppermute | solution.py:240
  13.2 0.0 collective-permute-done.after_ref.refs_1_
  13.2 0.5 %collective-permute-start.7 = (bf16[256,128]{1,0:T(8,128)(2,1)S(1)}, bf16[256,128]{1,0:T(8,128)(2,1)S(1)}, u32[]{:S(2)}, u32[]{:S(2)}) collective-permute-start(bf16[256,128]{1,0:T(8,128)(2,1)S(1)} %get-tuple-element.36), channel_id=1, source_target_pairs={{0,4},{4,0},{8,12},{12,8},{16,20},{20,16},{24,28},{28,24},{1,5},{5... | collective-permute-start | bytes 196616 | tf_op jit(solution)/shard_map/ppermute | solution.py:240
  13.7 0.0 collective-permute-done.3.refs_2_
  13.7 0.0 collective-permute-start.8
  13.7 0.0 copy-done.2
  13.7 0.0 copy-done.7
  13.7 0.0 copy-start.1
  13.7 0.0 copy-start.3
  13.7 0.0 copy-start.4
  13.8 0.0 copy-start.8
  13.8 2.3 %row_state.1 = (bf16[2,4,32,128]{3,2,1,0:T(8,128)(2,1)S(1)}, bf16[2,4,512,128]{3,2,1,0:T(8,128)(2,1)S(1)}, f32[2,4,512,128]{3,2,1,0:T(8,128)S(1)}) custom-call(bf16[4,512,128]{2,1,0:T(8,128)(2,1)S(1)} %copy-done, f32[1,128]{1,0:T(1,128)S(1)} %bitcast.2, bf16[3,128,512]{2,1,0:T(8,128)(2,1)S(1)} %copy-done.2, ...), custom_call_target="tpu_custom_call" | custom-call | tf_op jit(solution)/shard_map/row_state/pallas_call | solution.py:283
  16.1 0.8 %collective-permute-done.4.refs_3_ = bf16[256,128]{1,0:T(8,128)(2,1)S(1)} collective-permute-done((bf16[256,128]{1,0:T(8,128)(2,1)S(1)}, bf16[256,128]{1,0:T(8,128)(2,1)S(1)}, u32[]{:S(2)}, u32[]{:S(2)}) %collective-permute-start.4) | collective-permute-done | bytes 65568 | tf_op jit(solution)/shard_map/ppermute | solution.py:240
  16.9 1.5 %collective-permute-start.1 = (bf16[2,4,32,128]{3,2,1,0:T(8,128)(2,1)S(1)}, bf16[2,4,32,128]{3,2,1,0:T(8,128)(2,1)S(1)}, u32[]{:S(2)}, u32[]{:S(2)}) collective-permute-start(bf16[2,4,32,128]{3,2,1,0:T(8,128)(2,1)S(1)} %get-tuple-element.30), channel_id=1, source_target_pairs={{0,2},{1,3},{2,0},{3,1},{4,6},{5,7},{6,4},{7,5},{8,10},{9,11},{10,... | collective-permute-start | bytes 196616 | tf_op jit(solution)/shard_map/ppermute | solution.py:292
  18.4 0.0 collective-permute-done.5.refs_4_
  18.4 0.0 collective-permute-done.6.refs_5_
  18.4 0.0 collective-permute-done.7.refs_6_
  18.4 0.2 collective-permute-done.8.refs_7_
  18.7 0.0 copy-done.5
  18.7 0.0 copy-done.6
  18.7 2.6 %column.1 = (bf16[256,128]{1,0:T(8,128)(2,1)S(1)}, bf16[256,128]{1,0:T(8,128)(2,1)S(1)}, bf16[256,128]{1,0:T(8,128)(2,1)S(1)}, bf16[256,128]{1,0:T(8,128)(2,1)S(...) custom-call(f32[1,128]{1,0:T(1,128)S(1)} %bitcast.3, ...), custom_call_target="tpu_custom_call" | custom-call | tf_op jit(solution)/shard_map/column/pallas_call | solution.py:295
  21.3 2.7 %collective-permute-start.9 = (bf16[256,128]{1,0:T(8,128)(2,1)S(1)}, bf16[256,128]{1,0:T(8,128)(2,1)S(1)}, u32[]{:S(2)}, u32[]{:S(2)}) collective-permute-start(bf16[256,128]{1,0:T(8,128)(2,1)S(1)} %get-tuple-element.39), channel_id=1, source_target_pairs={{0,16},{4,20},{8,24},{12,28},{16,0},{20,4},{24,8},{28,12},{1,17},{... | collective-permute-start | bytes 196616 | tf_op jit(solution)/shard_map/ppermute | solution.py:240
  24.0 0.7 %collective-permute-start.10 = (bf16[256,128]{1,0:T(8,128)(2,1)S(1)}, bf16[256,128]{1,0:T(8,128)(2,1)S(1)}, u32[]{:S(2)}, u32[]{:S(2)}) collective-permute-start(bf16[256,128]{1,0:T(8,128)(2,1)S(1)} %get-tuple-element.40), channel_id=1, source_target_pairs={{0,12},{4,8},{8,4},{12,0},{16,28},{20,24},{24,20},{28,16},{1,13},{... | collective-permute-start | bytes 196616 | tf_op jit(solution)/shard_map/ppermute | solution.py:240
  24.6 0.0 collective-permute-done.1
  24.7 0.1 collective-permute-start.2
  24.8 1.7 %collective-permute-start.11 = (bf16[256,128]{1,0:T(8,128)(2,1)S(1)}, bf16[256,128]{1,0:T(8,128)(2,1)S(1)}, u32[]{:S(2)}, u32[]{:S(2)}) collective-permute-start(bf16[256,128]{1,0:T(8,128)(2,1)S(1)} %get-tuple-element.43), channel_id=1, source_target_pairs={{0,20},{4,16},{8,28},{12,24},{16,4},{20,0},{24,12},{28,8},{1,21},{... | collective-permute-start | bytes 196616 | tf_op jit(solution)/shard_map/ppermute | solution.py:240
  26.4 3.4 %collective-permute-start.12 = (bf16[256,128]{1,0:T(8,128)(2,1)S(1)}, bf16[256,128]{1,0:T(8,128)(2,1)S(1)}, u32[]{:S(2)}, u32[]{:S(2)}) collective-permute-start(bf16[256,128]{1,0:T(8,128)(2,1)S(1)} %get-tuple-element.44), channel_id=1, source_target_pairs={{0,28},{4,24},{8,20},{12,16},{16,12},{20,8},{24,4},{28,0},{1,29},{... | collective-permute-start | bytes 196616 | tf_op jit(solution)/shard_map/ppermute | solution.py:240
  29.8 0.0 collective-permute-done.9.refs_1_
  29.8 1.4 %collective-permute-start.13 = (bf16[256,128]{1,0:T(8,128)(2,1)S(1)}, bf16[256,128]{1,0:T(8,128)(2,1)S(1)}, u32[]{:S(2)}, u32[]{:S(2)}) collective-permute-start(bf16[256,128]{1,0:T(8,128)(2,1)S(1)} %get-tuple-element.45), channel_id=1, source_target_pairs={{0,24},{4,28},{8,16},{12,20},{16,8},{20,12},{24,0},{28,4},{1,25},{... | collective-permute-start | bytes 196616 | tf_op jit(solution)/shard_map/ppermute | solution.py:240
  31.2 0.0 collective-permute-done.10.refs_2_
  31.2 0.0 collective-permute-start.14
  31.2 0.0 collective-permute-done.2
  31.2 0.6 %collective-permute-start.15 = (bf16[256,128]{1,0:T(8,128)(2,1)S(1)}, bf16[256,128]{1,0:T(8,128)(2,1)S(1)}, u32[]{:S(2)}, u32[]{:S(2)}) collective-permute-start(bf16[256,128]{1,0:T(8,128)(2,1)S(1)} %get-tuple-element.47), channel_id=1, source_target_pairs={{0,4},{4,0},{8,12},{12,8},{16,20},{20,16},{24,28},{28,24},{1,5},{5... | collective-permute-start | bytes 196616 | tf_op jit(solution)/shard_map/ppermute | solution.py:240
  31.8 0.0 copy-done.1
  31.8 0.0 copy-done.3
  31.8 0.0 copy-done.4
  31.8 0.0 copy-done.8
  31.8 2.5 %row_out.1 = (f32[4,512,128]{2,1,0:T(8,128)S(1)}, f32[1,128]{1,0:T(1,128)S(1)}, bf16[4,512,128]{2,1,0:T(8,128)(2,1)}) custom-call(bf16[4,512,128]{2,1,0:T(8,128)(2,1)S(1)} %copy-done.1, bf16[2,4,512,128]{3,2,1,0:T(8,128)(2,1)S(1)} %get-tuple-element.28.query_ref, f32[2,4,512,128]{3,2,1,0:T(8,128)S(1)} %get-tuple-element.29.refs_8_.gate_ref, ...), custom_call_target="tpu_custom_call" | custom-call | tf_op jit(solution)/shard_map/row_out/pallas_call | solution.py:325
  34.4 0.0 collective-permute-done.11.refs_0_
  34.4 0.0 collective-permute-done.12.refs_1_
  34.4 1.9 %collective-permute-done.13.refs_2_ = bf16[256,128]{1,0:T(8,128)(2,1)S(1)} collective-permute-done((bf16[256,128]{1,0:T(8,128)(2,1)S(1)}, bf16[256,128]{1,0:T(8,128)(2,1)S(1)}, u32[]{:S(2)}, u32[]{:S(2)}) %collective-permute-start.13) | collective-permute-done | bytes 65568 | tf_op jit(solution)/shard_map/ppermute | solution.py:240
  36.3 0.3 collective-permute-done.14.refs_3_
  36.6 0.0 collective-permute-done.15.refs_4_
  36.6 2.0 %final.1 = bf16[4,512,128]{2,1,0:T(8,128)(2,1)} custom-call(f32[4,512,128]{2,1,0:T(8,128)S(1)} %get-tuple-element.41.updated_ref, f32[1,128]{1,0:T(1,128)S(1)} %get-tuple-element.42.gain_ref, bf16[128,512]{1,0:T(8,128)(2,1)S(1)} %copy-done.3, bf16[512,128]{1,0:T(8,128)(2,1)S(1)} %copy-done.4, ...), custom_call_target="tpu_custom_call", output_to_operand_aliasing={{}: (9, {})} | custom-call | tf_op jit(solution)/shard_map/final/pallas_call | solution.py:350
  (2 shorter events, 0.0 us)
Async XLA Ops:
  0.0 1.0 %copy-start = (bf16[4,512,128]{2,1,0:T(8,128)(2,1)S(1)}, bf16[4,512,128]{2,1,0:T(8,128)(2,1)}, u32[]{:S(2)}) copy-start(bf16[4,512,128]{2,1,0:T(8,128)(2,1)} %x_ref.5) | copy-start | bytes 1572868
  1.0 12.7 %copy-start.2 = (bf16[3,128,512]{2,1,0:T(8,128)(2,1)S(1)}, bf16[3,128,512]{2,1,0:T(8,128)(2,1)}, u32[]{:S(2)}) copy-start(bf16[3,128,512]{2,1,0:T(8,128)(2,1)} %weight_ref.3) | copy-start | bytes 1179652
  1.0 12.7 %copy-start.7 = (f32[128]{0:T(128)S(1)}, f32[128]{0:T(128)}, u32[]{:S(2)}) copy-start(f32[128]{0:T(128)} %param.9) | copy-start | bytes 1540
  1.0 17.6 %copy-start.5 = (bf16[3,128,128]{2,1,0:T(8,128)(2,1)S(1)}, bf16[3,128,128]{2,1,0:T(8,128)(2,1)}, u32[]{:S(2)}) copy-start(bf16[3,128,128]{2,1,0:T(8,128)(2,1)} %out_weight_ref.3) | copy-start | bytes 294916
  1.0 17.6 %copy-start.6 = (f32[3,128]{1,0:T(4,128)S(1)}, f32[3,128]{1,0:T(4,128)}, u32[]{:S(2)}) copy-start(f32[3,128]{1,0:T(4,128)} %head_gain_ref.3) | copy-start | bytes 4612
  1.5 11.7 %collective-permute-start = (bf16[256,128]{1,0:T(8,128)(2,1)S(1)}, bf16[256,128]{1,0:T(8,128)(2,1)S(1)}, u32[]{:S(2)}, u32[]{:S(2)}) collective-permute-start(bf16[256,128]{1,0:T(8,128)(2,1)S(1)} %get-tuple-element.27), channel_id=1, source_target_pairs={{0,16},{4,20},{8,24},{12,28},{16,0},{20,4},{24,8},{28,12},{1,17},{... | collective-permute-start | bytes 196616 | tf_op jit(solution)/shard_map/ppermute | solution.py:240
  5.6 8.1 %collective-permute-start.3 = (bf16[256,128]{1,0:T(8,128)(2,1)S(1)}, bf16[256,128]{1,0:T(8,128)(2,1)S(1)}, u32[]{:S(2)}, u32[]{:S(2)}) collective-permute-start(bf16[256,128]{1,0:T(8,128)(2,1)S(1)} %get-tuple-element.32), channel_id=1, source_target_pairs={{0,12},{4,8},{8,4},{12,0},{16,28},{20,24},{24,20},{28,16},{1,13},{... | collective-permute-start | bytes 196616 | tf_op jit(solution)/shard_map/ppermute | solution.py:240
  8.1 8.8 %collective-permute-start.4 = (bf16[256,128]{1,0:T(8,128)(2,1)S(1)}, bf16[256,128]{1,0:T(8,128)(2,1)S(1)}, u32[]{:S(2)}, u32[]{:S(2)}) collective-permute-start(bf16[256,128]{1,0:T(8,128)(2,1)S(1)} %get-tuple-element.33), channel_id=1, source_target_pairs={{0,20},{4,16},{8,28},{12,24},{16,4},{20,0},{24,12},{28,8},{1,21},{... | collective-permute-start | bytes 196616 | tf_op jit(solution)/shard_map/ppermute | solution.py:240
  8.4 10.0 %collective-permute-start.5 = (bf16[256,128]{1,0:T(8,128)(2,1)S(1)}, bf16[256,128]{1,0:T(8,128)(2,1)S(1)}, u32[]{:S(2)}, u32[]{:S(2)}) collective-permute-start(bf16[256,128]{1,0:T(8,128)(2,1)S(1)} %get-tuple-element.34), channel_id=1, source_target_pairs={{0,28},{4,24},{8,20},{12,16},{16,12},{20,8},{24,4},{28,0},{1,29},{... | collective-permute-start | bytes 196616 | tf_op jit(solution)/shard_map/ppermute | solution.py:240
  11.8 6.6 %collective-permute-start.6 = (bf16[256,128]{1,0:T(8,128)(2,1)S(1)}, bf16[256,128]{1,0:T(8,128)(2,1)S(1)}, u32[]{:S(2)}, u32[]{:S(2)}) collective-permute-start(bf16[256,128]{1,0:T(8,128)(2,1)S(1)} %get-tuple-element.35), channel_id=1, source_target_pairs={{0,24},{4,28},{8,16},{12,20},{16,8},{20,12},{24,0},{28,4},{1,25},{... | collective-permute-start | bytes 196616 | tf_op jit(solution)/shard_map/ppermute | solution.py:240
  13.2 5.2 %collective-permute-start.7 = (bf16[256,128]{1,0:T(8,128)(2,1)S(1)}, bf16[256,128]{1,0:T(8,128)(2,1)S(1)}, u32[]{:S(2)}, u32[]{:S(2)}) collective-permute-start(bf16[256,128]{1,0:T(8,128)(2,1)S(1)} %get-tuple-element.36), channel_id=1, source_target_pairs={{0,4},{4,0},{8,12},{12,8},{16,20},{20,16},{24,28},{28,24},{1,5},{5... | collective-permute-start | bytes 196616 | tf_op jit(solution)/shard_map/ppermute | solution.py:240
  13.7 5.0 %collective-permute-start.8 = (bf16[256,128]{1,0:T(8,128)(2,1)S(1)}, bf16[256,128]{1,0:T(8,128)(2,1)S(1)}, u32[]{:S(2)}, u32[]{:S(2)}) collective-permute-start(bf16[256,128]{1,0:T(8,128)(2,1)S(1)} %get-tuple-element.37), channel_id=1, source_target_pairs={{0,8},{4,12},{8,0},{12,4},{16,24},{20,28},{24,16},{28,20},{1,9},{5... | collective-permute-start | bytes 196616 | tf_op jit(solution)/shard_map/ppermute | solution.py:240
  13.7 18.1 %copy-start.1 = (bf16[4,512,128]{2,1,0:T(8,128)(2,1)S(1)}, bf16[4,512,128]{2,1,0:T(8,128)(2,1)}, u32[]{:S(2)}) copy-start(bf16[4,512,128]{2,1,0:T(8,128)(2,1)} %x_ref.5) | copy-start | bytes 1572868
  13.7 18.1 %copy-start.3 = (bf16[128,512]{1,0:T(8,128)(2,1)S(1)}, bf16[128,512]{1,0:T(8,128)(2,1)}, u32[]{:S(2)}) copy-start(bf16[128,512]{1,0:T(8,128)(2,1)} %up_ref.3) | copy-start | bytes 393220
  13.7 18.1 %copy-start.4 = (bf16[512,128]{1,0:T(8,128)(2,1)S(1)}, bf16[512,128]{1,0:T(8,128)(2,1)}, u32[]{:S(2)}) copy-start(bf16[512,128]{1,0:T(8,128)(2,1)} %down_ref.3) | copy-start | bytes 393220
  13.8 18.1 %copy-start.8 = (f32[128]{0:T(128)S(1)}, f32[128]{0:T(128)}, u32[]{:S(2)}) copy-start(f32[128]{0:T(128)} %param.13) | copy-start | bytes 1540
  16.9 7.7 %collective-permute-start.1 = (bf16[2,4,32,128]{3,2,1,0:T(8,128)(2,1)S(1)}, bf16[2,4,32,128]{3,2,1,0:T(8,128)(2,1)S(1)}, u32[]{:S(2)}, u32[]{:S(2)}) collective-permute-start(bf16[2,4,32,128]{3,2,1,0:T(8,128)(2,1)S(1)} %get-tuple-element.30), channel_id=1, source_target_pairs={{0,2},{1,3},{2,0},{3,1},{4,6},{5,7},{6,4},{7,5},{8,10},{9,11},{10,... | collective-permute-start | bytes 196616 | tf_op jit(solution)/shard_map/ppermute | solution.py:292
  21.3 8.6 %collective-permute-start.9 = (bf16[256,128]{1,0:T(8,128)(2,1)S(1)}, bf16[256,128]{1,0:T(8,128)(2,1)S(1)}, u32[]{:S(2)}, u32[]{:S(2)}) collective-permute-start(bf16[256,128]{1,0:T(8,128)(2,1)S(1)} %get-tuple-element.39), channel_id=1, source_target_pairs={{0,16},{4,20},{8,24},{12,28},{16,0},{20,4},{24,8},{28,12},{1,17},{... | collective-permute-start | bytes 196616 | tf_op jit(solution)/shard_map/ppermute | solution.py:240
  24.0 7.2 %collective-permute-start.10 = (bf16[256,128]{1,0:T(8,128)(2,1)S(1)}, bf16[256,128]{1,0:T(8,128)(2,1)S(1)}, u32[]{:S(2)}, u32[]{:S(2)}) collective-permute-start(bf16[256,128]{1,0:T(8,128)(2,1)S(1)} %get-tuple-element.40), channel_id=1, source_target_pairs={{0,12},{4,8},{8,4},{12,0},{16,28},{20,24},{24,20},{28,16},{1,13},{... | collective-permute-start | bytes 196616 | tf_op jit(solution)/shard_map/ppermute | solution.py:240
  24.7 6.5 %collective-permute-start.2 = (bf16[2,4,32,128]{3,2,1,0:T(8,128)(2,1)S(1)}, bf16[2,4,32,128]{3,2,1,0:T(8,128)(2,1)S(1)}, u32[]{:S(2)}, u32[]{:S(2)}) collective-permute-start(bf16[2,4,32,128]{3,2,1,0:T(8,128)(2,1)S(1)} %add_convert_fusion.1), channel_id=1, source_target_pairs={{0,1},{1,0},{2,3},{3,2},{4,5},{5,4},{6,7},{7,6},{8,9},{9,8},{10,11... | collective-permute-start | bytes 196616 | tf_op jit(solution)/shard_map/ppermute | solution.py:292
  24.8 9.6 %collective-permute-start.11 = (bf16[256,128]{1,0:T(8,128)(2,1)S(1)}, bf16[256,128]{1,0:T(8,128)(2,1)S(1)}, u32[]{:S(2)}, u32[]{:S(2)}) collective-permute-start(bf16[256,128]{1,0:T(8,128)(2,1)S(1)} %get-tuple-element.43), channel_id=1, source_target_pairs={{0,20},{4,16},{8,28},{12,24},{16,4},{20,0},{24,12},{28,8},{1,21},{... | collective-permute-start | bytes 196616 | tf_op jit(solution)/shard_map/ppermute | solution.py:240
  26.4 8.0 %collective-permute-start.12 = (bf16[256,128]{1,0:T(8,128)(2,1)S(1)}, bf16[256,128]{1,0:T(8,128)(2,1)S(1)}, u32[]{:S(2)}, u32[]{:S(2)}) collective-permute-start(bf16[256,128]{1,0:T(8,128)(2,1)S(1)} %get-tuple-element.44), channel_id=1, source_target_pairs={{0,28},{4,24},{8,20},{12,16},{16,12},{20,8},{24,4},{28,0},{1,29},{... | collective-permute-start | bytes 196616 | tf_op jit(solution)/shard_map/ppermute | solution.py:240
  29.8 6.4 %collective-permute-start.13 = (bf16[256,128]{1,0:T(8,128)(2,1)S(1)}, bf16[256,128]{1,0:T(8,128)(2,1)S(1)}, u32[]{:S(2)}, u32[]{:S(2)}) collective-permute-start(bf16[256,128]{1,0:T(8,128)(2,1)S(1)} %get-tuple-element.45), channel_id=1, source_target_pairs={{0,24},{4,28},{8,16},{12,20},{16,8},{20,12},{24,0},{28,4},{1,25},{... | collective-permute-start | bytes 196616 | tf_op jit(solution)/shard_map/ppermute | solution.py:240
  31.2 5.4 %collective-permute-start.14 = (bf16[256,128]{1,0:T(8,128)(2,1)S(1)}, bf16[256,128]{1,0:T(8,128)(2,1)S(1)}, u32[]{:S(2)}, u32[]{:S(2)}) collective-permute-start(bf16[256,128]{1,0:T(8,128)(2,1)S(1)} %get-tuple-element.46), channel_id=1, source_target_pairs={{0,8},{4,12},{8,0},{12,4},{16,24},{20,28},{24,16},{28,20},{1,9},{5... | collective-permute-start | bytes 196616 | tf_op jit(solution)/shard_map/ppermute | solution.py:240
  31.2 5.4 %collective-permute-start.15 = (bf16[256,128]{1,0:T(8,128)(2,1)S(1)}, bf16[256,128]{1,0:T(8,128)(2,1)S(1)}, u32[]{:S(2)}, u32[]{:S(2)}) collective-permute-start(bf16[256,128]{1,0:T(8,128)(2,1)S(1)} %get-tuple-element.47), channel_id=1, source_target_pairs={{0,4},{4,0},{8,12},{12,8},{16,20},{20,16},{24,28},{28,24},{1,5},{5... | collective-permute-start | bytes 196616 | tf_op jit(solution)/shard_map/ppermute | solution.py:240

commit v7 on v5

--- a/solution.py
+++ b/solution.py
@@ -220,7 +220,7 @@
 
 def inward_order(parts):
     half = parts // 2
-    steps = (0, half, half - 1, *far_steps(parts), *range(1, half - 1))
+    steps = (0, half, half - 1, parts - 1, *range(half + 1, parts - 1), *range(half - 2, 0, -1))
     return tuple(dict.fromkeys(steps))
 
 

time: 38.7 us -> 38.7 us (level)
  transfers between devices with their start and end apart: 16 -> 16, of which waited for: 4 -> 3; matrix products, arithmetic and copies ran while one was open for 0% -> 0% of each run, Pallas kernels for 20% -> 20%
where the time goes in v7:
time: 38.7 us; the launch traced here: 38.6 us
  starting transfers between devices  24.4 us (63%)
  Pallas kernels  9.97 us (26%)
  waiting for transfers between devices  2.91 us (8%)
  local copies, waits for them, and re-layouts  1.08 us (3%)
    ppermute x14, starting transfers between devices, exchange(): moved[step] = lax.ppermute(pieces[step], 'row', pairs)  22.8 us
    ppermute x14, waiting for transfers between devices, exchange(): moved[step] = lax.ppermute(pieces[step], 'row', pairs)  2.91 us
    pallas_call x1, Pallas kernels, shards(): call(functools.partial(column_kernel, row_count, order), [struct((tokens,...  2.61 us
    pallas_call x1, Pallas kernels, shards(): call(functools.partial(row_kernel, early, parts), (struct(pair_map.shape,...  2.61 us
    pallas_call x1, Pallas kernels, shards(): call(state_kernel, (struct((2, row_count, HEAD, width), BF16), struct(bot...  2.33 us
    pallas_call x1, Pallas kernels, shards(): call(functools.partial(final_kernel, late, parts), struct(pair_map.shape,...  1.98 us
    ppermute x2, starting transfers between devices, shards(): lax.ppermute(state, 'col', pairs).astype(F32)  1.62 us
    unnamed x18, local copies, waits for them, and re-layouts  1.08 us
  transfers between devices with their start and end apart: 16, of which 3 were waited for; matrix products, arithmetic and copies ran while one was open for 0% of the time, Pallas kernels for 20%

profile of v7, /device:TPU:0, one launch (start us, length us, event | category | flops | bytes accessed | tf_op | source)
XLA Modules:
  0.0 38.6 jit_solution(8629465368890168260)
XLA Ops:
  0.0 0.0 copy-start
  0.0 1.0 %copy-done = bf16[4,512,128]{2,1,0:T(8,128)(2,1)S(1)} copy-done((bf16[4,512,128]{2,1,0:T(8,128)(2,1)S(1)}, bf16[4,512,128]{2,1,0:T(8,128)(2,1)}, u32[]{:S(2)}) %copy-start) | copy-done | bytes 524312
  1.0 0.0 copy-start.2
  1.0 0.0 copy-start.7
  1.0 0.0 copy-start.5
  1.0 0.0 copy-start.6
  1.1 0.4 %pieces.1 = (bf16[256,128]{1,0:T(8,128)(2,1)S(1)}, bf16[256,128]{1,0:T(8,128)(2,1)S(1)}, bf16[256,128]{1,0:T(8,128)(2,1)S(1)}, bf16[256,128]{1,0:T(8,128)(2,1)S(...) custom-call(bf16[4,512,128]{2,1,0:T(8,128)(2,1)S(1)} %copy-done), custom_call_target="tpu_custom_call" | custom-call | flops 10000000000 | tf_op jit(solution)/shard_map/pieces/pallas_call | solution.py:275
  1.5 4.1 %collective-permute-start = (bf16[256,128]{1,0:T(8,128)(2,1)S(1)}, bf16[256,128]{1,0:T(8,128)(2,1)S(1)}, u32[]{:S(2)}, u32[]{:S(2)}) collective-permute-start(bf16[256,128]{1,0:T(8,128)(2,1)S(1)} %get-tuple-element.27), channel_id=1, source_target_pairs={{0,16},{4,20},{8,24},{12,28},{16,0},{20,4},{24,8},{28,12},{1,17},{... | collective-permute-start | bytes 196616 | tf_op jit(solution)/shard_map/ppermute | solution.py:239
  5.6 2.5 %collective-permute-start.3 = (bf16[256,128]{1,0:T(8,128)(2,1)S(1)}, bf16[256,128]{1,0:T(8,128)(2,1)S(1)}, u32[]{:S(2)}, u32[]{:S(2)}) collective-permute-start(bf16[256,128]{1,0:T(8,128)(2,1)S(1)} %get-tuple-element.32), channel_id=1, source_target_pairs={{0,12},{4,8},{8,4},{12,0},{16,28},{20,24},{24,20},{28,16},{1,13},{... | collective-permute-start | bytes 196616 | tf_op jit(solution)/shard_map/ppermute | solution.py:239
  8.1 0.0 collective-permute-start.4
  8.1 2.8 %collective-permute-start.5 = (bf16[256,128]{1,0:T(8,128)(2,1)S(1)}, bf16[256,128]{1,0:T(8,128)(2,1)S(1)}, u32[]{:S(2)}, u32[]{:S(2)}) collective-permute-start(bf16[256,128]{1,0:T(8,128)(2,1)S(1)} %get-tuple-element.34), channel_id=1, source_target_pairs={{0,20},{4,16},{8,28},{12,24},{16,4},{20,0},{24,12},{28,8},{1,21},{... | collective-permute-start | bytes 196616 | tf_op jit(solution)/shard_map/ppermute | solution.py:239
  10.9 1.3 %collective-permute-start.6 = (bf16[256,128]{1,0:T(8,128)(2,1)S(1)}, bf16[256,128]{1,0:T(8,128)(2,1)S(1)}, u32[]{:S(2)}, u32[]{:S(2)}) collective-permute-start(bf16[256,128]{1,0:T(8,128)(2,1)S(1)} %get-tuple-element.35), channel_id=1, source_target_pairs={{0,24},{4,28},{8,16},{12,20},{16,8},{20,12},{24,0},{28,4},{1,25},{... | collective-permute-start | bytes 196616 | tf_op jit(solution)/shard_map/ppermute | solution.py:239
  12.3 0.0 collective-permute-done.after_ref.refs_1_
  12.3 1.1 %collective-permute-start.7 = (bf16[256,128]{1,0:T(8,128)(2,1)S(1)}, bf16[256,128]{1,0:T(8,128)(2,1)S(1)}, u32[]{:S(2)}, u32[]{:S(2)}) collective-permute-start(bf16[256,128]{1,0:T(8,128)(2,1)S(1)} %get-tuple-element.36), channel_id=1, source_target_pairs={{0,8},{4,12},{8,0},{12,4},{16,24},{20,28},{24,16},{28,20},{1,9},{5... | collective-permute-start | bytes 196616 | tf_op jit(solution)/shard_map/ppermute | solution.py:239
  13.4 0.0 collective-permute-done.3.refs_2_
  13.4 0.5 %collective-permute-start.8 = (bf16[256,128]{1,0:T(8,128)(2,1)S(1)}, bf16[256,128]{1,0:T(8,128)(2,1)S(1)}, u32[]{:S(2)}, u32[]{:S(2)}) collective-permute-start(bf16[256,128]{1,0:T(8,128)(2,1)S(1)} %get-tuple-element.37), channel_id=1, source_target_pairs={{0,4},{4,0},{8,12},{12,8},{16,20},{20,16},{24,28},{28,24},{1,5},{5... | collective-permute-start | bytes 196616 | tf_op jit(solution)/shard_map/ppermute | solution.py:239
  13.9 0.0 copy-done.2
  13.9 0.0 copy-done.7
  13.9 0.0 copy-start.1
  13.9 0.0 copy-start.3
  14.0 0.0 copy-start.4
  14.0 0.0 copy-start.8
  14.0 2.3 %row_state.1 = (bf16[2,4,32,128]{3,2,1,0:T(8,128)(2,1)S(1)}, bf16[2,4,512,128]{3,2,1,0:T(8,128)(2,1)S(1)}, f32[2,4,512,128]{3,2,1,0:T(8,128)S(1)}) custom-call(bf16[4,512,128]{2,1,0:T(8,128)(2,1)S(1)} %copy-done, f32[1,128]{1,0:T(1,128)S(1)} %bitcast.2, bf16[3,128,512]{2,1,0:T(8,128)(2,1)S(1)} %copy-done.2, ...), custom_call_target="tpu_custom_call" | custom-call | tf_op jit(solution)/shard_map/row_state/pallas_call | solution.py:282
  16.3 0.0 collective-permute-done.4.refs_3_
  16.3 1.6 %collective-permute-start.1 = (bf16[2,4,32,128]{3,2,1,0:T(8,128)(2,1)S(1)}, bf16[2,4,32,128]{3,2,1,0:T(8,128)(2,1)S(1)}, u32[]{:S(2)}, u32[]{:S(2)}) collective-permute-start(bf16[2,4,32,128]{3,2,1,0:T(8,128)(2,1)S(1)} %get-tuple-element.30), channel_id=1, source_target_pairs={{0,2},{1,3},{2,0},{3,1},{4,6},{5,7},{6,4},{7,5},{8,10},{9,11},{10,... | collective-permute-start | bytes 196616 | tf_op jit(solution)/shard_map/ppermute | solution.py:291
  17.9 0.9 %collective-permute-done.5.refs_4_ = bf16[256,128]{1,0:T(8,128)(2,1)S(1)} collective-permute-done((bf16[256,128]{1,0:T(8,128)(2,1)S(1)}, bf16[256,128]{1,0:T(8,128)(2,1)S(1)}, u32[]{:S(2)}, u32[]{:S(2)}) %collective-permute-start.5) | collective-permute-done | bytes 65568 | tf_op jit(solution)/shard_map/ppermute | solution.py:239
  18.8 0.0 collective-permute-done.6.refs_5_
  18.8 0.0 collective-permute-done.7.refs_6_
  18.8 0.0 collective-permute-done.8.refs_7_
  18.8 0.0 copy-done.5
  18.8 0.0 copy-done.6
  18.9 2.6 %column.1 = (bf16[256,128]{1,0:T(8,128)(2,1)S(1)}, bf16[256,128]{1,0:T(8,128)(2,1)S(1)}, bf16[256,128]{1,0:T(8,128)(2,1)S(1)}, bf16[256,128]{1,0:T(8,128)(2,1)S(...) custom-call(f32[1,128]{1,0:T(1,128)S(1)} %bitcast.3, ...), custom_call_target="tpu_custom_call" | custom-call | tf_op jit(solution)/shard_map/column/pallas_call | solution.py:294
  21.5 2.5 %collective-permute-start.9 = (bf16[256,128]{1,0:T(8,128)(2,1)S(1)}, bf16[256,128]{1,0:T(8,128)(2,1)S(1)}, u32[]{:S(2)}, u32[]{:S(2)}) collective-permute-start(bf16[256,128]{1,0:T(8,128)(2,1)S(1)} %get-tuple-element.39), channel_id=1, source_target_pairs={{0,16},{4,20},{8,24},{12,28},{16,0},{20,4},{24,8},{28,12},{1,17},{... | collective-permute-start | bytes 196616 | tf_op jit(solution)/shard_map/ppermute | solution.py:239
  24.0 1.1 %collective-permute-start.10 = (bf16[256,128]{1,0:T(8,128)(2,1)S(1)}, bf16[256,128]{1,0:T(8,128)(2,1)S(1)}, u32[]{:S(2)}, u32[]{:S(2)}) collective-permute-start(bf16[256,128]{1,0:T(8,128)(2,1)S(1)} %get-tuple-element.40), channel_id=1, source_target_pairs={{0,12},{4,8},{8,4},{12,0},{16,28},{20,24},{24,20},{28,16},{1,13},{... | collective-permute-start | bytes 196616 | tf_op jit(solution)/shard_map/ppermute | solution.py:239
  25.0 0.0 collective-permute-done.1
  25.1 0.1 collective-permute-start.2
  25.2 1.4 %collective-permute-start.11 = (bf16[256,128]{1,0:T(8,128)(2,1)S(1)}, bf16[256,128]{1,0:T(8,128)(2,1)S(1)}, u32[]{:S(2)}, u32[]{:S(2)}) collective-permute-start(bf16[256,128]{1,0:T(8,128)(2,1)S(1)} %get-tuple-element.43), channel_id=1, source_target_pairs={{0,20},{4,16},{8,28},{12,24},{16,4},{20,0},{24,12},{28,8},{1,21},{... | collective-permute-start | bytes 196616 | tf_op jit(solution)/shard_map/ppermute | solution.py:239
  26.6 2.7 %collective-permute-start.12 = (bf16[256,128]{1,0:T(8,128)(2,1)S(1)}, bf16[256,128]{1,0:T(8,128)(2,1)S(1)}, u32[]{:S(2)}, u32[]{:S(2)}) collective-permute-start(bf16[256,128]{1,0:T(8,128)(2,1)S(1)} %get-tuple-element.44), channel_id=1, source_target_pairs={{0,28},{4,24},{8,20},{12,16},{16,12},{20,8},{24,4},{28,0},{1,29},{... | collective-permute-start | bytes 196616 | tf_op jit(solution)/shard_map/ppermute | solution.py:239
  29.3 0.0 collective-permute-done.9.refs_1_
  29.3 1.3 %collective-permute-start.13 = (bf16[256,128]{1,0:T(8,128)(2,1)S(1)}, bf16[256,128]{1,0:T(8,128)(2,1)S(1)}, u32[]{:S(2)}, u32[]{:S(2)}) collective-permute-start(bf16[256,128]{1,0:T(8,128)(2,1)S(1)} %get-tuple-element.45), channel_id=1, source_target_pairs={{0,24},{4,28},{8,16},{12,20},{16,8},{20,12},{24,0},{28,4},{1,25},{... | collective-permute-start | bytes 196616 | tf_op jit(solution)/shard_map/ppermute | solution.py:239
  30.6 0.0 collective-permute-done.10.refs_2_
  30.6 0.0 collective-permute-start.14
  30.6 0.0 collective-permute-done.2
  30.6 1.3 %collective-permute-start.15 = (bf16[256,128]{1,0:T(8,128)(2,1)S(1)}, bf16[256,128]{1,0:T(8,128)(2,1)S(1)}, u32[]{:S(2)}, u32[]{:S(2)}) collective-permute-start(bf16[256,128]{1,0:T(8,128)(2,1)S(1)} %get-tuple-element.47), channel_id=1, source_target_pairs={{0,4},{4,0},{8,12},{12,8},{16,20},{20,16},{24,28},{28,24},{1,5},{5... | collective-permute-start | bytes 196616 | tf_op jit(solution)/shard_map/ppermute | solution.py:239
  32.0 0.0 copy-done.1
  32.0 0.0 copy-done.3
  32.0 0.0 copy-done.4
  32.0 0.0 copy-done.8
  32.0 2.6 %row_out.1 = (f32[4,512,128]{2,1,0:T(8,128)S(1)}, f32[1,128]{1,0:T(1,128)S(1)}, bf16[4,512,128]{2,1,0:T(8,128)(2,1)}) custom-call(bf16[4,512,128]{2,1,0:T(8,128)(2,1)S(1)} %copy-done.1, bf16[2,4,512,128]{3,2,1,0:T(8,128)(2,1)S(1)} %get-tuple-element.28.query_ref, f32[2,4,512,128]{3,2,1,0:T(8,128)S(1)} %get-tuple-element.29.refs_8_.gate_ref, ...), custom_call_target="tpu_custom_call" | custom-call | tf_op jit(solution)/shard_map/row_out/pallas_call | solution.py:324
  34.7 0.0 collective-permute-done.11.refs_0_
  34.7 0.0 collective-permute-done.12.refs_1_
  34.7 1.0 %collective-permute-done.13.refs_2_ = bf16[256,128]{1,0:T(8,128)(2,1)S(1)} collective-permute-done((bf16[256,128]{1,0:T(8,128)(2,1)S(1)}, bf16[256,128]{1,0:T(8,128)(2,1)S(1)}, u32[]{:S(2)}, u32[]{:S(2)}) %collective-permute-start.13) | collective-permute-done | bytes 65568 | tf_op jit(solution)/shard_map/ppermute | solution.py:239
  35.7 0.9 %collective-permute-done.14.refs_3_ = bf16[256,128]{1,0:T(8,128)(2,1)S(1)} collective-permute-done((bf16[256,128]{1,0:T(8,128)(2,1)S(1)}, bf16[256,128]{1,0:T(8,128)(2,1)S(1)}, u32[]{:S(2)}, u32[]{:S(2)}) %collective-permute-start.14) | collective-permute-done | bytes 65568 | tf_op jit(solution)/shard_map/ppermute | solution.py:239
  36.6 0.0 collective-permute-done.15.refs_4_
  36.6 2.0 %final.1 = bf16[4,512,128]{2,1,0:T(8,128)(2,1)} custom-call(f32[4,512,128]{2,1,0:T(8,128)S(1)} %get-tuple-element.41.updated_ref, f32[1,128]{1,0:T(1,128)S(1)} %get-tuple-element.42.gain_ref, bf16[128,512]{1,0:T(8,128)(2,1)S(1)} %copy-done.3, bf16[512,128]{1,0:T(8,128)(2,1)S(1)} %copy-done.4, ...), custom_call_target="tpu_custom_call", output_to_operand_aliasing={{}: (9, {})} | custom-call | tf_op jit(solution)/shard_map/final/pallas_call | solution.py:349
  (2 shorter events, 0.0 us)
Async XLA Ops:
  0.0 1.0 %copy-start = (bf16[4,512,128]{2,1,0:T(8,128)(2,1)S(1)}, bf16[4,512,128]{2,1,0:T(8,128)(2,1)}, u32[]{:S(2)}) copy-start(bf16[4,512,128]{2,1,0:T(8,128)(2,1)} %x_ref.5) | copy-start | bytes 1572868
  1.0 12.9 %copy-start.2 = (bf16[3,128,512]{2,1,0:T(8,128)(2,1)S(1)}, bf16[3,128,512]{2,1,0:T(8,128)(2,1)}, u32[]{:S(2)}) copy-start(bf16[3,128,512]{2,1,0:T(8,128)(2,1)} %weight_ref.3) | copy-start | bytes 1179652
  1.0 12.9 %copy-start.7 = (f32[128]{0:T(128)S(1)}, f32[128]{0:T(128)}, u32[]{:S(2)}) copy-start(f32[128]{0:T(128)} %param.9) | copy-start | bytes 1540
  1.0 17.8 %copy-start.5 = (bf16[3,128,128]{2,1,0:T(8,128)(2,1)S(1)}, bf16[3,128,128]{2,1,0:T(8,128)(2,1)}, u32[]{:S(2)}) copy-start(bf16[3,128,128]{2,1,0:T(8,128)(2,1)} %out_weight_ref.3) | copy-start | bytes 294916
  1.0 17.8 %copy-start.6 = (f32[3,128]{1,0:T(4,128)S(1)}, f32[3,128]{1,0:T(4,128)}, u32[]{:S(2)}) copy-start(f32[3,128]{1,0:T(4,128)} %head_gain_ref.3) | copy-start | bytes 4612
  1.5 10.8 %collective-permute-start = (bf16[256,128]{1,0:T(8,128)(2,1)S(1)}, bf16[256,128]{1,0:T(8,128)(2,1)S(1)}, u32[]{:S(2)}, u32[]{:S(2)}) collective-permute-start(bf16[256,128]{1,0:T(8,128)(2,1)S(1)} %get-tuple-element.27), channel_id=1, source_target_pairs={{0,16},{4,20},{8,24},{12,28},{16,0},{20,4},{24,8},{28,12},{1,17},{... | collective-permute-start | bytes 196616 | tf_op jit(solution)/shard_map/ppermute | solution.py:239
  5.6 7.8 %collective-permute-start.3 = (bf16[256,128]{1,0:T(8,128)(2,1)S(1)}, bf16[256,128]{1,0:T(8,128)(2,1)S(1)}, u32[]{:S(2)}, u32[]{:S(2)}) collective-permute-start(bf16[256,128]{1,0:T(8,128)(2,1)S(1)} %get-tuple-element.32), channel_id=1, source_target_pairs={{0,12},{4,8},{8,4},{12,0},{16,28},{20,24},{24,20},{28,16},{1,13},{... | collective-permute-start | bytes 196616 | tf_op jit(solution)/shard_map/ppermute | solution.py:239
  8.1 8.2 %collective-permute-start.4 = (bf16[256,128]{1,0:T(8,128)(2,1)S(1)}, bf16[256,128]{1,0:T(8,128)(2,1)S(1)}, u32[]{:S(2)}, u32[]{:S(2)}) collective-permute-start(bf16[256,128]{1,0:T(8,128)(2,1)S(1)} %get-tuple-element.33), channel_id=1, source_target_pairs={{0,28},{4,24},{8,20},{12,16},{16,12},{20,8},{24,4},{28,0},{1,29},{... | collective-permute-start | bytes 196616 | tf_op jit(solution)/shard_map/ppermute | solution.py:239
  8.1 10.7 %collective-permute-start.5 = (bf16[256,128]{1,0:T(8,128)(2,1)S(1)}, bf16[256,128]{1,0:T(8,128)(2,1)S(1)}, u32[]{:S(2)}, u32[]{:S(2)}) collective-permute-start(bf16[256,128]{1,0:T(8,128)(2,1)S(1)} %get-tuple-element.34), channel_id=1, source_target_pairs={{0,20},{4,16},{8,28},{12,24},{16,4},{20,0},{24,12},{28,8},{1,21},{... | collective-permute-start | bytes 196616 | tf_op jit(solution)/shard_map/ppermute | solution.py:239
  10.9 7.9 %collective-permute-start.6 = (bf16[256,128]{1,0:T(8,128)(2,1)S(1)}, bf16[256,128]{1,0:T(8,128)(2,1)S(1)}, u32[]{:S(2)}, u32[]{:S(2)}) collective-permute-start(bf16[256,128]{1,0:T(8,128)(2,1)S(1)} %get-tuple-element.35), channel_id=1, source_target_pairs={{0,24},{4,28},{8,16},{12,20},{16,8},{20,12},{24,0},{28,4},{1,25},{... | collective-permute-start | bytes 196616 | tf_op jit(solution)/shard_map/ppermute | solution.py:239
  12.3 6.5 %collective-permute-start.7 = (bf16[256,128]{1,0:T(8,128)(2,1)S(1)}, bf16[256,128]{1,0:T(8,128)(2,1)S(1)}, u32[]{:S(2)}, u32[]{:S(2)}) collective-permute-start(bf16[256,128]{1,0:T(8,128)(2,1)S(1)} %get-tuple-element.36), channel_id=1, source_target_pairs={{0,8},{4,12},{8,0},{12,4},{16,24},{20,28},{24,16},{28,20},{1,9},{5... | collective-permute-start | bytes 196616 | tf_op jit(solution)/shard_map/ppermute | solution.py:239
  13.4 5.4 %collective-permute-start.8 = (bf16[256,128]{1,0:T(8,128)(2,1)S(1)}, bf16[256,128]{1,0:T(8,128)(2,1)S(1)}, u32[]{:S(2)}, u32[]{:S(2)}) collective-permute-start(bf16[256,128]{1,0:T(8,128)(2,1)S(1)} %get-tuple-element.37), channel_id=1, source_target_pairs={{0,4},{4,0},{8,12},{12,8},{16,20},{20,16},{24,28},{28,24},{1,5},{5... | collective-permute-start | bytes 196616 | tf_op jit(solution)/shard_map/ppermute | solution.py:239
  13.9 18.1 %copy-start.1 = (bf16[4,512,128]{2,1,0:T(8,128)(2,1)S(1)}, bf16[4,512,128]{2,1,0:T(8,128)(2,1)}, u32[]{:S(2)}) copy-start(bf16[4,512,128]{2,1,0:T(8,128)(2,1)} %x_ref.5) | copy-start | bytes 1572868
  13.9 18.1 %copy-start.3 = (bf16[128,512]{1,0:T(8,128)(2,1)S(1)}, bf16[128,512]{1,0:T(8,128)(2,1)}, u32[]{:S(2)}) copy-start(bf16[128,512]{1,0:T(8,128)(2,1)} %up_ref.3) | copy-start | bytes 393220
  14.0 18.1 %copy-start.4 = (bf16[512,128]{1,0:T(8,128)(2,1)S(1)}, bf16[512,128]{1,0:T(8,128)(2,1)}, u32[]{:S(2)}) copy-start(bf16[512,128]{1,0:T(8,128)(2,1)} %down_ref.3) | copy-start | bytes 393220
  14.0 18.1 %copy-start.8 = (f32[128]{0:T(128)S(1)}, f32[128]{0:T(128)}, u32[]{:S(2)}) copy-start(f32[128]{0:T(128)} %param.13) | copy-start | bytes 1540
  16.3 8.7 %collective-permute-start.1 = (bf16[2,4,32,128]{3,2,1,0:T(8,128)(2,1)S(1)}, bf16[2,4,32,128]{3,2,1,0:T(8,128)(2,1)S(1)}, u32[]{:S(2)}, u32[]{:S(2)}) collective-permute-start(bf16[2,4,32,128]{3,2,1,0:T(8,128)(2,1)S(1)} %get-tuple-element.30), channel_id=1, source_target_pairs={{0,2},{1,3},{2,0},{3,1},{4,6},{5,7},{6,4},{7,5},{8,10},{9,11},{10,... | collective-permute-start | bytes 196616 | tf_op jit(solution)/shard_map/ppermute | solution.py:291
  21.5 7.8 %collective-permute-start.9 = (bf16[256,128]{1,0:T(8,128)(2,1)S(1)}, bf16[256,128]{1,0:T(8,128)(2,1)S(1)}, u32[]{:S(2)}, u32[]{:S(2)}) collective-permute-start(bf16[256,128]{1,0:T(8,128)(2,1)S(1)} %get-tuple-element.39), channel_id=1, source_target_pairs={{0,16},{4,20},{8,24},{12,28},{16,0},{20,4},{24,8},{28,12},{1,17},{... | collective-permute-start | bytes 196616 | tf_op jit(solution)/shard_map/ppermute | solution.py:239
  24.0 6.7 %collective-permute-start.10 = (bf16[256,128]{1,0:T(8,128)(2,1)S(1)}, bf16[256,128]{1,0:T(8,128)(2,1)S(1)}, u32[]{:S(2)}, u32[]{:S(2)}) collective-permute-start(bf16[256,128]{1,0:T(8,128)(2,1)S(1)} %get-tuple-element.40), channel_id=1, source_target_pairs={{0,12},{4,8},{8,4},{12,0},{16,28},{20,24},{24,20},{28,16},{1,13},{... | collective-permute-start | bytes 196616 | tf_op jit(solution)/shard_map/ppermute | solution.py:239
  25.1 5.5 %collective-permute-start.2 = (bf16[2,4,32,128]{3,2,1,0:T(8,128)(2,1)S(1)}, bf16[2,4,32,128]{3,2,1,0:T(8,128)(2,1)S(1)}, u32[]{:S(2)}, u32[]{:S(2)}) collective-permute-start(bf16[2,4,32,128]{3,2,1,0:T(8,128)(2,1)S(1)} %add_convert_fusion.1), channel_id=1, source_target_pairs={{0,1},{1,0},{2,3},{3,2},{4,5},{5,4},{6,7},{7,6},{8,9},{9,8},{10,11... | collective-permute-start | bytes 196616 | tf_op jit(solution)/shard_map/ppermute | solution.py:291
  25.2 9.5 %collective-permute-start.11 = (bf16[256,128]{1,0:T(8,128)(2,1)S(1)}, bf16[256,128]{1,0:T(8,128)(2,1)S(1)}, u32[]{:S(2)}, u32[]{:S(2)}) collective-permute-start(bf16[256,128]{1,0:T(8,128)(2,1)S(1)} %get-tuple-element.43), channel_id=1, source_target_pairs={{0,20},{4,16},{8,28},{12,24},{16,4},{20,0},{24,12},{28,8},{1,21},{... | collective-permute-start | bytes 196616 | tf_op jit(solution)/shard_map/ppermute | solution.py:239
  26.6 8.1 %collective-permute-start.12 = (bf16[256,128]{1,0:T(8,128)(2,1)S(1)}, bf16[256,128]{1,0:T(8,128)(2,1)S(1)}, u32[]{:S(2)}, u32[]{:S(2)}) collective-permute-start(bf16[256,128]{1,0:T(8,128)(2,1)S(1)} %get-tuple-element.44), channel_id=1, source_target_pairs={{0,28},{4,24},{8,20},{12,16},{16,12},{20,8},{24,4},{28,0},{1,29},{... | collective-permute-start | bytes 196616 | tf_op jit(solution)/shard_map/ppermute | solution.py:239
  29.3 6.4 %collective-permute-start.13 = (bf16[256,128]{1,0:T(8,128)(2,1)S(1)}, bf16[256,128]{1,0:T(8,128)(2,1)S(1)}, u32[]{:S(2)}, u32[]{:S(2)}) collective-permute-start(bf16[256,128]{1,0:T(8,128)(2,1)S(1)} %get-tuple-element.45), channel_id=1, source_target_pairs={{0,24},{4,28},{8,16},{12,20},{16,8},{20,12},{24,0},{28,4},{1,25},{... | collective-permute-start | bytes 196616 | tf_op jit(solution)/shard_map/ppermute | solution.py:239
  30.6 6.0 %collective-permute-start.14 = (bf16[256,128]{1,0:T(8,128)(2,1)S(1)}, bf16[256,128]{1,0:T(8,128)(2,1)S(1)}, u32[]{:S(2)}, u32[]{:S(2)}) collective-permute-start(bf16[256,128]{1,0:T(8,128)(2,1)S(1)} %get-tuple-element.46), channel_id=1, source_target_pairs={{0,8},{4,12},{8,0},{12,4},{16,24},{20,28},{24,16},{28,20},{1,9},{5... | collective-permute-start | bytes 196616 | tf_op jit(solution)/shard_map/ppermute | solution.py:239
  30.6 6.0 %collective-permute-start.15 = (bf16[256,128]{1,0:T(8,128)(2,1)S(1)}, bf16[256,128]{1,0:T(8,128)(2,1)S(1)}, u32[]{:S(2)}, u32[]{:S(2)}) collective-permute-start(bf16[256,128]{1,0:T(8,128)(2,1)S(1)} %get-tuple-element.47), channel_id=1, source_target_pairs={{0,4},{4,0},{8,12},{12,8},{16,20},{20,16},{24,28},{28,24},{1,5},{5... | collective-permute-start | bytes 196616 | tf_op jit(solution)/shard_map/ppermute | solution.py:239
